TPU v7x, 128 devices: a whole 4x4x4 slice. The times are simulated.
128 devices in a mesh: dp: 4 (over x), expert: 32 (over z, y, core).
Axes of the slice: x: 4, y: 4, z: 4, core: 2. Of those that a mesh axis runs over, the one named last changes fastest.
Arguments:
- tokens: bfloat16 [16384, 7168], P(('dp', 'expert')), may hold values from -6 to 6
- expert_ids: int32 [16384, 2], P(('dp', 'expert')), may hold values from 0 to 127, all different within a row
- gates: float32 [16384, 2], P(('dp', 'expert')), may hold values from 0.1 to 1
- grad_mixed: bfloat16 [16384, 7168], P(('dp', 'expert')), may hold values from -6 to 6
- w_gate: bfloat16 [32, 7168, 1024], P('expert', None, 'dp'), may hold values from -0.0625 to 0.0625
- w_up: bfloat16 [32, 7168, 1024], P('expert', None, 'dp'), may hold values from -0.0625 to 0.0625
- w_down: bfloat16 [32, 1024, 7168], P('expert', 'dp'), may hold values from -0.09375 to 0.09375
Outputs:
- mixed: bfloat16 [16384, 7168], P(('dp', 'expert'))
- grad_tokens: bfloat16 [16384, 7168], P(('dp', 'expert'))
- grad_gates: float32 [16384, 2], P(('dp', 'expert'))
All inputs are finite; a program needn't handle non-finite values.
Results may differ from a plain program's by a relative error of at most 0.02.
Values may be sent and summed in bfloat16 or wider, within the bound.
No kernel may reach another device: no remote copies, remote signals or barrier semaphores. Data moves between devices by JAX's collectives and lax.ppermute only.
A program may use at most 128 MiB of HBM per device.

v0:
```python
import jax
import jax.numpy as jnp
from jax import lax
from jax.sharding import PartitionSpec as P

CAP = 2
QUARTERS = 4


def shards(tokens, expert_ids, gates, grad_mixed, w_gate, w_up, w_down):
    n_expert = lax.axis_size("expert")
    experts = n_expert // QUARTERS
    tok_rows = tokens.shape[0]
    width = tokens.shape[1]
    fdev = w_gate.shape[2]
    slots = experts * CAP
    precise = lax.Precision.HIGHEST
    chosen = jnp.concatenate([expert_ids[:, 0], expert_ids[:, 1]])
    onehot = (chosen[:, None] == jnp.arange(experts, dtype=jnp.int32)[None, :]).astype(jnp.int32)
    before = jnp.cumsum(onehot, axis=0) - onehot
    place = jnp.sum(before * onehot, axis=1)
    kept = (jnp.sum(onehot, axis=1) > 0) & (place < CAP)
    target = chosen * CAP + place
    select = (
        (target[:, None] == jnp.arange(slots, dtype=jnp.int32)[None, :]) & kept[:, None]
    ).astype(jnp.float32)
    select = select.reshape(2, tok_rows, slots)
    member = select[0] + select[1]
    weighted = select[0] * gates[:, 0:1] + select[1] * gates[:, 1:2]
    outbound = lax.dot_general(
        member.astype(jnp.bfloat16),
        tokens,
        (((0,), (0,)), ((), ())),
        preferred_element_type=jnp.float32,
    ).astype(jnp.bfloat16)
    w_both = jnp.concatenate([w_gate[0], w_up[0]], axis=1)
    copies = jnp.broadcast_to(
        outbound.reshape(experts, 1, CAP, width), (experts, QUARTERS, CAP, width)
    ).reshape(n_expert, CAP, width)
    arrived = lax.all_to_all(copies, "expert", split_axis=0, concat_axis=0, tiled=True)
    both = jnp.dot(
        lax.all_gather(arrived[None], "dp", axis=0, tiled=True).reshape(-1, width),
        w_both,
        preferred_element_type=jnp.float32,
    )
    pre_gate = both[:, :fdev]
    pre_up = both[:, fdev:]
    hidden = (jax.nn.silu(pre_gate) * pre_up).astype(jnp.bfloat16)
    part = hidden
    reduced = lax.psum_scatter(
        jnp.dot(part, w_down[0], preferred_element_type=jnp.float32).astype(jnp.bfloat16),
        "dp",
        scatter_dimension=0,
        tiled=True,
    )
    returned = lax.all_to_all(
        reduced.reshape(n_expert, CAP, width), "expert", split_axis=0, concat_axis=0, tiled=True
    )
    expert_out = jnp.sum(
        returned.reshape(experts, QUARTERS, CAP, width).astype(jnp.float32), axis=1
    ).reshape(slots, width)
    upstream = grad_mixed.astype(jnp.float32)
    mixed = (tokens.astype(jnp.float32) + jnp.dot(weighted, expert_out, precision=precise)).astype(
        jnp.bfloat16
    )
    scores = jnp.dot(upstream, expert_out.T, precision=precise)
    grad_gates = jnp.stack(
        [jnp.sum(select[0] * scores, axis=1), jnp.sum(select[1] * scores, axis=1)], axis=1
    )
    scaled = jnp.dot(weighted.T, upstream, precision=precise).astype(jnp.bfloat16)
    grad_copies = jnp.broadcast_to(
        scaled.reshape(experts, 1, CAP, width), (experts, QUARTERS, CAP, width)
    ).reshape(n_expert, CAP, width)
    grad_arrived = lax.all_to_all(grad_copies, "expert", split_axis=0, concat_axis=0, tiled=True)
    grad_hidden = lax.dot_general(
        lax.all_gather(grad_arrived[None], "dp", axis=0, tiled=True).reshape(-1, width),
        w_down[0],
        (((1,), (1,)), ((), ())),
        preferred_element_type=jnp.float32,
    )
    sigmoid_gate = jax.nn.sigmoid(pre_gate)
    grad_a = (grad_hidden * pre_up * sigmoid_gate * (1.0 + pre_gate * (1.0 - sigmoid_gate))).astype(
        jnp.bfloat16
    )
    grad_b = (grad_hidden * pre_gate * sigmoid_gate).astype(jnp.bfloat16)
    joined = jnp.concatenate([grad_a, grad_b], axis=1)
    part = joined
    grad_reduced = lax.psum_scatter(
        lax.dot_general(
            part, w_both, (((1,), (1,)), ((), ())), preferred_element_type=jnp.float32
        ).astype(jnp.bfloat16),
        "dp",
        scatter_dimension=0,
        tiled=True,
    )
    grad_returned = lax.all_to_all(
        grad_reduced.reshape(n_expert, CAP, width),
        "expert",
        split_axis=0,
        concat_axis=0,
        tiled=True,
    )
    grad_rows = jnp.sum(
        grad_returned.reshape(experts, QUARTERS, CAP, width).astype(jnp.float32), axis=1
    ).reshape(slots, width)
    grad_tokens = (upstream + jnp.dot(member, grad_rows, precision=precise)).astype(jnp.bfloat16)
    return (mixed, grad_tokens, grad_gates)


def solution(mesh):
    return jax.shard_map(
        shards,
        mesh=mesh,
        in_specs=(
            P(("dp", "expert"), None),
            P(("dp", "expert"), None),
            P(("dp", "expert"), None),
            P(("dp", "expert"), None),
            P("expert", None, "dp"),
            P("expert", None, "dp"),
            P("expert", "dp", None),
        ),
        out_specs=(P(("dp", "expert"), None), P(("dp", "expert"), None), P(("dp", "expert"), None)),
        check_vma=False,
    )
```

profile of v0, /device:TPU:1, one launch (start us, length us, event | category | flops | bytes accessed | tf_op | source)
XLA Modules:
  0.0 254.5 jit_solution(9238786884693307322)
XLA Ops:
  9.1 1.8 convolution_convert_fusion.3
  11.5 25.3 %all_to_all.20 = bf16[32,2,7168]{2,1,0:T(2,128)(2,1)} all-to-all(bf16[32,2,7168]{2,1,0:T(2,128)(2,1)S(1)} %bitcast.43), channel_id=1, replica_groups=mesh['dp'=4,'expert'=32] {'expert'}, dimensions={0} | all-to-all | bytes 1835008 | tf_op jit(solution)/shard_map/all_to_all | solution.py:40
  38.3 19.6 %all_to_all.21 = bf16[32,2,7168]{2,1,0:T(2,128)(2,1)} all-to-all(bf16[32,2,7168]{2,1,0:T(2,128)(2,1)S(1)} %bitcast.44), channel_id=1, replica_groups=mesh['dp'=4,'expert'=32] {'expert'}, dimensions={0} | all-to-all | bytes 1835008 | tf_op jit(solution)/shard_map/all_to_all | solution.py:74
  58.0 20.2 %all-gather.5.cloned.1.call-done = bf16[128,2,7168]{2,1,0:T(2,128)(2,1)} async-done(((bf16[32,2,7168]{2,1,0:T(2,128)(2,1)}), bf16[128,2,7168]{2,1,0:T(2,128)(2,1)}) %all-gather.5.cloned.1.call-update) | async-done | bytes 3670032 | tf_op jit(solution)/shard_map/all_gather | solution.py:42
  78.2 8.4 %reshape.88 = bf16[256,7168]{1,0:T(8,128)(2,1)} reshape(bf16[128,2,7168]{2,1,0:T(2,128)(2,1)} %all-gather.5.cloned.1.call-done) | data formatting | bytes 7340032 | tf_op jit(solution)/shard_map/reshape | solution.py:42
  86.6 7.0 %fusion.2 = f32[256,512]{1,0:T(8,128)S(1)} fusion(bf16[256,7168]{1,0:T(8,128)(2,1)} %reshape.88, bf16[7168,256]{1,0:T(8,128)(2,1)} %bitcast.47, bf16[7168,256]{1,0:T(8,128)(2,1)} %bitcast.49), kind=kOutput, calls=%fused_computation.9 | convolution fusion | flops 1893728256 | bytes 11534336 | tf_op jit(solution)/shard_map/dot_general | solution.py:41
  93.6 3.0 %convolution_convert_fusion.1 = bf16[256,7168]{1,0:T(8,128)(2,1)} fusion(bf16[1,256,7168]{2,1,0:T(8,128)(2,1)S(1)} %copy-done.1, f32[256,512]{1,0:T(8,128)S(1)} %fusion.2), kind=kOutput, calls=%fused_computation.1 | convolution fusion | flops 941752320 | bytes 7864320 | tf_op jit(solution)/shard_map/dot_general | solution.py:51
  96.8 27.2 %all-gather.7.cloned.1.call-done = bf16[128,2,7168]{2,1,0:T(2,128)(2,1)} async-done(((bf16[32,2,7168]{2,1,0:T(2,128)(2,1)}), bf16[128,2,7168]{2,1,0:T(2,128)(2,1)}) %all-gather.7.cloned.1.call-update) | async-done | bytes 3670032 | tf_op jit(solution)/shard_map/all_gather | solution.py:76
  124.1 8.4 %reshape.92 = bf16[256,7168]{1,0:T(8,128)(2,1)} reshape(bf16[128,2,7168]{2,1,0:T(2,128)(2,1)} %all-gather.7.cloned.1.call-done) | data formatting | bytes 7340032 | tf_op jit(solution)/shard_map/reshape | solution.py:76
  132.4 4.5 %multiply_convert_fusion.1 = (bf16[256,256]{1,0:T(8,128)(2,1)S(1)}, bf16[256,256]{1,0:T(8,128)(2,1)S(1)}) fusion(f32[256,512]{1,0:T(8,128)S(1)} %fusion.2, bf16[256,7168]{1,0:T(8,128)(2,1)} %reshape.92, bf16[1,256,7168]{2,1,0:T(8,128)(2,1)} %param.13), kind=kOutput, calls=%fused_computation.20 | convolution fusion | flops 940376064 | bytes 8126464 | tf_op jit(solution)/shard_map/dot_general | solution.py:75
  137.3 1.1 copy-done.4
  138.4 3.6 %convolution_convert_fusion = bf16[256,7168]{1,0:T(8,128)(2,1)} fusion(bf16[7168,256]{1,0:T(8,128)(2,1)S(1)} %bitcast.48, bf16[7168,256]{1,0:T(8,128)(2,1)S(1)} %bitcast.50, bf16[256,256]{1,0:T(8,128)(2,1)S(1)} %get-tuple-element.8, bf16[256,256]{1,0:T(8,128)(2,1)S(1)} %get-tuple-element.7), kind=kOutput, calls=%fused_computation | convolution fusion | flops 1896087552 | bytes 11272192 | tf_op jit(solution)/shard_map/dot_general | solution.py:89
  142.0 27.3 %reduce-scatter.3.cloned.1.call-done = bf16[64,7168]{1,0:T(8,128)(2,1)} async-done(((bf16[256,7168]{1,0:T(8,128)(2,1)}), bf16[64,7168]{1,0:T(8,128)(2,1)}) %reduce-scatter.3.cloned.1.call-update) | async-done | bytes 917520 | tf_op jit(solution)/shard_map/reduce_scatter | solution.py:50
  169.3 3.1 %reshape.89 = bf16[32,2,7168]{2,1,0:T(2,128)(2,1)} reshape(bf16[64,7168]{1,0:T(8,128)(2,1)} %reduce-scatter.3.cloned.1.call-done) | data formatting | bytes 1835008 | tf_op jit(solution)/shard_map/reshape | solution.py:57
  172.4 7.6 %all-to-all-start.1 = ((bf16[32,2,7168]{2,1,0:T(2,128)(2,1)}), bf16[32,2,7168]{2,1,0:T(2,128)(2,1)S(1)}, u32[]{:S(2)}, u32[]{:S(2)}) async-start(bf16[32,2,7168]{2,1,0:T(2,128)(2,1)} %reshape.89), calls=%async_computation.2 | async-start | bytes 1835008 | tf_op jit(solution)/shard_map/all_to_all | solution.py:56
  180.1 33.8 %reduce-scatter.5.cloned.1.call-done = bf16[64,7168]{1,0:T(8,128)(2,1)} async-done(((bf16[256,7168]{1,0:T(8,128)(2,1)}), bf16[64,7168]{1,0:T(8,128)(2,1)}) %reduce-scatter.5.cloned.1.call-update) | async-done | bytes 917520 | tf_op jit(solution)/shard_map/reduce_scatter | solution.py:88
  213.9 3.1 %reshape.93 = bf16[32,2,7168]{2,1,0:T(2,128)(2,1)} reshape(bf16[64,7168]{1,0:T(8,128)(2,1)} %reduce-scatter.5.cloned.1.call-done) | data formatting | bytes 1835008 | tf_op jit(solution)/shard_map/reshape | solution.py:97
  217.0 7.7 %all-to-all-start.3 = ((bf16[32,2,7168]{2,1,0:T(2,128)(2,1)}), bf16[32,2,7168]{2,1,0:T(2,128)(2,1)}, u32[]{:S(2)}, u32[]{:S(2)}) async-start(bf16[32,2,7168]{2,1,0:T(2,128)(2,1)} %reshape.93), calls=%async_computation.5 | async-start | bytes 1835008 | tf_op jit(solution)/shard_map/all_to_all | solution.py:96
  224.7 0.9 convert_reduce_fusion.1
  225.9 1.5 multiply_reduce_fusion.1
  227.4 5.5 %fusion = bf16[128,7168]{1,0:T(8,128)(2,1)} fusion(f32[16,7168]{1,0:T(8,128)S(1)} %reshape.90, bf16[128,7168]{1,0:T(8,128)(2,1)} %param.7, f32[256,16]{0,1:T(8,128)S(1)} %fusion.11, f32[128]{0:T(128)S(1)} %get-tuple-element.10, f32[128]{0:T(128)S(1)} %get-tuple-element.9), kind=kOutput, calls=%fused_computation.4 | convolution fusion | flops 178919424 | bytes 4146176 | tf_op jit(solution)/shard_map/dot_general | solution.py:63
  232.9 7.6 %all-to-all-done.3 = bf16[32,2,7168]{2,1,0:T(2,128)(2,1)} async-done(((bf16[32,2,7168]{2,1,0:T(2,128)(2,1)}), bf16[32,2,7168]{2,1,0:T(2,128)(2,1)}, u32[]{:S(2)}, u32[]{:S(2)}) %all-to-all-start.3) | async-done | bytes 917536 | tf_op jit(solution)/shard_map/all_to_all | solution.py:96
  240.5 2.3 convert_reduce_fusion
  243.1 4.3 %fusion.1 = bf16[128,7168]{1,0:T(8,128)(2,1)} fusion(f32[16,7168]{1,0:T(8,128)S(1)} %reshape.94, bf16[128,7168]{1,0:T(8,128)(2,1)S(1)} %copy-done, f32[256,16]{0,1:T(8,128)S(1)} %fusion.11), kind=kOutput, calls=%fused_computation.5 | convolution fusion | flops 178915328 | bytes 4145152 | tf_op jit(solution)/shard_map/dot_general | solution.py:106
  (38 shorter events, 5.8 us)
Async XLA Ops:
  7.2 29.7 %copy-start.2 = (f32[128,2]{0,1:T(2,128)S(1)}, f32[128,2]{0,1:T(2,128)}, u32[]{:S(2)}) copy-start(f32[128,2]{0,1:T(2,128)} %param.9) | copy-start | bytes 3076
  7.2 29.7 %copy-start = (bf16[128,7168]{1,0:T(8,128)(2,1)S(1)}, bf16[128,7168]{1,0:T(8,128)(2,1)}, u32[]{:S(2)}) copy-start(bf16[128,7168]{1,0:T(8,128)(2,1)} %param.10) | copy-start | bytes 5505028
  7.2 71.0 %all-gather.5.cloned.1.call-start = ((), (), s32[]{:S(2)}) async-start(), calls=%async_computation.8 | async-start | bytes 4587520 | tf_op jit(solution)/shard_map/all_gather | solution.py:42
  36.8 87.3 %all-gather.7.cloned.1.call-start = ((), (), s32[]{:S(2)}) async-start(), calls=%async_computation.9 | async-start | bytes 4587520 | tf_op jit(solution)/shard_map/all_gather | solution.py:76
  57.9 111.4 %reduce-scatter.3.cloned.1.call-start = ((), (), s32[]{:S(2)}) async-start(), calls=%async_computation.6 | async-start | bytes 4587520 | tf_op jit(solution)/shard_map/reduce_scatter | solution.py:50
  86.6 7.0 %copy-start.1 = (bf16[1,256,7168]{2,1,0:T(8,128)(2,1)S(1)}, bf16[1,256,7168]{2,1,0:T(8,128)(2,1)}, u32[]{:S(2)}) copy-start(bf16[1,256,7168]{2,1,0:T(8,128)(2,1)} %param.13) | copy-start | bytes 11010052
  96.6 117.3 %reduce-scatter.5.cloned.1.call-start = ((), (), s32[]{:S(2)}) async-start(), calls=%async_computation.7 | async-start | bytes 4587520 | tf_op jit(solution)/shard_map/reduce_scatter | solution.py:88
  132.4 4.9 %copy-start.3 = (bf16[1,7168,256]{2,1,0:T(8,128)(2,1)S(1)}, bf16[1,7168,256]{2,1,0:T(8,128)(2,1)}, u32[]{:S(2)}) copy-start(bf16[1,7168,256]{2,1,0:T(8,128)(2,1)} %param.12) | copy-start | bytes 11010052
  132.4 6.0 %copy-start.4 = (bf16[1,7168,256]{2,1,0:T(8,128)(2,1)S(1)}, bf16[1,7168,256]{2,1,0:T(8,128)(2,1)}, u32[]{:S(2)}) copy-start(bf16[1,7168,256]{2,1,0:T(8,128)(2,1)} %param.11) | copy-start | bytes 11010052
  172.4 44.6 %all-to-all-start.1 = ((bf16[32,2,7168]{2,1,0:T(2,128)(2,1)}), bf16[32,2,7168]{2,1,0:T(2,128)(2,1)S(1)}, u32[]{:S(2)}, u32[]{:S(2)}) async-start(bf16[32,2,7168]{2,1,0:T(2,128)(2,1)} %reshape.89), calls=%async_computation.2 | async-start | bytes 1835008 | tf_op jit(solution)/shard_map/all_to_all | solution.py:56
  217.0 23.5 %all-to-all-start.3 = ((bf16[32,2,7168]{2,1,0:T(2,128)(2,1)}), bf16[32,2,7168]{2,1,0:T(2,128)(2,1)}, u32[]{:S(2)}, u32[]{:S(2)}) async-start(bf16[32,2,7168]{2,1,0:T(2,128)(2,1)} %reshape.93), calls=%async_computation.5 | async-start | bytes 1835008 | tf_op jit(solution)/shard_map/all_to_all | solution.py:96
Sparse Core Ops, SparseCore 0:
  36.9 41.2 all-gather.4
  79.9 44.1 all-gather.6
  126.5 42.8 reduce-scatter.2
  171.6 42.2 reduce-scatter.4
where the time goes:
time: 255 us
  waiting for transfers between devices  116 us (45%)
  blocking collectives  44.9 us (18%)
  matrix products  32 us (13%)
  local copies, waits for them, and re-layouts  27.3 us (11%)
  starting transfers between devices  15.7 us (6%)
  between operations  13.9 us (5%)
  other arithmetic  4.48 us (2%)
    reduce_scatter x1, waiting for transfers between devices, shards(): lax.psum_scatter(lax.dot_general(part, w_both, (((1,), (1,)), ((), ())),...  33.8 us
    reduce_scatter x1, waiting for transfers between devices, shards(): lax.psum_scatter(jnp.dot(part, w_down[0], preferred_element_type=jnp.floa...  27.3 us
    all_gather x1, waiting for transfers between devices, shards(): lax.all_gather(grad_arrived[None], 'dp', axis=0, tiled=True)  27.2 us
    all_to_all x1, blocking collectives, shards(): lax.all_to_all(copies, 'expert', split_axis=0, concat_axis=0, tiled=True)  25.3 us
    all_gather x1, waiting for transfers between devices, shards(): lax.all_gather(arrived[None], 'dp', axis=0, tiled=True).reshape(-1, width)  20.2 us
    all_to_all x1, blocking collectives, shards(): lax.all_to_all(grad_copies, 'expert', split_axis=0, concat_axis=0, tiled=...  19.6 us
    reshape x1, local copies, waits for them, and re-layouts, shards(): lax.all_gather(arrived[None], 'dp', axis=0, tiled=True).reshape(-1, width)  8.39 us
    reshape x1, local copies, waits for them, and re-layouts, shards(): lax.all_gather(grad_arrived[None], 'dp', axis=0, tiled=True)  8.39 us
  transfers between devices with their start and end apart: 6, of which 5 were waited for; matrix products, arithmetic and copies ran while one was open for 20% of the time, Pallas kernels for 0%

commit v1 on v0

v1 whole, which is shorter than its diff:
```python
import functools

import jax
import jax.numpy as jnp
from jax import lax
from jax.experimental import pallas as pl
from jax.experimental.pallas import tpu as pltpu
from jax.sharding import PartitionSpec as P

BF = jnp.bfloat16
F32 = jnp.float32
VMEM = pl.BlockSpec(memory_space=pltpu.VMEM)
ANY = pl.BlockSpec(memory_space=pl.ANY)
LIMIT = 48 * 1024 * 1024
NZ = 4
STEPS = 7


def dot(a, b, dims):
    return lax.dot_general(a, b, (dims, ((), ())), preferred_element_type=F32)


def place_of(index):
    return index // 8, (index // 4) % 2, (index // 2) % 2, index % 2


def index_of(z, h, l, c):
    return ((z * 2 + h) * 2 + l) * 2 + c


def over_expert(value, move):
    pairs = []
    for at in range(32):
        pairs.append((at, index_of(*move(*place_of(at)))))
    return lax.ppermute(value, "expert", pairs)


def other_core(value):
    return over_expert(value, lambda z, h, l, c: (z, h, l, 1 - c))


def other_l(value):
    return over_expert(value, lambda z, h, l, c: (z, h, 1 - l, c))


def out_to(value, i):
    k, r = i // 2, i % 2
    return over_expert(value, lambda z, h, l, c: ((z + k) % NZ, h ^ r, l ^ r, c))


def back_to(value, i):
    k, r = i // 2, i % 2
    return over_expert(value, lambda z, h, l, c: ((z - k) % NZ, h ^ r, l ^ r, c))


def along_x(value, step):
    return lax.ppermute(value, "dp", [(x, (x + step) % 4) for x in range(4)])


def selection(ids, rows, expert, place):
    tok = ids.shape[1]
    up = (lax.broadcasted_iota(jnp.int32, (tok, tok), 0) < lax.broadcasted_iota(jnp.int32, (tok, tok), 1))
    up = jnp.where(up, 1.0, 0.0).astype(BF)
    first = jnp.where(jnp.broadcast_to(ids[0:1, :], (rows, tok)) == expert, 1.0, 0.0)
    second = jnp.where(jnp.broadcast_to(ids[1:2, :], (rows, tok)) == expert, 1.0, 0.0)
    before_first = dot(first.astype(BF), up, ((1,), (0,)))
    before_second = dot(second.astype(BF), up, ((1,), (0,))) + jnp.sum(first, axis=1, keepdims=True)
    want = place.astype(F32)
    sel_first = jnp.where(before_first == want, first, 0.0)
    sel_second = jnp.where(before_second == want, second, 0.0)
    return sel_first, sel_second


def slot_expert(i, z, h):
    return ((z + (i >> 1)) & 3) * 2 + ((h + (i & 1)) & 1)


def dispatch_kernel(half, ids_ref, gates_ref, tok_hbm, grad_hbm, keep_ref, send_ref, tok_v, grad_v, sems):
    at = lax.axis_index("expert")
    core = at & 1
    h = (at >> 2) & 1
    z = at >> 3
    copies = []
    for n, which in enumerate((1 - core, core)):
        cols = pl.ds(pl.multiple_of(which * half, 128), half)
        one = pltpu.make_async_copy(tok_hbm.at[:, cols], tok_v.at[n], sems.at[n, 0])
        two = pltpu.make_async_copy(grad_hbm.at[:, cols], grad_v.at[n], sems.at[n, 1])
        one.start()
        two.start()
        copies.append((one, two))
    rows, tok = 64, ids_ref.shape[1]
    s = lax.broadcasted_iota(jnp.int32, (rows, tok), 0)
    sel_first, sel_second = selection(ids_ref[...], rows, slot_expert(s >> 3, z, h), s & 1)
    mine = ((s >> 1) & 1) == core
    is_grad = ((s >> 2) & 1) == 1
    member = jnp.where(mine, sel_first + sel_second, 0.0)
    gate = jnp.sum(
        sel_first * jnp.broadcast_to(gates_ref[0:1, :], (rows, tok))
        + sel_second * jnp.broadcast_to(gates_ref[1:2, :], (rows, tok)),
        axis=1,
        keepdims=True,
    )
    of_tok = jnp.where(is_grad, 0.0, member).astype(BF)
    of_grad = jnp.where(is_grad, member, 0.0).astype(BF)
    for n, out in enumerate((send_ref, keep_ref)):
        copies[n][0].wait()
        copies[n][1].wait()
        got = dot(of_tok, tok_v[n], ((1,), (0,))) + dot(of_grad, grad_v[n], ((1,), (0,))) * gate
        out[...] = got.astype(BF)


def merge_kernel(keep_ref, recv_ref, *outs):
    both = keep_ref[...].astype(F32) + recv_ref[...].astype(F32)
    for i, out in enumerate(outs):
        out[...] = both[8 * i : 8 * i + 8, :].astype(BF)


def assemble_kernel(*refs):
    msgs, (tok_ref, grad_ref), wide = refs[:8], refs[8:10], refs[10]
    for i, m in enumerate(msgs):
        wide[pl.ds(8 * i, 8), :] = m[...].astype(F32)
    full = wide[...].astype(BF)
    s = lax.broadcasted_iota(jnp.int32, (32, 64), 0)
    t = lax.broadcasted_iota(jnp.int32, (32, 64), 1)
    base = (s >> 2) * 8 + (s & 3)
    tok_ref[...] = dot(jnp.where(t == base, 1.0, 0.0).astype(BF), full, ((1,), (0,))).astype(BF)
    grad_ref[...] = dot(jnp.where(t == base + 4, 1.0, 0.0).astype(BF), full, ((1,), (0,))).astype(BF)


def up_kernel(core_ref, *refs):
    chunks = refs[:8]
    wg_own, wu_own, wg_got, wu_got, out, rows = refs[8:]
    step = pl.program_id(0)
    for n, chunk in enumerate(chunks):
        rows[pl.ds(32 * n, 32), :] = chunk[...]
    x = rows[...]

    @pl.when(step == 0)
    def _():
        out[...] = jnp.zeros_like(out)

    out[:, 0:256] += dot(x, wg_own[0], ((1,), (0,)))
    out[:, 256:512] += dot(x, wg_got[...], ((1,), (0,)))
    out[:, 512:768] += dot(x, wu_own[0], ((1,), (0,)))
    out[:, 768:1024] += dot(x, wu_got[...], ((1,), (0,)))


def summed(mine, got, base):
    return jnp.concatenate(
        [
            mine[:, base : base + 256] + got[:, base + 256 : base + 512],
            mine[:, base + 256 : base + 512] + got[:, base : base + 256],
        ],
        axis=1,
    )


def down_kernel(core_ref, mine, got, wd_own, wd_got, *refs):
    outs, hidden = refs[:8], refs[8]

    @pl.when(pl.program_id(0) == 0)
    def _():
        a = summed(mine, got, 0)
        b = summed(mine, got, 512)
        hidden[...] = (a * jax.nn.sigmoid(a) * b).astype(BF)

    res = dot(hidden[:, 0:256], wd_own[0], ((1,), (0,))) + dot(hidden[:, 256:512], wd_got[...], ((1,), (0,)))
    res = res.astype(BF)
    for n, out in enumerate(outs):
        out[...] = res[32 * n : 32 * n + 32, :]


def down_back_kernel(core_ref, *refs):
    chunks = refs[:8]
    wd_own, wd_got, out, rows = refs[8:]
    for n, chunk in enumerate(chunks):
        rows[pl.ds(32 * n, 32), :] = chunk[...]
    g = rows[...]

    @pl.when(pl.program_id(0) == 0)
    def _():
        out[...] = jnp.zeros_like(out)

    out[:, 0:256] += dot(g, wd_own[0], ((1,), (1,)))
    out[:, 256:512] += dot(g, wd_got[...], ((1,), (1,)))


def up_back_kernel(core_ref, mine, got, g_mine, g_got, wg_own, wu_own, wg_got, wu_got, *refs):
    outs, (ga_ref, gb_ref) = refs[:8], refs[8:]

    @pl.when(pl.program_id(0) == 0)
    def _():
        a = summed(mine, got, 0)
        b = summed(mine, got, 512)
        gh = summed(g_mine, g_got, 0)
        sg = jax.nn.sigmoid(a)
        ga_ref[...] = (gh * b * sg * (1.0 + a * (1.0 - sg))).astype(BF)
        gb_ref[...] = (gh * a * sg).astype(BF)

    res = dot(ga_ref[:, 0:256], wg_own[0], ((1,), (1,)))
    res += dot(ga_ref[:, 256:512], wg_got[...], ((1,), (1,)))
    res += dot(gb_ref[:, 0:256], wu_own[0], ((1,), (1,)))
    res += dot(gb_ref[:, 256:512], wu_got[...], ((1,), (1,)))
    res = res.astype(BF)
    for n, out in enumerate(outs):
        out[...] = res[32 * n : 32 * n + 32, :]


def add_kernel(*refs):
    total = refs[0][...].astype(F32)
    for ref in refs[1:-1]:
        total += ref[...].astype(F32)
    refs[-1][...] = total.astype(BF)


def split_kernel(*refs):
    terms, outs = refs[:-8], refs[-8:]
    total = terms[0][...].astype(F32)
    for ref in terms[1:]:
        total += ref[...].astype(F32)
    for i, out in enumerate(outs):
        out[...] = total[4 * i : 4 * i + 4, :].astype(BF)


def cores_kernel(*refs):
    msgs, (own_ref, send_ref), wide = refs[:8], refs[8:10], refs[10]
    core = lax.axis_index("expert") & 1
    for i, m in enumerate(msgs):
        wide[pl.ds(8 * i, 4), :] = m[...].astype(F32)
        wide[pl.ds(8 * i + 4, 4), :] = jnp.zeros((4, wide.shape[1]), F32)
    full = wide[...].astype(BF)
    s = lax.broadcasted_iota(jnp.int32, (16, 64), 0)
    t = lax.broadcasted_iota(jnp.int32, (16, 64), 1)
    base = (s >> 1) * 8 + (s & 1)
    own_ref[...] = dot(jnp.where(t == base + 2 * core, 1.0, 0.0).astype(BF), full, ((1,), (0,))).astype(BF)
    send_ref[...] = dot(jnp.where(t == base + 2 - 2 * core, 1.0, 0.0).astype(BF), full, ((1,), (0,))).astype(BF)


def slots_of(ids_ref, at):
    rows, tok = 16, ids_ref.shape[1]
    s = lax.broadcasted_iota(jnp.int32, (rows, tok), 0)
    return selection(ids_ref[...], rows, slot_expert(s >> 1, at >> 3, (at >> 2) & 1), s & 1)


def mixed_kernel(half, ids_ref, gates_ref, tok_ref, grad_ref, own_ref, got_ref, out_ref, gg_ref):
    at = lax.axis_index("expert")
    core = at & 1
    sel_first, sel_second = slots_of(ids_ref, at)
    member = (sel_first + sel_second).astype(BF)
    gate = jnp.sum(
        sel_first * jnp.broadcast_to(gates_ref[0:1, :], sel_first.shape)
        + sel_second * jnp.broadcast_to(gates_ref[1:2, :], sel_first.shape),
        axis=1,
        keepdims=True,
    )
    inner = jnp.zeros((16, 1), F32)
    for n, ref in enumerate((own_ref, got_ref)):
        which = core if n == 0 else 1 - core
        cols = pl.ds(pl.multiple_of(which * half, 128), half)
        rows = ref[...].astype(F32)
        inner += jnp.sum(dot(member, grad_ref[:, cols], ((1,), (0,))) * rows, axis=1, keepdims=True)
        scaled = rows * gate
        high = scaled.astype(BF)
        low = (scaled - high.astype(F32)).astype(BF)
        add = dot(member, high, ((0,), (0,))) + dot(member, low, ((0,), (0,)))
        out_ref[:, cols] = (tok_ref[:, cols].astype(F32) + add).astype(BF)
    gg_ref[0:1, :] = jnp.sum(sel_first * inner, axis=0, keepdims=True)
    gg_ref[1:2, :] = jnp.sum(sel_second * inner, axis=0, keepdims=True)


def grad_tokens_kernel(half, ids_ref, grad_ref, own_ref, got_ref, out_ref):
    at = lax.axis_index("expert")
    core = at & 1
    sel_first, sel_second = slots_of(ids_ref, at)
    member = (sel_first + sel_second).astype(BF)
    for n, ref in enumerate((own_ref, got_ref)):
        which = core if n == 0 else 1 - core
        cols = pl.ds(pl.multiple_of(which * half, 128), half)
        add = dot(member, ref[...], ((0,), (0,)))
        out_ref[:, cols] = (grad_ref[:, cols].astype(F32) + add).astype(BF)


def params():
    return pltpu.CompilerParams(vmem_limit_bytes=LIMIT)


def shape(rows, cols, dtype=BF):
    return jax.ShapeDtypeStruct((rows, cols), dtype)


def whole(kernel, outs, args, scratch=(), specs=None):
    return pl.pallas_call(
        kernel,
        out_shape=outs,
        in_specs=specs or [VMEM] * len(args),
        out_specs=jax.tree.map(lambda _: VMEM, outs),
        scratch_shapes=list(scratch),
        compiler_params=params(),
    )(*args)


def stepped(kernel, core, args, in_specs, outs, out_specs, scratch):
    return pl.pallas_call(
        kernel,
        grid_spec=pltpu.PrefetchScalarGridSpec(
            num_scalar_prefetch=1,
            grid=(STEPS,),
            in_specs=in_specs,
            out_specs=out_specs,
            scratch_shapes=scratch,
        ),
        out_shape=outs,
        compiler_params=params(),
    )(core, *args)


def shards(tokens, expert_ids, gates, grad_mixed, w_gate, w_up, w_down):
    tok, width = tokens.shape
    half = width // 2
    block = half // STEPS
    core = lax.axis_index("expert") % 2
    core1 = core.reshape(1).astype(jnp.int32)
    ids_t = expert_ids.T
    gates_t = gates.T

    keep, send = whole(
        functools.partial(dispatch_kernel, half),
        [shape(64, half)] * 2,
        (ids_t, gates_t, tokens, grad_mixed),
        [pltpu.VMEM((2, tok, half), BF), pltpu.VMEM((2, tok, half), BF), pltpu.SemaphoreType.DMA((2, 2))],
        [VMEM, VMEM, ANY, ANY],
    )
    recv = other_core(send)
    wg_got = other_core(lax.dynamic_slice(w_gate[0], ((1 - core) * half, 0), (half, w_gate.shape[2])))
    wu_got = other_core(lax.dynamic_slice(w_up[0], ((1 - core) * half, 0), (half, w_up.shape[2])))
    wd_got = other_core(lax.dynamic_slice(w_down[0], (0, (1 - core) * half), (w_down.shape[1], half)))
    msgs = whole(merge_kernel, [shape(8, half)] * 8, (keep, recv))
    msgs = [msgs[0]] + [out_to(msgs[i], i) for i in range(1, 8)]
    t00, g00 = whole(assemble_kernel, [shape(32, half)] * 2, msgs, [pltpu.VMEM((64, half), F32)])

    t = {(0, 0): t00}
    t[3, 0] = along_x(t00, 1)
    t[1, 0] = along_x(t00, -1)
    t[0, 1] = other_l(t00)
    t[3, 1] = along_x(t[0, 1], 1)
    t[1, 1] = along_x(t[0, 1], -1)
    t[2, 0] = along_x(t[3, 0], 1)
    t[2, 1] = along_x(t[1, 1], -1)
    order = [(a, b) for a in range(4) for b in range(2)]
    g = {(0, 0): g00}
    g[3, 0] = along_x(g00, 1)
    g[1, 0] = along_x(g00, -1)
    g[0, 1] = other_l(g00)
    g[1, 1] = other_l(g[1, 0])
    g[3, 1] = other_l(g[3, 0])
    g[2, 0] = along_x(g[3, 0], 1)
    g[2, 1] = along_x(g[1, 1], -1)

    fdev = w_gate.shape[2]
    chunk_spec = [pl.BlockSpec((32, block), lambda n, c: (0, n))] * 8
    up_own = pl.BlockSpec((1, block, fdev), lambda n, c: (0, c[0] * STEPS + n, 0))
    up_got = pl.BlockSpec((block, fdev), lambda n, c: (n, 0))
    down_own = pl.BlockSpec((1, fdev, block), lambda n, c: (0, 0, c[0] * STEPS + n))
    down_got = pl.BlockSpec((fdev, block), lambda n, c: (0, n))

    def resident(rows, cols):
        return pl.BlockSpec((rows, cols), lambda n, c: (0, 0))

    part = stepped(
        up_kernel,
        core1,
        [t[o] for o in order] + [w_gate, w_up, wg_got, wu_got],
        chunk_spec + [up_own, up_own, up_got, up_got],
        shape(256, 4 * fdev, F32),
        resident(256, 4 * fdev),
        [pltpu.VMEM((256, block), BF)],
    )
    part_got = other_core(part)
    q = stepped(
        down_kernel,
        core1,
        [part, part_got, w_down, wd_got],
        [resident(256, 4 * fdev)] * 2 + [down_own, down_got],
        [shape(32, half)] * 8,
        chunk_spec,
        [pltpu.VMEM((256, 2 * fdev), BF)],
    )
    q = dict(zip(order, q))

    def add(*terms):
        total = terms[0].astype(F32)
        for term in terms[1:]:
            total = total + term.astype(F32)
        return total.astype(BF)

    f20 = along_x(q[2, 0], 1)
    f21 = along_x(q[2, 1], -1)
    f11 = along_x(q[1, 1], 1)
    f30 = along_x(q[3, 0], -1)
    f10 = along_x(add(q[1, 0], f20), 1)
    f31 = along_x(add(q[3, 1], f21), -1)
    s1 = add(q[0, 1], f11, f31)
    out_l = other_l(s1)
    omsgs = whole(split_kernel, [shape(4, half)] * 8, (q[0, 0], f10, f30, out_l))
    omsgs = [omsgs[0]] + [back_to(omsgs[i], i) for i in range(1, 8)]
    o_own, o_send = whole(cores_kernel, [shape(16, half)] * 2, omsgs, [pltpu.VMEM((64, half), F32)])
    o_got = other_core(o_send)

    g_part = stepped(
        down_back_kernel,
        core1,
        [g[o] for o in order] + [w_down, wd_got],
        chunk_spec + [down_own, down_got],
        shape(256, 2 * fdev, F32),
        resident(256, 2 * fdev),
        [pltpu.VMEM((256, block), BF)],
    )
    g_part_got = other_core(g_part)
    p = stepped(
        up_back_kernel,
        core1,
        [part, part_got, g_part, g_part_got, w_gate, w_up, wg_got, wu_got],
        [resident(256, 4 * fdev)] * 2 + [resident(256, 2 * fdev)] * 2 + [up_own, up_own, up_got, up_got],
        [shape(32, half)] * 8,
        chunk_spec,
        [pltpu.VMEM((256, 2 * fdev), BF)] * 2,
    )
    p = dict(zip(order, p))
    h20 = along_x(p[2, 0], -1)
    h21 = along_x(p[2, 1], 1)
    y01 = other_l(p[0, 1])
    y31 = other_l(p[3, 1])
    y11 = other_l(add(p[1, 1], h21))
    x30 = along_x(add(p[3, 0], h20, y31), -1)
    x10 = along_x(add(p[1, 0], y11), 1)
    gmsgs = whole(split_kernel, [shape(4, half)] * 8, (p[0, 0], y01, x30, x10))
    gmsgs = [gmsgs[0]] + [back_to(gmsgs[i], i) for i in range(1, 8)]
    r_own, r_send = whole(cores_kernel, [shape(16, half)] * 2, gmsgs, [pltpu.VMEM((64, half), F32)])
    r_got = other_core(r_send)

    mixed, grad_gates = whole(
        functools.partial(mixed_kernel, half),
        [shape(tok, width), shape(2, tok, F32)],
        (ids_t, gates_t, tokens, grad_mixed, o_own, o_got),
    )
    grad_tokens = whole(
        functools.partial(grad_tokens_kernel, half),
        shape(tok, width),
        (ids_t, grad_mixed, r_own, r_got),
    )
    return mixed, grad_tokens, grad_gates.T


def solution(mesh):
    return jax.shard_map(
        shards,
        mesh=mesh,
        in_specs=(
            P(("dp", "expert"), None),
            P(("dp", "expert"), None),
            P(("dp", "expert"), None),
            P(("dp", "expert"), None),
            P("expert", None, "dp"),
            P("expert", None, "dp"),
            P("expert", "dp", None),
        ),
        out_specs=(P(("dp", "expert"), None), P(("dp", "expert"), None), P(("dp", "expert"), None)),
        check_vma=False,
    )
```

time: 255 us -> 196 us (0.77)
  starting transfers between devices: 15.7 us -> 99.7 us
  waiting for transfers between devices: 116 us -> 54.8 us
  blocking collectives: 44.9 us -> 0 us
  Pallas kernels: 0 us -> 32.2 us
  matrix products: 32 us -> 0 us
  local copies, waits for them, and re-layouts: 27.3 us -> 7.01 us
  between operations: 13.9 us -> 0.93 us
  other arithmetic: 4.48 us -> 0.39 us
    ppermute x0 -> x57, starting transfers between devices: none -> 99.7 us  [the longest x37 76.7 us: over_expert(): return lax.ppermute(value, 'expert', pairs)]
    reduce_scatter x2 -> x0, waiting for transfers between devices: 61.1 us -> none  [the longest x1 33.8 us: shards(): lax.psum_scatter(lax.dot_general(part, w_both, (((1,), (1,)), ((), ())),...]
    ppermute x0 -> x57, waiting for transfers between devices: none -> 54.8 us  [the longest x20 40.6 us: along_x(): return lax.ppermute(value, 'dp', [(x, (x + step) % 4) for x in range(4)])]
    all_gather x2 -> x0, waiting for transfers between devices: 47.5 us -> none  [the longest x1 27.2 us: shards(): lax.all_gather(grad_arrived[None], 'dp', axis=0, tiled=True)]
    all_to_all x2 -> x0, blocking collectives: 44.9 us -> none  [the longest x1 25.3 us: shards(): lax.all_to_all(copies, 'expert', split_axis=0, concat_axis=0, tiled=True)]
    pallas_call x0 -> x13, Pallas kernels: none -> 32.2 us  [the longest x4 24.8 us: stepped(): pl.pallas_call(kernel, grid_spec=pltpu.PrefetchScalarGridSpec(num_scalar_...]
    dot_general x9 -> x0, matrix products: 32 us -> none  [the longest x1 6.96 us: shards(): jnp.dot(lax.all_gather(arrived[None], 'dp', axis=0, tiled=True).reshape(-...]
    reshape x6 -> x0, local copies, waits for them, and re-layouts: 23.5 us -> none  [the longest x1 8.39 us: shards(): lax.all_gather(arrived[None], 'dp', axis=0, tiled=True).reshape(-1, width)]
  transfers between devices with their start and end apart: 6 -> 57, of which waited for: 5 -> 21; matrix products, arithmetic and copies ran while one was open for 20% -> 2% of each run, Pallas kernels for 0% -> 11%
where the time goes in v1:
time: 196 us; the launch traced here: 195 us
  starting transfers between devices  99.7 us (51%)
  waiting for transfers between devices  54.8 us (28%)
  Pallas kernels  32.2 us (16%)
  local copies, waits for them, and re-layouts  7.01 us (4%)
    ppermute x37, starting transfers between devices, over_expert(): return lax.ppermute(value, 'expert', pairs)  76.7 us
    ppermute x20, waiting for transfers between devices, along_x(): return lax.ppermute(value, 'dp', [(x, (x + step) % 4) for x in range(4)])  40.6 us
    pallas_call x4, Pallas kernels, stepped(): pl.pallas_call(kernel, grid_spec=pltpu.PrefetchScalarGridSpec(num_scalar_...  24.8 us
    ppermute x20, starting transfers between devices, along_x(): return lax.ppermute(value, 'dp', [(x, (x + step) % 4) for x in range(4)])  23 us
    ppermute x37, waiting for transfers between devices, over_expert(): return lax.ppermute(value, 'expert', pairs)  14.2 us
    pallas_call x9, Pallas kernels, whole(): pl.pallas_call(kernel, out_shape=outs, in_specs=specs or [VMEM] * len(arg...  7.39 us
  transfers between devices with their start and end apart: 57, of which 21 were waited for; matrix products, arithmetic and copies ran while one was open for 2% of the time, Pallas kernels for 11%

profile of v1, /device:TPU:1, one launch (start us, length us, event | category | flops | bytes accessed | tf_op | source)
XLA Modules:
  0.0 195.0 jit_solution(5723729783129296353)
XLA Ops:
  0.7 3.0 %dynamic-slice_bitcast_fusion.2 = bf16[3584,256]{1,0:T(8,128)(2,1)} fusion(bf16[1,7168,256]{2,1,0:T(8,128)(2,1)} %wg_own.1, s32[]{:T(128)S(6)} %select_n.13), kind=kLoop, calls=%fused_computation.2 | loop fusion | bytes 3670020 | tf_op jit(solution)/shard_map/dynamic_slice | solution.py:334
  16.5 4.0 %collective-permute-start.3 = (bf16[8,3584]{1,0:T(8,128)(2,1)S(1)}, bf16[8,3584]{1,0:T(8,128)(2,1)S(1)}, u32[]{:S(2)}, u32[]{:S(2)}) collective-permute-start(bf16[8,3584]{1,0:T(8,128)(2,1)S(1)} %get-tuple-element.58), channel_id=1, source_target_pairs={{0,14},{1,15},{2,12},{3,13},{4,10},{5,11},{6,8},{7,9},{8,22},{9,23... | collective-permute-start | bytes 172040 | tf_op jit(solution)/shard_map/ppermute | solution.py:35
  20.5 3.3 %collective-permute-start.4 = (bf16[8,3584]{1,0:T(8,128)(2,1)S(1)}, bf16[8,3584]{1,0:T(8,128)(2,1)S(1)}, u32[]{:S(2)}, u32[]{:S(2)}) collective-permute-start(bf16[8,3584]{1,0:T(8,128)(2,1)S(1)} %get-tuple-element.59), channel_id=1, source_target_pairs={{0,16},{1,17},{2,18},{3,19},{4,20},{5,21},{6,22},{7,23},{8,24},{9,... | collective-permute-start | bytes 172040 | tf_op jit(solution)/shard_map/ppermute | solution.py:35
  24.1 3.6 %collective-permute-start.5 = (bf16[8,3584]{1,0:T(8,128)(2,1)S(1)}, bf16[8,3584]{1,0:T(8,128)(2,1)S(1)}, u32[]{:S(2)}, u32[]{:S(2)}) collective-permute-start(bf16[8,3584]{1,0:T(8,128)(2,1)S(1)} %get-tuple-element.60), channel_id=1, source_target_pairs={{0,22},{1,23},{2,20},{3,21},{4,18},{5,19},{6,16},{7,17},{8,30},{9,... | collective-permute-start | bytes 172040 | tf_op jit(solution)/shard_map/ppermute | solution.py:35
  30.8 3.7 %collective-permute-start.7 = (bf16[8,3584]{1,0:T(8,128)(2,1)S(1)}, bf16[8,3584]{1,0:T(8,128)(2,1)S(1)}, u32[]{:S(2)}, u32[]{:S(2)}) collective-permute-start(bf16[8,3584]{1,0:T(8,128)(2,1)S(1)} %get-tuple-element.62), channel_id=1, source_target_pairs={{0,30},{1,31},{2,28},{3,29},{4,26},{5,27},{6,24},{7,25},{8,6},{9,7... | collective-permute-start | bytes 172040 | tf_op jit(solution)/shard_map/ppermute | solution.py:35
  37.6 3.6 %collective-permute-done.8.refs_1_ = bf16[32,3584]{1,0:T(8,128)(2,1)S(1)} collective-permute-done((bf16[32,3584]{1,0:T(8,128)(2,1)S(1)}, bf16[32,3584]{1,0:T(8,128)(2,1)S(1)}, u32[]{:S(2)}, u32[]{:S(2)}) %collective-permute-start.8) | collective-permute-done | bytes 229408 | tf_op jit(solution)/shard_map/ppermute | solution.py:35
  49.7 3.4 %collective-permute-done.14.refs_7_ = bf16[32,3584]{1,0:T(8,128)(2,1)S(1)} collective-permute-done((bf16[32,3584]{1,0:T(8,128)(2,1)S(1)}, bf16[32,3584]{1,0:T(8,128)(2,1)S(1)}, u32[]{:S(2)}, u32[]{:S(2)}) %collective-permute-start.14) | collective-permute-done | bytes 229408 | tf_op jit(solution)/shard_map/ppermute | solution.py:57
  59.5 6.7 %shard_map.97.mine = f32[256,1024]{1,0:T(8,128)S(1)} custom-call(s32[1]{0:T(128)} %bitcast.2.core_ref, bf16[32,3584]{1,0:T(8,128)(2,1)S(1)} %get-tuple-element.63.refs_0_, bf16[32,3584]{1,0:T(8,128)(2,1)S(1)} %collective-permute-done.8.refs_1_, bf16[32,3584]{1,0:T(8,128)(2,1)S(1)} %collective-permute-done.9.refs_2_, ...), custom_call_target="tpu_custom_call" | custom-call | tf_op jit(solution)/shard_map/pallas_call | solution.py:303
  66.2 9.3 %collective-permute-start.17 = (f32[256,1024]{1,0:T(8,128)S(1)}, f32[256,1024]{1,0:T(8,128)S(1)}, u32[]{:S(2)}, u32[]{:S(2)}) collective-permute-start(f32[256,1024]{1,0:T(8,128)S(1)} %shard_map.97.mine), channel_id=1, source_target_pairs={{0,1},{1,0},{2,3},{3,2},{4,5},{5,4},{6,7},{7,6},{8,9},{9,8},{10,11... | collective-permute-start | bytes 3145736 | tf_op jit(solution)/shard_map/ppermute | solution.py:35
  77.0 7.4 %collective-permute-done.37.refs_6_ = bf16[32,3584]{1,0:T(8,128)(2,1)S(1)} collective-permute-done((bf16[32,3584]{1,0:T(8,128)(2,1)S(1)}, bf16[32,3584]{1,0:T(8,128)(2,1)S(1)}, u32[]{:S(2)}, u32[]{:S(2)}) %collective-permute-start.37) | collective-permute-done | bytes 229408 | tf_op jit(solution)/shard_map/ppermute | solution.py:57
  84.3 3.1 %collective-permute-done.36.refs_3_ = bf16[32,3584]{1,0:T(8,128)(2,1)S(1)} collective-permute-done((bf16[32,3584]{1,0:T(8,128)(2,1)S(1)}, bf16[32,3584]{1,0:T(8,128)(2,1)S(1)}, u32[]{:S(2)}, u32[]{:S(2)}) %collective-permute-start.36) | collective-permute-done | bytes 229408 | tf_op jit(solution)/shard_map/ppermute | solution.py:35
  87.4 3.0 %collective-permute-start.39 = (bf16[32,3584]{1,0:T(8,128)(2,1)S(1)}, bf16[32,3584]{1,0:T(8,128)(2,1)S(1)}, u32[]{:S(2)}, u32[]{:S(2)}) collective-permute-start(bf16[32,3584]{1,0:T(8,128)(2,1)S(1)} %collective-permute-done.36.refs_3_), channel_id=1, source_target_pairs={{0,96},{32,0},{64,32},{96,64},{1,97},{33,1},{65,33},{97,65},{2,98}... | collective-permute-start | bytes 688136 | tf_op jit(solution)/shard_map/ppermute | solution.py:57
  93.7 5.5 %shard_map.102.g_mine = f32[256,512]{1,0:T(8,128)S(1)} custom-call(s32[1]{0:T(128)} %bitcast.2.core_ref, bf16[32,3584]{1,0:T(8,128)(2,1)S(1)} %get-tuple-element.83.refs_0_, bf16[32,3584]{1,0:T(8,128)(2,1)S(1)} %collective-permute-done.34.refs_1_, bf16[32,3584]{1,0:T(8,128)(2,1)S(1)} %collective-permute-done.35.refs_2_, ...), custom_call_target="tpu_custom_call" | custom-call | tf_op jit(solution)/shard_map/pallas_call | solution.py:303
  103.6 7.2 %shard_map.103 = (bf16[32,3584]{1,0:T(8,128)(2,1)S(1)}, bf16[32,3584]{1,0:T(8,128)(2,1)S(1)}, bf16[32,3584]{1,0:T(8,128)(2,1)S(1)}, bf16[32,3584]{1,0:T(8,128)(2...) custom-call(s32[1]{0:T(128)} %bitcast.2.core_ref, ...), custom_call_target="tpu_custom_call" | custom-call | tf_op jit(solution)/shard_map/pallas_call | solution.py:303
  110.8 3.5 %collective-permute-start.43 = (bf16[32,3584]{1,0:T(8,128)(2,1)S(1)}, bf16[32,3584]{1,0:T(8,128)(2,1)S(1)}, u32[]{:S(2)}, u32[]{:S(2)}) collective-permute-start(bf16[32,3584]{1,0:T(8,128)(2,1)S(1)} %get-tuple-element.87), channel_id=1, source_target_pairs={{0,96},{32,0},{64,32},{96,64},{1,97},{33,1},{65,33},{97,65},{2,98}... | collective-permute-start | bytes 688136 | tf_op jit(solution)/shard_map/ppermute | solution.py:57
  115.7 5.4 %shard_map.98 = (bf16[32,3584]{1,0:T(8,128)(2,1)S(1)}, bf16[32,3584]{1,0:T(8,128)(2,1)S(1)}, bf16[32,3584]{1,0:T(8,128)(2,1)S(1)}, bf16[32,3584]{1,0:T(8,128)(2,...) custom-call(s32[1]{0:T(128)} %bitcast.2.core_ref, ...), custom_call_target="tpu_custom_call" | custom-call | tf_op jit(solution)/shard_map/pallas_call | solution.py:303
  127.6 7.7 %collective-permute-done.19 = bf16[32,3584]{1,0:T(8,128)(2,1)S(1)} collective-permute-done((bf16[32,3584]{1,0:T(8,128)(2,1)S(1)}, bf16[32,3584]{1,0:T(8,128)(2,1)S(1)}, u32[]{:S(2)}, u32[]{:S(2)}) %collective-permute-start.19) | collective-permute-done | bytes 229408 | tf_op jit(solution)/shard_map/ppermute | solution.py:57
  137.1 7.6 %collective-permute-done.24 = bf16[32,3584]{1,0:T(8,128)(2,1)S(1)} collective-permute-done((bf16[32,3584]{1,0:T(8,128)(2,1)S(1)}, bf16[32,3584]{1,0:T(8,128)(2,1)S(1)}, u32[]{:S(2)}, u32[]{:S(2)}) %collective-permute-start.24) | collective-permute-done | bytes 229408 | tf_op jit(solution)/shard_map/ppermute | solution.py:57
  145.1 5.6 %collective-permute-done.48.refs_3_ = bf16[32,3584]{1,0:T(8,128)(2,1)S(1)} collective-permute-done((bf16[32,3584]{1,0:T(8,128)(2,1)S(1)}, bf16[32,3584]{1,0:T(8,128)(2,1)S(1)}, u32[]{:S(2)}, u32[]{:S(2)}) %collective-permute-start.48) | collective-permute-done | bytes 229408 | tf_op jit(solution)/shard_map/ppermute | solution.py:57
  152.5 3.4 %collective-permute-start.50 = (bf16[4,3584]{1,0:T(4,128)(2,1)S(1)}, bf16[4,3584]{1,0:T(4,128)(2,1)S(1)}, u32[]{:S(2)}, u32[]{:S(2)}) collective-permute-start(bf16[4,3584]{1,0:T(4,128)(2,1)S(1)} %get-tuple-element.94), channel_id=1, source_target_pairs={{0,24},{1,25},{2,26},{3,27},{4,28},{5,29},{6,30},{7,31},{8,0},{9,1... | collective-permute-start | bytes 86024 | tf_op jit(solution)/shard_map/ppermute | solution.py:35
  156.6 4.4 %collective-permute-start.53 = (bf16[4,3584]{1,0:T(4,128)(2,1)S(1)}, bf16[4,3584]{1,0:T(4,128)(2,1)S(1)}, u32[]{:S(2)}, u32[]{:S(2)}) collective-permute-start(bf16[4,3584]{1,0:T(4,128)(2,1)S(1)} %get-tuple-element.97), channel_id=1, source_target_pairs={{0,22},{1,23},{2,20},{3,21},{4,18},{5,19},{6,16},{7,17},{8,30},{9,... | collective-permute-start | bytes 86024 | tf_op jit(solution)/shard_map/ppermute | solution.py:35
  168.7 4.2 %collective-permute-start.30 = (bf16[4,3584]{1,0:T(4,128)(2,1)S(1)}, bf16[4,3584]{1,0:T(4,128)(2,1)S(1)}, u32[]{:S(2)}, u32[]{:S(2)}) collective-permute-start(bf16[4,3584]{1,0:T(4,128)(2,1)S(1)} %get-tuple-element.77), channel_id=1, source_target_pairs={{0,22},{1,23},{2,20},{3,21},{4,18},{5,19},{6,16},{7,17},{8,30},{9,... | collective-permute-start | bytes 86024 | tf_op jit(solution)/shard_map/ppermute | solution.py:35
  174.6 8.5 %collective-permute-start.56 = (bf16[16,3584]{1,0:T(8,128)(2,1)S(1)}, bf16[16,3584]{1,0:T(8,128)(2,1)S(1)}, u32[]{:S(2)}, u32[]{:S(2)}) collective-permute-start(bf16[16,3584]{1,0:T(8,128)(2,1)S(1)} %get-tuple-element.101), channel_id=1, source_target_pairs={{0,1},{1,0},{2,3},{3,2},{4,5},{5,4},{6,7},{7,6},{8,9},{9,8},{10,11... | collective-permute-start | bytes 344072 | tf_op jit(solution)/shard_map/ppermute | solution.py:35
  183.5 6.8 %collective-permute-start.33 = (bf16[16,3584]{1,0:T(8,128)(2,1)S(1)}, bf16[16,3584]{1,0:T(8,128)(2,1)S(1)}, u32[]{:S(2)}, u32[]{:S(2)}) collective-permute-start(bf16[16,3584]{1,0:T(8,128)(2,1)S(1)} %get-tuple-element.81), channel_id=1, source_target_pairs={{0,1},{1,0},{2,3},{3,2},{4,5},{5,4},{6,7},{7,6},{8,9},{9,8},{10,11... | collective-permute-start | bytes 344072 | tf_op jit(solution)/shard_map/ppermute | solution.py:35
  (128 shorter events, 70.5 us)
Async XLA Ops:
  3.7 54.6 %collective-permute-start.15 = (bf16[3584,256]{1,0:T(8,128)(2,1)}, bf16[3584,256]{1,0:T(8,128)(2,1)S(1)}, u32[]{:S(2)}, u32[]{:S(2)}) collective-permute-start(bf16[3584,256]{1,0:T(8,128)(2,1)} %dynamic-slice_bitcast_fusion.2), channel_id=1, source_target_pairs={{0,1},{1,0},{2,3},{3,2},{4,5},{5,4},{6,7},{7,6},{8,9},{9,8},{10,11... | collective-permute-start | bytes 5505032 | tf_op jit(solution)/shard_map/ppermute | solution.py:35
  6.5 51.7 %collective-permute-start.16 = (bf16[3584,256]{1,0:T(8,128)(2,1)}, bf16[3584,256]{1,0:T(8,128)(2,1)S(1)}, u32[]{:S(2)}, u32[]{:S(2)}) collective-permute-start(bf16[3584,256]{1,0:T(8,128)(2,1)} %dynamic-slice_bitcast_fusion.1), channel_id=1, source_target_pairs={{0,1},{1,0},{2,3},{3,2},{4,5},{5,4},{6,7},{7,6},{8,9},{9,8},{10,11... | collective-permute-start | bytes 5505032 | tf_op jit(solution)/shard_map/ppermute | solution.py:35
  10.6 83.1 %collective-permute-start.18 = (bf16[256,3584]{1,0:T(8,128)(2,1)}, bf16[256,3584]{1,0:T(8,128)(2,1)S(1)}, u32[]{:S(2)}, u32[]{:S(2)}) collective-permute-start(bf16[256,3584]{1,0:T(8,128)(2,1)} %dynamic-slice_bitcast_fusion), channel_id=1, source_target_pairs={{0,1},{1,0},{2,3},{3,2},{4,5},{5,4},{6,7},{7,6},{8,9},{9,8},{10,11... | collective-permute-start | bytes 5505032 | tf_op jit(solution)/shard_map/ppermute | solution.py:35
  55.6 19.9 %collective-permute-start.35 = (bf16[32,3584]{1,0:T(8,128)(2,1)S(1)}, bf16[32,3584]{1,0:T(8,128)(2,1)S(1)}, u32[]{:S(2)}, u32[]{:S(2)}) collective-permute-start(bf16[32,3584]{1,0:T(8,128)(2,1)S(1)} %get-tuple-element.83.refs_0_), channel_id=1, source_target_pairs={{0,96},{32,0},{64,32},{96,64},{1,97},{33,1},{65,33},{97,65},{2,98}... | collective-permute-start | bytes 688136 | tf_op jit(solution)/shard_map/ppermute | solution.py:57
  66.2 37.4 %collective-permute-start.17 = (f32[256,1024]{1,0:T(8,128)S(1)}, f32[256,1024]{1,0:T(8,128)S(1)}, u32[]{:S(2)}, u32[]{:S(2)}) collective-permute-start(f32[256,1024]{1,0:T(8,128)S(1)} %shard_map.97.mine), channel_id=1, source_target_pairs={{0,1},{1,0},{2,3},{3,2},{4,5},{5,4},{6,7},{7,6},{8,9},{9,8},{10,11... | collective-permute-start | bytes 3145736 | tf_op jit(solution)/shard_map/ppermute | solution.py:35
  75.5 11.9 %collective-permute-start.36 = (bf16[32,3584]{1,0:T(8,128)(2,1)S(1)}, bf16[32,3584]{1,0:T(8,128)(2,1)S(1)}, u32[]{:S(2)}, u32[]{:S(2)}) collective-permute-start(bf16[32,3584]{1,0:T(8,128)(2,1)S(1)} %collective-permute-done.35.refs_2_), channel_id=1, source_target_pairs={{0,2},{1,3},{2,0},{3,1},{4,6},{5,7},{6,4},{7,5},{8,10},{9,11},{10,... | collective-permute-start | bytes 688136 | tf_op jit(solution)/shard_map/ppermute | solution.py:35
  110.8 13.1 %collective-permute-start.43 = (bf16[32,3584]{1,0:T(8,128)(2,1)S(1)}, bf16[32,3584]{1,0:T(8,128)(2,1)S(1)}, u32[]{:S(2)}, u32[]{:S(2)}) collective-permute-start(bf16[32,3584]{1,0:T(8,128)(2,1)S(1)} %get-tuple-element.87), channel_id=1, source_target_pairs={{0,96},{32,0},{64,32},{96,64},{1,97},{33,1},{65,33},{97,65},{2,98}... | collective-permute-start | bytes 688136 | tf_op jit(solution)/shard_map/ppermute | solution.py:57
  114.3 9.6 %collective-permute-start.44 = (bf16[32,3584]{1,0:T(8,128)(2,1)S(1)}, bf16[32,3584]{1,0:T(8,128)(2,1)S(1)}, u32[]{:S(2)}, u32[]{:S(2)}) collective-permute-start(bf16[32,3584]{1,0:T(8,128)(2,1)S(1)} %get-tuple-element.88), channel_id=1, source_target_pairs={{0,2},{1,3},{2,0},{3,1},{4,6},{5,7},{6,4},{7,5},{8,10},{9,11},{10,... | collective-permute-start | bytes 688136 | tf_op jit(solution)/shard_map/ppermute | solution.py:35
  114.6 9.5 %collective-permute-start.46 = (bf16[32,3584]{1,0:T(8,128)(2,1)S(1)}, bf16[32,3584]{1,0:T(8,128)(2,1)S(1)}, u32[]{:S(2)}, u32[]{:S(2)}) collective-permute-start(bf16[32,3584]{1,0:T(8,128)(2,1)S(1)} %get-tuple-element.91), channel_id=1, source_target_pairs={{0,32},{32,64},{64,96},{96,0},{1,33},{33,65},{65,97},{97,1},{2,34}... | collective-permute-start | bytes 688136 | tf_op jit(solution)/shard_map/ppermute | solution.py:57
  114.6 30.2 %collective-permute-start.42 = (bf16[32,3584]{1,0:T(8,128)(2,1)S(1)}, bf16[32,3584]{1,0:T(8,128)(2,1)S(1)}, u32[]{:S(2)}, u32[]{:S(2)}) collective-permute-start(bf16[32,3584]{1,0:T(8,128)(2,1)S(1)} %get-tuple-element.85), channel_id=1, source_target_pairs={{0,2},{1,3},{2,0},{3,1},{4,6},{5,7},{6,4},{7,5},{8,10},{9,11},{10,... | collective-permute-start | bytes 688136 | tf_op jit(solution)/shard_map/ppermute | solution.py:35
  123.9 12.0 %collective-permute-start.22 = (bf16[32,3584]{1,0:T(8,128)(2,1)S(1)}, bf16[32,3584]{1,0:T(8,128)(2,1)S(1)}, u32[]{:S(2)}, u32[]{:S(2)}) collective-permute-start(bf16[32,3584]{1,0:T(8,128)(2,1)S(1)} %get-tuple-element.69), channel_id=1, source_target_pairs={{0,32},{32,64},{64,96},{96,0},{1,33},{33,65},{65,97},{97,1},{2,34}... | collective-permute-start | bytes 688136 | tf_op jit(solution)/shard_map/ppermute | solution.py:57
  123.9 11.4 %collective-permute-start.19 = (bf16[32,3584]{1,0:T(8,128)(2,1)S(1)}, bf16[32,3584]{1,0:T(8,128)(2,1)S(1)}, u32[]{:S(2)}, u32[]{:S(2)}) collective-permute-start(bf16[32,3584]{1,0:T(8,128)(2,1)S(1)} %get-tuple-element.66), channel_id=1, source_target_pairs={{0,32},{32,64},{64,96},{96,0},{1,33},{33,65},{65,97},{97,1},{2,34}... | collective-permute-start | bytes 688136 | tf_op jit(solution)/shard_map/ppermute | solution.py:57
  124.1 31.8 %collective-permute-start.21 = (bf16[32,3584]{1,0:T(8,128)(2,1)S(1)}, bf16[32,3584]{1,0:T(8,128)(2,1)S(1)}, u32[]{:S(2)}, u32[]{:S(2)}) collective-permute-start(bf16[32,3584]{1,0:T(8,128)(2,1)S(1)} %get-tuple-element.67), channel_id=1, source_target_pairs={{0,96},{32,0},{64,32},{96,64},{1,97},{33,1},{65,33},{97,65},{2,98}... | collective-permute-start | bytes 688136 | tf_op jit(solution)/shard_map/ppermute | solution.py:57
  135.3 9.8 %collective-permute-start.45 = (bf16[32,3584]{1,0:T(8,128)(2,1)S(1)}, bf16[32,3584]{1,0:T(8,128)(2,1)S(1)}, u32[]{:S(2)}, u32[]{:S(2)}) collective-permute-start(bf16[32,3584]{1,0:T(8,128)(2,1)S(1)} %add_convert_fusion.2), channel_id=1, source_target_pairs={{0,96},{32,0},{64,32},{96,64},{1,97},{33,1},{65,33},{97,65},{2,98}... | collective-permute-start | bytes 688136 | tf_op jit(solution)/shard_map/ppermute | solution.py:57
  135.9 19.9 %collective-permute-start.20 = (bf16[32,3584]{1,0:T(8,128)(2,1)S(1)}, bf16[32,3584]{1,0:T(8,128)(2,1)S(1)}, u32[]{:S(2)}, u32[]{:S(2)}) collective-permute-start(bf16[32,3584]{1,0:T(8,128)(2,1)S(1)} %add_convert_fusion.5), channel_id=1, source_target_pairs={{0,32},{32,64},{64,96},{96,0},{1,33},{33,65},{65,97},{97,1},{2,34}... | collective-permute-start | bytes 688136 | tf_op jit(solution)/shard_map/ppermute | solution.py:57
  144.7 11.9 %collective-permute-start.25 = (bf16[32,3584]{1,0:T(8,128)(2,1)S(1)}, bf16[32,3584]{1,0:T(8,128)(2,1)S(1)}, u32[]{:S(2)}, u32[]{:S(2)}) collective-permute-start(bf16[32,3584]{1,0:T(8,128)(2,1)S(1)} %add_convert_fusion.3), channel_id=1, source_target_pairs={{0,2},{1,3},{2,0},{3,1},{4,6},{5,7},{6,4},{7,5},{8,10},{9,11},{10,... | collective-permute-start | bytes 688136 | tf_op jit(solution)/shard_map/ppermute | solution.py:35
  150.9 10.2 %collective-permute-start.49 = (bf16[4,3584]{1,0:T(4,128)(2,1)S(1)}, bf16[4,3584]{1,0:T(4,128)(2,1)S(1)}, u32[]{:S(2)}, u32[]{:S(2)}) collective-permute-start(bf16[4,3584]{1,0:T(4,128)(2,1)S(1)} %get-tuple-element.93), channel_id=1, source_target_pairs={{0,6},{1,7},{2,4},{3,5},{4,2},{5,3},{6,0},{7,1},{8,14},{9,15},{10,... | collective-permute-start | bytes 86024 | tf_op jit(solution)/shard_map/ppermute | solution.py:35
  152.5 10.2 %collective-permute-start.50 = (bf16[4,3584]{1,0:T(4,128)(2,1)S(1)}, bf16[4,3584]{1,0:T(4,128)(2,1)S(1)}, u32[]{:S(2)}, u32[]{:S(2)}) collective-permute-start(bf16[4,3584]{1,0:T(4,128)(2,1)S(1)} %get-tuple-element.94), channel_id=1, source_target_pairs={{0,24},{1,25},{2,26},{3,27},{4,28},{5,29},{6,30},{7,31},{8,0},{9,1... | collective-permute-start | bytes 86024 | tf_op jit(solution)/shard_map/ppermute | solution.py:35
  156.6 11.1 %collective-permute-start.53 = (bf16[4,3584]{1,0:T(4,128)(2,1)S(1)}, bf16[4,3584]{1,0:T(4,128)(2,1)S(1)}, u32[]{:S(2)}, u32[]{:S(2)}) collective-permute-start(bf16[4,3584]{1,0:T(4,128)(2,1)S(1)} %get-tuple-element.97), channel_id=1, source_target_pairs={{0,22},{1,23},{2,20},{3,21},{4,18},{5,19},{6,16},{7,17},{8,30},{9,... | collective-permute-start | bytes 86024 | tf_op jit(solution)/shard_map/ppermute | solution.py:35
  162.6 10.2 %collective-permute-start.26 = (bf16[4,3584]{1,0:T(4,128)(2,1)S(1)}, bf16[4,3584]{1,0:T(4,128)(2,1)S(1)}, u32[]{:S(2)}, u32[]{:S(2)}) collective-permute-start(bf16[4,3584]{1,0:T(4,128)(2,1)S(1)} %get-tuple-element.73), channel_id=1, source_target_pairs={{0,6},{1,7},{2,4},{3,5},{4,2},{5,3},{6,0},{7,1},{8,14},{9,15},{10,... | collective-permute-start | bytes 86024 | tf_op jit(solution)/shard_map/ppermute | solution.py:35
  168.2 14.9 %collective-permute-start.29 = (bf16[4,3584]{1,0:T(4,128)(2,1)S(1)}, bf16[4,3584]{1,0:T(4,128)(2,1)S(1)}, u32[]{:S(2)}, u32[]{:S(2)}) collective-permute-start(bf16[4,3584]{1,0:T(4,128)(2,1)S(1)} %get-tuple-element.76), channel_id=1, source_target_pairs={{0,16},{1,17},{2,18},{3,19},{4,20},{5,21},{6,22},{7,23},{8,24},{9,... | collective-permute-start | bytes 86024 | tf_op jit(solution)/shard_map/ppermute | solution.py:35
  168.7 14.4 %collective-permute-start.30 = (bf16[4,3584]{1,0:T(4,128)(2,1)S(1)}, bf16[4,3584]{1,0:T(4,128)(2,1)S(1)}, u32[]{:S(2)}, u32[]{:S(2)}) collective-permute-start(bf16[4,3584]{1,0:T(4,128)(2,1)S(1)} %get-tuple-element.77), channel_id=1, source_target_pairs={{0,22},{1,23},{2,20},{3,21},{4,18},{5,19},{6,16},{7,17},{8,30},{9,... | collective-permute-start | bytes 86024 | tf_op jit(solution)/shard_map/ppermute | solution.py:35
  172.9 10.2 %collective-permute-start.31 = (bf16[4,3584]{1,0:T(4,128)(2,1)S(1)}, bf16[4,3584]{1,0:T(4,128)(2,1)S(1)}, u32[]{:S(2)}, u32[]{:S(2)}) collective-permute-start(bf16[4,3584]{1,0:T(4,128)(2,1)S(1)} %get-tuple-element.78), channel_id=1, source_target_pairs={{0,8},{1,9},{2,10},{3,11},{4,12},{5,13},{6,14},{7,15},{8,16},{9,17... | collective-permute-start | bytes 86024 | tf_op jit(solution)/shard_map/ppermute | solution.py:35
  174.6 15.7 %collective-permute-start.56 = (bf16[16,3584]{1,0:T(8,128)(2,1)S(1)}, bf16[16,3584]{1,0:T(8,128)(2,1)S(1)}, u32[]{:S(2)}, u32[]{:S(2)}) collective-permute-start(bf16[16,3584]{1,0:T(8,128)(2,1)S(1)} %get-tuple-element.101), channel_id=1, source_target_pairs={{0,1},{1,0},{2,3},{3,2},{4,5},{5,4},{6,7},{7,6},{8,9},{9,8},{10,11... | collective-permute-start | bytes 344072 | tf_op jit(solution)/shard_map/ppermute | solution.py:35
  (41 other events, 253.3 us)

commit v2 on v0

v2 whole, which is shorter than its diff:
```python
import functools

import jax
import jax.numpy as jnp
from jax import lax
from jax.experimental import pallas as pl
from jax.experimental.pallas import tpu as pltpu
from jax.sharding import PartitionSpec as P

BF = jnp.bfloat16
F32 = jnp.float32
VMEM = pl.BlockSpec(memory_space=pltpu.VMEM)
HBM = pl.BlockSpec(memory_space=pltpu.HBM)
LIMIT = 16 * 1024 * 1024
NZ = 4


def dot(a, b, dims):
    return lax.dot_general(a, b, (dims, ((), ())), preferred_element_type=F32)


def place_of(index):
    return index // 8, (index // 4) % 2, (index // 2) % 2, index % 2


def index_of(z, h, l, c):
    return ((z * 2 + h) * 2 + l) * 2 + c


def over_expert(value, move):
    pairs = []
    for at in range(32):
        pairs.append((at, index_of(*move(*place_of(at)))))
    return lax.ppermute(value, "expert", pairs)


def other_core(value):
    return over_expert(value, lambda z, h, l, c: (z, h, l, 1 - c))


def other_l(value):
    return over_expert(value, lambda z, h, l, c: (z, h, 1 - l, c))


def other_y(value):
    return over_expert(value, lambda z, h, l, c: (z, 1 - h, 1 - l, c))


def other_y_core(value):
    return over_expert(value, lambda z, h, l, c: (z, 1 - h, 1 - l, 1 - c))


def along_z(value, step):
    return over_expert(value, lambda z, h, l, c: ((z + step) % NZ, h, l, c))


def along_x(value, step):
    pairs = []
    for x in range(4):
        for at in range(32):
            to = (x + step) % 4 if at % 2 == 0 else (x - step) % 4
            pairs.append((x * 32 + at, to * 32 + at))
    return lax.ppermute(value, ("dp", "expert"), pairs)


def selection(ids, rows, expert, place):
    tok = ids.shape[1]
    up = (lax.broadcasted_iota(jnp.int32, (tok, tok), 0) < lax.broadcasted_iota(jnp.int32, (tok, tok), 1))
    up = jnp.where(up, 1.0, 0.0).astype(BF)
    first = jnp.where(jnp.broadcast_to(ids[0:1, :], (rows, tok)) == expert, 1.0, 0.0)
    second = jnp.where(jnp.broadcast_to(ids[1:2, :], (rows, tok)) == expert, 1.0, 0.0)
    before_first = dot(first.astype(BF), up, ((1,), (0,)))
    before_second = dot(second.astype(BF), up, ((1,), (0,))) + jnp.sum(first, axis=1, keepdims=True)
    want = place.astype(F32)
    sel_first = jnp.where(before_first == want, first, 0.0)
    sel_second = jnp.where(before_second == want, second, 0.0)
    return sel_first, sel_second


def slot_expert(k, r, z, h):
    return ((z + k) & 3) * 2 + ((h + r) & 1)


def dispatch_kernel(half, ids_ref, gates_ref, tok_hbm, grad_hbm, near_own, far_own, near_other, far_other, tok_v, grad_v, sems):
    at = lax.axis_index("expert")
    core = at & 1
    h = (at >> 2) & 1
    z = at >> 3
    copies = []
    for n, which in enumerate((1 - core, core)):
        cols = pl.ds(pl.multiple_of(which * half, 128), half)
        one = pltpu.make_async_copy(tok_hbm.at[:, cols], tok_v.at[n], sems.at[n, 0])
        two = pltpu.make_async_copy(grad_hbm.at[:, cols], grad_v.at[n], sems.at[n, 1])
        one.start()
        two.start()
        copies.append((one, two))
    rows, tok = 32, ids_ref.shape[1]
    s = lax.broadcasted_iota(jnp.int32, (rows, tok), 0)
    sel_first, sel_second = selection(ids_ref[...], rows, slot_expert((s >> 1) & 3, s >> 4, z, h), s & 1)
    is_grad = ((s >> 3) & 1) == 1
    member = sel_first + sel_second
    gate = jnp.sum(
        sel_first * jnp.broadcast_to(gates_ref[0:1, :], (rows, tok))
        + sel_second * jnp.broadcast_to(gates_ref[1:2, :], (rows, tok)),
        axis=1,
        keepdims=True,
    )
    of_tok = jnp.where(is_grad, 0.0, member).astype(BF)
    of_grad = jnp.where(is_grad, member, 0.0).astype(BF)
    for n, (near, far) in enumerate(((near_other, far_other), (near_own, far_own))):
        copies[n][0].wait()
        copies[n][1].wait()
        got = dot(of_tok, tok_v[n], ((1,), (0,))) + dot(of_grad, grad_v[n], ((1,), (0,))) * gate
        got = got.astype(BF)
        near[...] = got[0:16, :]
        far[...] = got[16:32, :]


def merge_kernel(near_own, near_got, far_own, far_got, *outs):
    core = lax.axis_index("expert") & 1
    full = jnp.concatenate([near_own[...], near_got[...], far_own[...], far_got[...]], axis=0)
    s = lax.broadcasted_iota(jnp.int32, (64, 64), 0)
    t = lax.broadcasted_iota(jnp.int32, (64, 64), 1)
    k, kind, r, c, j = s >> 4, (s >> 3) & 1, (s >> 2) & 1, (s >> 1) & 1, s & 1
    source = r * 32 + ((c + core) & 1) * 16 + kind * 8 + k * 2 + j
    both = dot(jnp.where(t == source, 1.0, 0.0).astype(BF), full, ((1,), (0,))).astype(BF)
    for n, out in enumerate(outs):
        out[...] = both[16 * n : 16 * n + 16, :]


def assemble_kernel(*refs):
    msgs, out = refs[:4], refs[4]
    wide = [m[...].astype(F32) for m in msgs]
    out[...] = jnp.concatenate([m[0:8] for m in wide] + [m[8:16] for m in wide], axis=0).astype(BF)


def weights_kernel(half, flip, wg_ref, wu_ref, wd_ref, out_ref, sems):
    core = lax.axis_index("expert") & 1
    at = (1 - core if flip else core) * half
    rows = pl.ds(pl.multiple_of(at, 256), half)
    copies = [
        pltpu.make_async_copy(wg_ref.at[0, rows, :], out_ref.at[pl.ds(0, half), :], sems.at[0]),
        pltpu.make_async_copy(wu_ref.at[0, rows, :], out_ref.at[pl.ds(half, half), :], sems.at[1]),
    ]
    for n in range(half // 256):
        cols = pl.ds(pl.multiple_of(at + 256 * n, 256), 256)
        into = out_ref.at[pl.ds(2 * half + 256 * n, 256), :]
        copies.append(pltpu.make_async_copy(wd_ref.at[0, :, cols], into, sems.at[2 + n]))
    for copy in copies:
        copy.start()
    for copy in copies:
        copy.wait()


def first_kernel(half, c0, c1, c2, c3, own, got, out, rows, grads):
    for n, chunk in enumerate((c0, c1, c2, c3)):
        rows[pl.ds(32 * n, 32), :] = chunk[0:32, :]
        grads[pl.ds(32 * n, 32), :] = chunk[32:64, :]
    for m, w in enumerate((own, got)):
        at = 256 * m
        out[:, at : at + 256] = dot(rows[...], w[0:half, :], ((1,), (0,)))
        out[:, 512 + at : 768 + at] = dot(rows[...], w[half : 2 * half, :], ((1,), (0,)))
        last = dot(grads[:, 0:256], w[2 * half : 2 * half + 256, :], ((1,), (1,)))
        for n in range(1, half // 256):
            block = w[2 * half + 256 * n : 2 * half + 256 * n + 256, :]
            last += dot(grads[:, 256 * n : 256 * n + 256], block, ((1,), (1,)))
        out[:, 1024 + at : 1280 + at] = last


EARLY = [(0, 0), (3, 0), (1, 0), (0, 1)]
LATE = [(1, 1), (3, 1), (2, 0), (2, 1)]
SENT = [(2, 1), (2, 0), (3, 1), (1, 0)]
KEPT = [(1, 1), (3, 0), (0, 1), (0, 0)]


def second_kernel(half, chunks, *refs):
    parts, (own, got) = refs[:4], refs[4:6]
    outs, (hid_ref, ga_ref, gb_ref) = refs[6:10], refs[10:]
    for n, (a_at, b_at) in enumerate(chunks):
        late = (a_at, b_at) in LATE
        mine, theirs = parts[1 if late else 0], parts[3 if late else 2]
        group = LATE if late else EARLY
        here = pl.ds(32 * group.index((a_at, b_at)), 32)
        there = pl.ds(32 * group.index(((-a_at) % 4, b_at)), 32)

        def both(base):
            return jnp.concatenate(
                [
                    mine[here, base : base + 256] + theirs[there, base + 256 : base + 512],
                    mine[here, base + 256 : base + 512] + theirs[there, base : base + 256],
                ],
                axis=1,
            )

        a, b, gh = both(0), both(512), both(1024)
        sg = jax.nn.sigmoid(a)
        at = pl.ds(32 * n, 32)
        hid_ref[at, :] = (a * sg * b).astype(BF)
        ga_ref[at, :] = (gh * b * sg * (1.0 + a * (1.0 - sg))).astype(BF)
        gb_ref[at, :] = (gh * a * sg).astype(BF)

    for n in range(half // 256):
        at = 256 * n
        res, gres = None, None
        for m, w in enumerate((own, got)):
            cols = slice(256 * m, 256 * m + 256)
            one = dot(hid_ref[:, cols], w[2 * half + at : 2 * half + at + 256, :], ((1,), (0,)))
            two = dot(ga_ref[:, cols], w[at : at + 256, :], ((1,), (1,)))
            two += dot(gb_ref[:, cols], w[half + at : half + at + 256, :], ((1,), (1,)))
            res = one if res is None else res + one
            gres = two if gres is None else gres + two
        res, gres = res.astype(BF), gres.astype(BF)
        for k, out in enumerate(outs):
            out[0:32, at : at + 256] = res[32 * k : 32 * k + 32, :]
            out[32:64, at : at + 256] = gres[32 * k : 32 * k + 32, :]


def finish_kernel(*refs):
    terms, outs = refs[:4], refs[4:]
    total = terms[0][...].astype(F32)
    for ref in terms[1:]:
        total += ref[...].astype(F32)
    for k, out in enumerate(outs):
        out[...] = jnp.concatenate([total[8 * k : 8 * k + 8], total[32 + 8 * k : 40 + 8 * k]], axis=0).astype(BF)


def cores_kernel(*refs):
    msgs, outs = refs[:4], refs[4:]
    core = lax.axis_index("expert") & 1
    full = jnp.concatenate([m[...] for m in msgs], axis=0)
    s = lax.broadcasted_iota(jnp.int32, (64, 64), 0)
    t = lax.broadcasted_iota(jnp.int32, (64, 64), 1)
    r, c, kind, k, j = s >> 5, (s >> 4) & 1, (s >> 3) & 1, (s >> 1) & 3, s & 1
    source = k * 16 + kind * 8 + r * 4 + ((c + core) & 1) * 2 + j
    both = dot(jnp.where(t == source, 1.0, 0.0).astype(BF), full, ((1,), (0,))).astype(BF)
    for n, out in enumerate(outs):
        out[...] = both[16 * n : 16 * n + 16, :]


def tail_kernel(half, ids_ref, gates_ref, tok_ref, grad_ref, near_own, near_got, far_own, far_got, mixed_ref, gt_ref, gg_ref):
    at = lax.axis_index("expert")
    core = at & 1
    rows, tok = 16, ids_ref.shape[1]
    s = lax.broadcasted_iota(jnp.int32, (rows, tok), 0)
    expert = slot_expert((s >> 1) & 3, s >> 3, at >> 3, (at >> 2) & 1)
    sel_first, sel_second = selection(ids_ref[...], rows, expert, s & 1)
    member = (sel_first + sel_second).astype(BF)
    gate = jnp.sum(
        sel_first * jnp.broadcast_to(gates_ref[0:1, :], (rows, tok))
        + sel_second * jnp.broadcast_to(gates_ref[1:2, :], (rows, tok)),
        axis=1,
        keepdims=True,
    )
    inner = jnp.zeros((16, 1), F32)
    for which, near, far in ((core, near_own, far_own), (1 - core, near_got, far_got)):
        cols = pl.ds(pl.multiple_of(which * half, 128), half)
        one, two = near[...].astype(F32), far[...].astype(F32)
        out_rows = jnp.concatenate([one[0:8], two[0:8]], axis=0)
        grad_rows = jnp.concatenate([one[8:16], two[8:16]], axis=0).astype(BF)
        grad = grad_ref[:, cols]
        inner += jnp.sum(dot(member, grad, ((1,), (0,))) * out_rows, axis=1, keepdims=True)
        scaled = out_rows * gate
        high = scaled.astype(BF)
        low = (scaled - high.astype(F32)).astype(BF)
        add = dot(member, high, ((0,), (0,))) + dot(member, low, ((0,), (0,)))
        mixed_ref[:, cols] = (tok_ref[:, cols].astype(F32) + add).astype(BF)
        gt_ref[:, cols] = (grad.astype(F32) + dot(member, grad_rows, ((0,), (0,)))).astype(BF)
    gg_ref[0:1, :] = jnp.sum(sel_first * inner, axis=0, keepdims=True)
    gg_ref[1:2, :] = jnp.sum(sel_second * inner, axis=0, keepdims=True)


def params():
    return pltpu.CompilerParams(vmem_limit_bytes=LIMIT)


def shape(rows, cols, dtype=BF):
    return jax.ShapeDtypeStruct((rows, cols), dtype)


def whole(kernel, outs, args, scratch=(), specs=None):
    return pl.pallas_call(
        kernel,
        out_shape=outs,
        in_specs=specs or [VMEM] * len(args),
        out_specs=jax.tree.map(lambda _: VMEM, outs),
        scratch_shapes=list(scratch),
        compiler_params=params(),
    )(*args)


def weights(half, flip, w_gate, w_up, w_down):
    return whole(
        functools.partial(weights_kernel, half, flip),
        shape(3 * half, w_gate.shape[2]),
        (w_gate, w_up, w_down),
        [pltpu.SemaphoreType.DMA((2 + half // 256,))],
        [HBM] * 3,
    )


def shards(tokens, expert_ids, gates, grad_mixed, w_gate, w_up, w_down):
    tok, width = tokens.shape
    half = width // 2
    ids_t = expert_ids.T
    gates_t = gates.T

    near_own, far_own, near_other, far_other = whole(
        functools.partial(dispatch_kernel, half),
        [shape(16, half)] * 4,
        (ids_t, gates_t, tokens, grad_mixed),
        [pltpu.VMEM((2, tok, half), BF), pltpu.VMEM((2, tok, half), BF), pltpu.SemaphoreType.DMA((2, 2))],
        [VMEM, VMEM, HBM, HBM],
    )
    near_got = other_core(near_other)
    far_got = [other_y(far_own), other_y_core(far_other)]
    near_got, wg_src, wu_src, wd_src = lax.optimization_barrier((near_got, w_gate, w_up, w_down))
    w_got = other_core(weights(half, True, wg_src, wu_src, wd_src))
    msgs = whole(merge_kernel, [shape(16, half)] * 4, (near_own, near_got, *far_got))
    across = along_z(msgs[2], 2)
    msgs = [msgs[0], along_z(msgs[1], 1), across, along_z(msgs[3], 3)]
    t = {(0, 0): whole(assemble_kernel, shape(64, half), msgs)}

    t[0, 1] = other_l(t[0, 0])
    t[3, 0] = along_x(t[0, 0], 1)
    t[1, 0] = along_x(t[0, 0], -1)
    w_got, wg_src, wu_src, wd_src = lax.optimization_barrier((w_got, wg_src, wu_src, wd_src))
    w_own = weights(half, False, wg_src, wu_src, wd_src)
    t[0, 1], t[3, 0], t[1, 0] = lax.optimization_barrier((t[0, 1], t[3, 0], t[1, 0]))
    t[1, 1] = along_x(t[0, 1], -1)
    t[3, 1] = other_l(t[3, 0])
    t[2, 0] = along_x(t[3, 0], 1)
    t[2, 1] = along_x(t[1, 1], -1)

    fdev = w_gate.shape[2]
    parts = []
    for group in (EARLY, LATE):
        parts.append(
            whole(
                functools.partial(first_kernel, half),
                shape(128, 6 * fdev, F32),
                [t[o] for o in group] + [w_own, w_got],
                [pltpu.VMEM((128, half), BF)] * 2,
            )
        )
    parts += [other_core(part) for part in parts]
    q = {}
    for group in (SENT, KEPT):
        res = whole(
            functools.partial(second_kernel, half, group),
            [shape(64, half)] * 4,
            parts + [w_own, w_got],
            [pltpu.VMEM((128, 2 * fdev), BF)] * 3,
        )
        q.update(zip(group, res))

    def add(*terms):
        total = terms[0].astype(F32)
        for term in terms[1:]:
            total = total + term.astype(F32)
        return total.astype(BF)

    f21 = along_x(q[2, 1], 1)
    f20 = along_x(q[2, 0], -1)
    f31 = other_l(q[3, 1])
    q[1, 0], f21 = lax.optimization_barrier((q[1, 0], f21))
    f10 = along_x(q[1, 0], 1)
    f11 = along_x(add(q[1, 1], f21), 1)
    f30 = along_x(add(q[3, 0], f20, f31), -1)
    f01 = other_l(add(q[0, 1], f11))
    back = whole(finish_kernel, [shape(16, half)] * 4, (q[0, 0], f10, f30, f01))
    across = along_z(back[2], -2)
    back = [back[0], along_z(back[1], -1), across, along_z(back[3], -3)]
    near_mine, near_theirs, far_mine, far_theirs = whole(cores_kernel, [shape(16, half)] * 4, back)
    mixed, grad_tokens, grad_gates = whole(
        functools.partial(tail_kernel, half),
        [shape(tok, width), shape(tok, width), shape(2, tok, F32)],
        (ids_t, gates_t, tokens, grad_mixed, near_mine, other_core(near_theirs), other_y(far_mine), other_y_core(far_theirs)),
    )
    return mixed, grad_tokens, grad_gates.T


def solution(mesh):
    return jax.shard_map(
        shards,
        mesh=mesh,
        in_specs=(
            P(("dp", "expert"), None),
            P(("dp", "expert"), None),
            P(("dp", "expert"), None),
            P(("dp", "expert"), None),
            P("expert", None, "dp"),
            P("expert", None, "dp"),
            P("expert", "dp", None),
        ),
        out_specs=(P(("dp", "expert"), None), P(("dp", "expert"), None), P(("dp", "expert"), None)),
        check_vma=False,
    )
```

time: 255 us -> 138 us (0.54)
  waiting for transfers between devices: 116 us -> 63.2 us
  blocking collectives: 44.9 us -> 0 us
  matrix products: 32 us -> 0 us
  starting transfers between devices: 15.7 us -> 47.5 us
  local copies, waits for them, and re-layouts: 27.3 us -> 8.61 us
  Pallas kernels: 0 us -> 17.6 us
  between operations: 13.9 us -> 0.81 us
  other arithmetic: 4.48 us -> 0.38 us
    ppermute x0 -> x29, waiting for transfers between devices: none -> 63.2 us  [the longest x10 36.3 us: along_x(): return lax.ppermute(value, ('dp', 'expert'), pairs)]
    reduce_scatter x2 -> x0, waiting for transfers between devices: 61.1 us -> none  [the longest x1 33.8 us: shards(): lax.psum_scatter(lax.dot_general(part, w_both, (((1,), (1,)), ((), ())),...]
    ppermute x0 -> x29, starting transfers between devices: none -> 47.5 us  [the longest x19 32.6 us: over_expert(): return lax.ppermute(value, 'expert', pairs)]
    all_gather x2 -> x0, waiting for transfers between devices: 47.5 us -> none  [the longest x1 27.2 us: shards(): lax.all_gather(grad_arrived[None], 'dp', axis=0, tiled=True)]
    all_to_all x2 -> x0, blocking collectives: 44.9 us -> none  [the longest x1 25.3 us: shards(): lax.all_to_all(copies, 'expert', split_axis=0, concat_axis=0, tiled=True)]
    dot_general x9 -> x0, matrix products: 32 us -> none  [the longest x1 6.96 us: shards(): jnp.dot(lax.all_gather(arrived[None], 'dp', axis=0, tiled=True).reshape(-...]
    reshape x6 -> x0, local copies, waits for them, and re-layouts: 23.5 us -> none  [the longest x1 8.39 us: shards(): lax.all_gather(arrived[None], 'dp', axis=0, tiled=True).reshape(-1, width)]
    pallas_call x0 -> x12, Pallas kernels: none -> 17.6 us  [whole(): pl.pallas_call(kernel, out_shape=outs, in_specs=specs or [VMEM] * len(arg...]
  transfers between devices with their start and end apart: 6 -> 29, of which waited for: 5 -> 18; matrix products, arithmetic and copies ran while one was open for 20% -> 0% of each run, Pallas kernels for 0% -> 6%
where the time goes in v2:
time: 138 us
  waiting for transfers between devices  63.2 us (46%)
  starting transfers between devices  47.5 us (34%)
  Pallas kernels  17.6 us (13%)
  local copies, waits for them, and re-layouts  8.61 us (6%)
    ppermute x10, waiting for transfers between devices, along_x(): return lax.ppermute(value, ('dp', 'expert'), pairs)  36.3 us
    ppermute x19, starting transfers between devices, over_expert(): return lax.ppermute(value, 'expert', pairs)  32.6 us
    ppermute x19, waiting for transfers between devices, over_expert(): return lax.ppermute(value, 'expert', pairs)  27 us
    pallas_call x12, Pallas kernels, whole(): pl.pallas_call(kernel, out_shape=outs, in_specs=specs or [VMEM] * len(arg...  17.6 us
    ppermute x10, starting transfers between devices, along_x(): return lax.ppermute(value, ('dp', 'expert'), pairs)  14.9 us
    unnamed x24, local copies, waits for them, and re-layouts  8.61 us
  transfers between devices with their start and end apart: 29, of which 18 were waited for; matrix products, arithmetic and copies ran while one was open for 0% of the time, Pallas kernels for 6%

profile of v2, /device:TPU:1, one launch (start us, length us, event | category | flops | bytes accessed | tf_op | source)
XLA Modules:
  0.0 138.1 jit_solution(233266565738240120)
XLA Ops:
  14.1 2.8 %collective-permute-start.1 = (bf16[16,3584]{1,0:T(8,128)(2,1)S(1)}, bf16[16,3584]{1,0:T(8,128)(2,1)S(1)}, u32[]{:S(2)}, u32[]{:S(2)}) collective-permute-start(bf16[16,3584]{1,0:T(8,128)(2,1)S(1)} %get-tuple-element.46), channel_id=1, source_target_pairs={{0,6},{1,7},{2,4},{3,5},{4,2},{5,3},{6,0},{7,1},{8,14},{9,15},{10,... | collective-permute-start | bytes 344072 | tf_op jit(solution)/shard_map/ppermute | solution.py:34
  17.1 3.1 %collective-permute-done.1.far_own = bf16[16,3584]{1,0:T(8,128)(2,1)S(1)} collective-permute-done((bf16[16,3584]{1,0:T(8,128)(2,1)S(1)}, bf16[16,3584]{1,0:T(8,128)(2,1)S(1)}, u32[]{:S(2)}, u32[]{:S(2)}) %collective-permute-start.1) | collective-permute-done | bytes 114720 | tf_op jit(solution)/shard_map/ppermute | solution.py:34
  20.2 3.2 %collective-permute-done.2.far_got = bf16[16,3584]{1,0:T(8,128)(2,1)S(1)} collective-permute-done((bf16[16,3584]{1,0:T(8,128)(2,1)S(1)}, bf16[16,3584]{1,0:T(8,128)(2,1)S(1)}, u32[]{:S(2)}, u32[]{:S(2)}) %collective-permute-start.2) | collective-permute-done | bytes 114720 | tf_op jit(solution)/shard_map/ppermute | solution.py:34
  25.4 3.3 %collective-permute-start.4 = (bf16[16,3584]{1,0:T(8,128)(2,1)S(1)}, bf16[16,3584]{1,0:T(8,128)(2,1)S(1)}, u32[]{:S(2)}, u32[]{:S(2)}) collective-permute-start(bf16[16,3584]{1,0:T(8,128)(2,1)S(1)} %get-tuple-element.50), channel_id=1, source_target_pairs={{0,16},{1,17},{2,18},{3,19},{4,20},{5,21},{6,22},{7,23},{8,24},{9,... | collective-permute-start | bytes 344072 | tf_op jit(solution)/shard_map/ppermute | solution.py:34
  30.7 3.3 %collective-permute-done.4.refs_2_ = bf16[16,3584]{1,0:T(8,128)(2,1)S(1)} collective-permute-done((bf16[16,3584]{1,0:T(8,128)(2,1)S(1)}, bf16[16,3584]{1,0:T(8,128)(2,1)S(1)}, u32[]{:S(2)}, u32[]{:S(2)}) %collective-permute-start.4) | collective-permute-done | bytes 114720 | tf_op jit(solution)/shard_map/ppermute | solution.py:34
  36.8 6.5 %collective-permute-done.8.c2 = bf16[64,3584]{1,0:T(8,128)(2,1)S(1)} collective-permute-done((bf16[64,3584]{1,0:T(8,128)(2,1)S(1)}, bf16[64,3584]{1,0:T(8,128)(2,1)S(1)}, u32[]{:S(2)}, u32[]{:S(2)}) %collective-permute-start.8) | collective-permute-done | bytes 458784 | tf_op jit(solution)/shard_map/ppermute | solution.py:63
  43.4 4.1 %collective-permute-done.7.c1 = bf16[64,3584]{1,0:T(8,128)(2,1)S(1)} collective-permute-done((bf16[64,3584]{1,0:T(8,128)(2,1)S(1)}, bf16[64,3584]{1,0:T(8,128)(2,1)S(1)}, u32[]{:S(2)}, u32[]{:S(2)}) %collective-permute-start.7) | collective-permute-done | bytes 458784 | tf_op jit(solution)/shard_map/ppermute | solution.py:63
  50.5 6.5 %collective-permute-done.10.c0 = bf16[64,3584]{1,0:T(8,128)(2,1)S(1)} collective-permute-done((bf16[64,3584]{1,0:T(8,128)(2,1)S(1)}, bf16[64,3584]{1,0:T(8,128)(2,1)S(1)}, u32[]{:S(2)}, u32[]{:S(2)}) %collective-permute-start.10) | collective-permute-done | bytes 458784 | tf_op jit(solution)/shard_map/ppermute | solution.py:63
  60.8 6.8 %collective-permute-start.14 = (f32[128,1536]{1,0:T(8,128)S(1)}, f32[128,1536]{1,0:T(8,128)S(1)}, u32[]{:S(2)}, u32[]{:S(2)}) collective-permute-start(f32[128,1536]{1,0:T(8,128)S(1)} %shard_map.99.refs_0_), channel_id=1, source_target_pairs={{0,1},{1,0},{2,3},{3,2},{4,5},{5,4},{6,7},{7,6},{8,9},{9,8},{10,11... | collective-permute-start | bytes 2359304 | tf_op jit(solution)/shard_map/ppermute | solution.py:34
  69.8 3.2 %collective-permute-start.15 = (f32[128,1536]{1,0:T(8,128)S(1)}, f32[128,1536]{1,0:T(8,128)S(1)}, u32[]{:S(2)}, u32[]{:S(2)}) collective-permute-start(f32[128,1536]{1,0:T(8,128)S(1)} %shard_map.100.refs_1_), channel_id=1, source_target_pairs={{0,1},{1,0},{2,3},{3,2},{4,5},{5,4},{6,7},{7,6},{8,9},{9,8},{10,11... | collective-permute-start | bytes 2359304 | tf_op jit(solution)/shard_map/ppermute | solution.py:34
  75.0 3.1 %shard_map.102 = (bf16[64,3584]{1,0:T(8,128)(2,1)S(1)}, bf16[64,3584]{1,0:T(8,128)(2,1)S(1)}, bf16[64,3584]{1,0:T(8,128)(2,1)S(1)}, bf16[64,3584]{1,0:T(8,128)(2,1)S(1)}) custom-call(f32[128,1536]{1,0:T(8,128)S(1)} %shard_map.99.refs_0_, f32[128,1536]{1,0:T(8,128)S(1)} %shard_map.100.refs_1_, f32[128,1536]{1,0:T(8,128)S(1)} %collective-permute-done.14.refs_2_, ...), custom_call_target="tpu_custom_call" | custom-call | tf_op jit(solution)/shard_map/pallas_call | solution.py:281
  78.0 3.5 %collective-permute-start.16 = (bf16[64,3584]{1,0:T(8,128)(2,1)S(1)}, bf16[64,3584]{1,0:T(8,128)(2,1)S(1)}, u32[]{:S(2)}, u32[]{:S(2)}) collective-permute-start(bf16[64,3584]{1,0:T(8,128)(2,1)S(1)} %get-tuple-element.64), channel_id=1, source_target_pairs={{0,32},{1,97},{2,34},{3,99},{4,36},{5,101},{6,38},{7,103},{8,40},{... | collective-permute-start | bytes 1376264 | tf_op jit(solution)/shard_map/ppermute | solution.py:63
  81.8 3.1 %shard_map.101 = (bf16[64,3584]{1,0:T(8,128)(2,1)S(1)}, bf16[64,3584]{1,0:T(8,128)(2,1)S(1)}, bf16[64,3584]{1,0:T(8,128)(2,1)S(1)}, bf16[64,3584]{1,0:T(8,128)(2,1)S(1)}) custom-call(f32[128,1536]{1,0:T(8,128)S(1)} %shard_map.99.refs_0_, f32[128,1536]{1,0:T(8,128)S(1)} %shard_map.100.refs_1_, f32[128,1536]{1,0:T(8,128)S(1)} %collective-permute-done.14.refs_2_, ...), custom_call_target="tpu_custom_call" | custom-call | tf_op jit(solution)/shard_map/pallas_call | solution.py:281
  84.9 6.0 %collective-permute-done.16 = bf16[64,3584]{1,0:T(8,128)(2,1)S(1)} collective-permute-done((bf16[64,3584]{1,0:T(8,128)(2,1)S(1)}, bf16[64,3584]{1,0:T(8,128)(2,1)S(1)}, u32[]{:S(2)}, u32[]{:S(2)}) %collective-permute-start.16) | collective-permute-done | bytes 458784 | tf_op jit(solution)/shard_map/ppermute | solution.py:63
  91.1 3.5 %collective-permute-start.21 = (bf16[64,3584]{1,0:T(8,128)(2,1)S(1)}, bf16[64,3584]{1,0:T(8,128)(2,1)S(1)}, u32[]{:S(2)}, u32[]{:S(2)}) collective-permute-start(bf16[64,3584]{1,0:T(8,128)(2,1)S(1)} %add_convert_fusion.1), channel_id=1, source_target_pairs={{0,32},{1,97},{2,34},{3,99},{4,36},{5,101},{6,38},{7,103},{8,40},{... | collective-permute-start | bytes 1376264 | tf_op jit(solution)/shard_map/ppermute | solution.py:63
  96.3 5.3 %collective-permute-done.21 = bf16[64,3584]{1,0:T(8,128)(2,1)S(1)} collective-permute-done((bf16[64,3584]{1,0:T(8,128)(2,1)S(1)}, bf16[64,3584]{1,0:T(8,128)(2,1)S(1)}, u32[]{:S(2)}, u32[]{:S(2)}) %collective-permute-start.21) | collective-permute-done | bytes 458784 | tf_op jit(solution)/shard_map/ppermute | solution.py:63
  102.0 7.8 %collective-permute-done.17.refs_1_ = bf16[64,3584]{1,0:T(8,128)(2,1)S(1)} collective-permute-done((bf16[64,3584]{1,0:T(8,128)(2,1)S(1)}, bf16[64,3584]{1,0:T(8,128)(2,1)S(1)}, u32[]{:S(2)}, u32[]{:S(2)}) %collective-permute-start.17) | collective-permute-done | bytes 458784 | tf_op jit(solution)/shard_map/ppermute | solution.py:63
  111.9 2.5 %collective-permute-start.23 = (bf16[16,3584]{1,0:T(8,128)(2,1)S(1)}, bf16[16,3584]{1,0:T(8,128)(2,1)S(1)}, u32[]{:S(2)}, u32[]{:S(2)}) collective-permute-start(bf16[16,3584]{1,0:T(8,128)(2,1)S(1)} %get-tuple-element.73), channel_id=1, source_target_pairs={{0,24},{1,25},{2,26},{3,27},{4,28},{5,29},{6,30},{7,31},{8,0},{9,1... | collective-permute-start | bytes 344072 | tf_op jit(solution)/shard_map/ppermute | solution.py:34
  117.3 2.2 %collective-permute-done.24.refs_2_ = bf16[16,3584]{1,0:T(8,128)(2,1)S(1)} collective-permute-done((bf16[16,3584]{1,0:T(8,128)(2,1)S(1)}, bf16[16,3584]{1,0:T(8,128)(2,1)S(1)}, u32[]{:S(2)}, u32[]{:S(2)}) %collective-permute-start.24) | collective-permute-done | bytes 114720 | tf_op jit(solution)/shard_map/ppermute | solution.py:34
  121.0 4.6 %collective-permute-start.26 = (bf16[16,3584]{1,0:T(8,128)(2,1)S(1)}, bf16[16,3584]{1,0:T(8,128)(2,1)S(1)}, u32[]{:S(2)}, u32[]{:S(2)}) collective-permute-start(bf16[16,3584]{1,0:T(8,128)(2,1)S(1)} %get-tuple-element.77), channel_id=1, source_target_pairs={{0,1},{1,0},{2,3},{3,2},{4,5},{5,4},{6,7},{7,6},{8,9},{9,8},{10,11... | collective-permute-start | bytes 344072 | tf_op jit(solution)/shard_map/ppermute | solution.py:34
  125.6 2.6 %collective-permute-start.27 = (bf16[16,3584]{1,0:T(8,128)(2,1)S(1)}, bf16[16,3584]{1,0:T(8,128)(2,1)S(1)}, u32[]{:S(2)}, u32[]{:S(2)}) collective-permute-start(bf16[16,3584]{1,0:T(8,128)(2,1)S(1)} %get-tuple-element.78), channel_id=1, source_target_pairs={{0,6},{1,7},{2,4},{3,5},{4,2},{5,3},{6,0},{7,1},{8,14},{9,15},{10,... | collective-permute-start | bytes 344072 | tf_op jit(solution)/shard_map/ppermute | solution.py:34
  128.5 3.0 %collective-permute-done.27.far_own = bf16[16,3584]{1,0:T(8,128)(2,1)S(1)} collective-permute-done((bf16[16,3584]{1,0:T(8,128)(2,1)S(1)}, bf16[16,3584]{1,0:T(8,128)(2,1)S(1)}, u32[]{:S(2)}, u32[]{:S(2)}) %collective-permute-start.27) | collective-permute-done | bytes 114720 | tf_op jit(solution)/shard_map/ppermute | solution.py:34
  131.5 3.0 %collective-permute-done.28.far_got = bf16[16,3584]{1,0:T(8,128)(2,1)S(1)} collective-permute-done((bf16[16,3584]{1,0:T(8,128)(2,1)S(1)}, bf16[16,3584]{1,0:T(8,128)(2,1)S(1)}, u32[]{:S(2)}, u32[]{:S(2)}) %collective-permute-start.28) | collective-permute-done | bytes 114720 | tf_op jit(solution)/shard_map/ppermute | solution.py:34
  134.5 3.6 %shard_map.105 = (bf16[128,7168]{1,0:T(8,128)(2,1)}, bf16[128,7168]{1,0:T(8,128)(2,1)}, f32[2,128]{1,0:T(2,128)}) custom-call(s32[2,128]{1,0:T(2,128)S(1)} %bitcast.4, f32[2,128]{1,0:T(2,128)S(1)} %bitcast.6, bf16[128,7168]{1,0:T(8,128)(2,1)S(1)} %copy-done.5, bf16[128,7168]{1,0:T(8,128)(2,1)S(1)} %copy-done.7, ...), custom_call_target="tpu_custom_call" | custom-call | tf_op jit(solution)/shard_map/pallas_call | solution.py:281
  (73 shorter events, 40.8 us)
Async XLA Ops:
  13.7 44.2 %collective-permute-start.9 = (bf16[10752,256]{1,0:T(8,128)(2,1)S(1)}, bf16[10752,256]{1,0:T(8,128)(2,1)S(1)}, u32[]{:S(2)}, u32[]{:S(2)}) collective-permute-start(bf16[10752,256]{1,0:T(8,128)(2,1)S(1)} %shard_map.97), channel_id=1, source_target_pairs={{0,1},{1,0},{2,3},{3,2},{4,5},{5,4},{6,7},{7,6},{8,9},{9,8},{10,11... | collective-permute-start | bytes 16515080 | tf_op jit(solution)/shard_map/ppermute | solution.py:34
  14.1 6.1 %collective-permute-start.1 = (bf16[16,3584]{1,0:T(8,128)(2,1)S(1)}, bf16[16,3584]{1,0:T(8,128)(2,1)S(1)}, u32[]{:S(2)}, u32[]{:S(2)}) collective-permute-start(bf16[16,3584]{1,0:T(8,128)(2,1)S(1)} %get-tuple-element.46), channel_id=1, source_target_pairs={{0,6},{1,7},{2,4},{3,5},{4,2},{5,3},{6,0},{7,1},{8,14},{9,15},{10,... | collective-permute-start | bytes 344072 | tf_op jit(solution)/shard_map/ppermute | solution.py:34
  17.0 6.5 %collective-permute-start.2 = (bf16[16,3584]{1,0:T(8,128)(2,1)S(1)}, bf16[16,3584]{1,0:T(8,128)(2,1)S(1)}, u32[]{:S(2)}, u32[]{:S(2)}) collective-permute-start(bf16[16,3584]{1,0:T(8,128)(2,1)S(1)} %get-tuple-element.47), channel_id=1, source_target_pairs={{0,7},{1,6},{2,5},{3,4},{4,3},{5,2},{6,1},{7,0},{8,15},{9,14},{10,... | collective-permute-start | bytes 344072 | tf_op jit(solution)/shard_map/ppermute | solution.py:34
  23.7 7.0 %collective-permute-start.3 = (bf16[16,3584]{1,0:T(8,128)(2,1)S(1)}, bf16[16,3584]{1,0:T(8,128)(2,1)S(1)}, u32[]{:S(2)}, u32[]{:S(2)}) collective-permute-start(bf16[16,3584]{1,0:T(8,128)(2,1)S(1)} %get-tuple-element.49), channel_id=1, source_target_pairs={{0,8},{1,9},{2,10},{3,11},{4,12},{5,13},{6,14},{7,15},{8,16},{9,17... | collective-permute-start | bytes 344072 | tf_op jit(solution)/shard_map/ppermute | solution.py:34
  25.4 8.6 %collective-permute-start.4 = (bf16[16,3584]{1,0:T(8,128)(2,1)S(1)}, bf16[16,3584]{1,0:T(8,128)(2,1)S(1)}, u32[]{:S(2)}, u32[]{:S(2)}) collective-permute-start(bf16[16,3584]{1,0:T(8,128)(2,1)S(1)} %get-tuple-element.50), channel_id=1, source_target_pairs={{0,16},{1,17},{2,18},{3,19},{4,20},{5,21},{6,22},{7,23},{8,24},{9,... | collective-permute-start | bytes 344072 | tf_op jit(solution)/shard_map/ppermute | solution.py:34
  34.1 9.3 %collective-permute-start.8 = (bf16[64,3584]{1,0:T(8,128)(2,1)S(1)}, bf16[64,3584]{1,0:T(8,128)(2,1)S(1)}, u32[]{:S(2)}, u32[]{:S(2)}) collective-permute-start(bf16[64,3584]{1,0:T(8,128)(2,1)S(1)} %shard_map.96.c0), channel_id=1, source_target_pairs={{0,96},{1,33},{2,98},{3,35},{4,100},{5,37},{6,102},{7,39},{8,104},... | collective-permute-start | bytes 1376264 | tf_op jit(solution)/shard_map/ppermute | solution.py:63
  35.3 12.1 %collective-permute-start.7 = (bf16[64,3584]{1,0:T(8,128)(2,1)S(1)}, bf16[64,3584]{1,0:T(8,128)(2,1)S(1)}, u32[]{:S(2)}, u32[]{:S(2)}) collective-permute-start(bf16[64,3584]{1,0:T(8,128)(2,1)S(1)} %shard_map.96.c0), channel_id=1, source_target_pairs={{0,32},{1,97},{2,34},{3,99},{4,36},{5,101},{6,38},{7,103},{8,40},{... | collective-permute-start | bytes 1376264 | tf_op jit(solution)/shard_map/ppermute | solution.py:63
  36.8 10.7 %collective-permute-start.6 = (bf16[64,3584]{1,0:T(8,128)(2,1)S(1)}, bf16[64,3584]{1,0:T(8,128)(2,1)S(1)}, u32[]{:S(2)}, u32[]{:S(2)}) collective-permute-start(bf16[64,3584]{1,0:T(8,128)(2,1)S(1)} %shard_map.96.c0), channel_id=1, source_target_pairs={{0,2},{1,3},{2,0},{3,1},{4,6},{5,7},{6,4},{7,5},{8,10},{9,11},{10,... | collective-permute-start | bytes 1376264 | tf_op jit(solution)/shard_map/ppermute | solution.py:34
  47.5 9.4 %collective-permute-start.10 = (bf16[64,3584]{1,0:T(8,128)(2,1)S(1)}, bf16[64,3584]{1,0:T(8,128)(2,1)S(1)}, u32[]{:S(2)}, u32[]{:S(2)}) collective-permute-start(bf16[64,3584]{1,0:T(8,128)(2,1)S(1)} %collective-permute-done.6.c3), channel_id=1, source_target_pairs={{0,96},{1,33},{2,98},{3,35},{4,100},{5,37},{6,102},{7,39},{8,104},... | collective-permute-start | bytes 1376264 | tf_op jit(solution)/shard_map/ppermute | solution.py:63
  48.7 18.9 %collective-permute-start.12 = (bf16[64,3584]{1,0:T(8,128)(2,1)S(1)}, bf16[64,3584]{1,0:T(8,128)(2,1)S(1)}, u32[]{:S(2)}, u32[]{:S(2)}) collective-permute-start(bf16[64,3584]{1,0:T(8,128)(2,1)S(1)} %collective-permute-done.7.c1), channel_id=1, source_target_pairs={{0,32},{1,97},{2,34},{3,99},{4,36},{5,101},{6,38},{7,103},{8,40},{... | collective-permute-start | bytes 1376264 | tf_op jit(solution)/shard_map/ppermute | solution.py:63
  50.2 17.4 %collective-permute-start.11 = (bf16[64,3584]{1,0:T(8,128)(2,1)S(1)}, bf16[64,3584]{1,0:T(8,128)(2,1)S(1)}, u32[]{:S(2)}, u32[]{:S(2)}) collective-permute-start(bf16[64,3584]{1,0:T(8,128)(2,1)S(1)} %collective-permute-done.7.c1), channel_id=1, source_target_pairs={{0,2},{1,3},{2,0},{3,1},{4,6},{5,7},{6,4},{7,5},{8,10},{9,11},{10,... | collective-permute-start | bytes 1376264 | tf_op jit(solution)/shard_map/ppermute | solution.py:34
  56.9 10.7 %collective-permute-start.13 = (bf16[64,3584]{1,0:T(8,128)(2,1)S(1)}, bf16[64,3584]{1,0:T(8,128)(2,1)S(1)}, u32[]{:S(2)}, u32[]{:S(2)}) collective-permute-start(bf16[64,3584]{1,0:T(8,128)(2,1)S(1)} %collective-permute-done.10.c0), channel_id=1, source_target_pairs={{0,96},{1,33},{2,98},{3,35},{4,100},{5,37},{6,102},{7,39},{8,104},... | collective-permute-start | bytes 1376264 | tf_op jit(solution)/shard_map/ppermute | solution.py:63
  60.8 12.3 %collective-permute-start.14 = (f32[128,1536]{1,0:T(8,128)S(1)}, f32[128,1536]{1,0:T(8,128)S(1)}, u32[]{:S(2)}, u32[]{:S(2)}) collective-permute-start(f32[128,1536]{1,0:T(8,128)S(1)} %shard_map.99.refs_0_), channel_id=1, source_target_pairs={{0,1},{1,0},{2,3},{3,2},{4,5},{5,4},{6,7},{7,6},{8,9},{9,8},{10,11... | collective-permute-start | bytes 2359304 | tf_op jit(solution)/shard_map/ppermute | solution.py:34
  78.0 12.9 %collective-permute-start.16 = (bf16[64,3584]{1,0:T(8,128)(2,1)S(1)}, bf16[64,3584]{1,0:T(8,128)(2,1)S(1)}, u32[]{:S(2)}, u32[]{:S(2)}) collective-permute-start(bf16[64,3584]{1,0:T(8,128)(2,1)S(1)} %get-tuple-element.64), channel_id=1, source_target_pairs={{0,32},{1,97},{2,34},{3,99},{4,36},{5,101},{6,38},{7,103},{8,40},{... | collective-permute-start | bytes 1376264 | tf_op jit(solution)/shard_map/ppermute | solution.py:63
  81.5 13.1 %collective-permute-start.18 = (bf16[64,3584]{1,0:T(8,128)(2,1)S(1)}, bf16[64,3584]{1,0:T(8,128)(2,1)S(1)}, u32[]{:S(2)}, u32[]{:S(2)}) collective-permute-start(bf16[64,3584]{1,0:T(8,128)(2,1)S(1)} %get-tuple-element.67), channel_id=1, source_target_pairs={{0,96},{1,33},{2,98},{3,35},{4,100},{5,37},{6,102},{7,39},{8,104},... | collective-permute-start | bytes 1376264 | tf_op jit(solution)/shard_map/ppermute | solution.py:63
  81.5 13.1 %collective-permute-start.19 = (bf16[64,3584]{1,0:T(8,128)(2,1)S(1)}, bf16[64,3584]{1,0:T(8,128)(2,1)S(1)}, u32[]{:S(2)}, u32[]{:S(2)}) collective-permute-start(bf16[64,3584]{1,0:T(8,128)(2,1)S(1)} %get-tuple-element.68), channel_id=1, source_target_pairs={{0,2},{1,3},{2,0},{3,1},{4,6},{5,7},{6,4},{7,5},{8,10},{9,11},{10,... | collective-permute-start | bytes 1376264 | tf_op jit(solution)/shard_map/ppermute | solution.py:34
  91.1 10.5 %collective-permute-start.21 = (bf16[64,3584]{1,0:T(8,128)(2,1)S(1)}, bf16[64,3584]{1,0:T(8,128)(2,1)S(1)}, u32[]{:S(2)}, u32[]{:S(2)}) collective-permute-start(bf16[64,3584]{1,0:T(8,128)(2,1)S(1)} %add_convert_fusion.1), channel_id=1, source_target_pairs={{0,32},{1,97},{2,34},{3,99},{4,36},{5,101},{6,38},{7,103},{8,40},{... | collective-permute-start | bytes 1376264 | tf_op jit(solution)/shard_map/ppermute | solution.py:63
  94.6 15.3 %collective-permute-start.17 = (bf16[64,3584]{1,0:T(8,128)(2,1)S(1)}, bf16[64,3584]{1,0:T(8,128)(2,1)S(1)}, u32[]{:S(2)}, u32[]{:S(2)}) collective-permute-start(bf16[64,3584]{1,0:T(8,128)(2,1)S(1)} %get-tuple-element.65), channel_id=1, source_target_pairs={{0,32},{1,97},{2,34},{3,99},{4,36},{5,101},{6,38},{7,103},{8,40},{... | collective-permute-start | bytes 1376264 | tf_op jit(solution)/shard_map/ppermute | solution.py:63
  94.8 15.0 %collective-permute-start.20 = (bf16[64,3584]{1,0:T(8,128)(2,1)S(1)}, bf16[64,3584]{1,0:T(8,128)(2,1)S(1)}, u32[]{:S(2)}, u32[]{:S(2)}) collective-permute-start(bf16[64,3584]{1,0:T(8,128)(2,1)S(1)} %add_convert_fusion.2), channel_id=1, source_target_pairs={{0,96},{1,33},{2,98},{3,35},{4,100},{5,37},{6,102},{7,39},{8,104},... | collective-permute-start | bytes 1376264 | tf_op jit(solution)/shard_map/ppermute | solution.py:63
  101.7 10.0 %collective-permute-start.22 = (bf16[64,3584]{1,0:T(8,128)(2,1)S(1)}, bf16[64,3584]{1,0:T(8,128)(2,1)S(1)}, u32[]{:S(2)}, u32[]{:S(2)}) collective-permute-start(bf16[64,3584]{1,0:T(8,128)(2,1)S(1)} %add_convert_fusion), channel_id=1, source_target_pairs={{0,2},{1,3},{2,0},{3,1},{4,6},{5,7},{6,4},{7,5},{8,10},{9,11},{10,... | collective-permute-start | bytes 1376264 | tf_op jit(solution)/shard_map/ppermute | solution.py:34
  111.9 5.5 %collective-permute-start.23 = (bf16[16,3584]{1,0:T(8,128)(2,1)S(1)}, bf16[16,3584]{1,0:T(8,128)(2,1)S(1)}, u32[]{:S(2)}, u32[]{:S(2)}) collective-permute-start(bf16[16,3584]{1,0:T(8,128)(2,1)S(1)} %get-tuple-element.73), channel_id=1, source_target_pairs={{0,24},{1,25},{2,26},{3,27},{4,28},{5,29},{6,30},{7,31},{8,0},{9,1... | collective-permute-start | bytes 344072 | tf_op jit(solution)/shard_map/ppermute | solution.py:34
  121.0 7.5 %collective-permute-start.26 = (bf16[16,3584]{1,0:T(8,128)(2,1)S(1)}, bf16[16,3584]{1,0:T(8,128)(2,1)S(1)}, u32[]{:S(2)}, u32[]{:S(2)}) collective-permute-start(bf16[16,3584]{1,0:T(8,128)(2,1)S(1)} %get-tuple-element.77), channel_id=1, source_target_pairs={{0,1},{1,0},{2,3},{3,2},{4,5},{5,4},{6,7},{7,6},{8,9},{9,8},{10,11... | collective-permute-start | bytes 344072 | tf_op jit(solution)/shard_map/ppermute | solution.py:34
  125.6 5.9 %collective-permute-start.27 = (bf16[16,3584]{1,0:T(8,128)(2,1)S(1)}, bf16[16,3584]{1,0:T(8,128)(2,1)S(1)}, u32[]{:S(2)}, u32[]{:S(2)}) collective-permute-start(bf16[16,3584]{1,0:T(8,128)(2,1)S(1)} %get-tuple-element.78), channel_id=1, source_target_pairs={{0,6},{1,7},{2,4},{3,5},{4,2},{5,3},{6,0},{7,1},{8,14},{9,15},{10,... | collective-permute-start | bytes 344072 | tf_op jit(solution)/shard_map/ppermute | solution.py:34
  128.2 6.3 %collective-permute-start.28 = (bf16[16,3584]{1,0:T(8,128)(2,1)S(1)}, bf16[16,3584]{1,0:T(8,128)(2,1)S(1)}, u32[]{:S(2)}, u32[]{:S(2)}) collective-permute-start(bf16[16,3584]{1,0:T(8,128)(2,1)S(1)} %get-tuple-element.79), channel_id=1, source_target_pairs={{0,7},{1,6},{2,5},{3,4},{4,3},{5,2},{6,1},{7,0},{8,15},{9,14},{10,... | collective-permute-start | bytes 344072 | tf_op jit(solution)/shard_map/ppermute | solution.py:34
  (17 other events, 283.8 us)

commit v3 on v2

--- a/solution.py
+++ b/solution.py
@@ -12,7 +12,9 @@
 VMEM = pl.BlockSpec(memory_space=pltpu.VMEM)
 HBM = pl.BlockSpec(memory_space=pltpu.HBM)
 LIMIT = 16 * 1024 * 1024
+BIG = 54 * 1024 * 1024
 NZ = 4
+HALVES = 2
 
 
 def dot(a, b, dims):
@@ -81,7 +83,56 @@
     return ((z + k) & 3) * 2 + ((h + r) & 1)
 
 
-def dispatch_kernel(half, ids_ref, gates_ref, tok_hbm, grad_hbm, near_own, far_own, near_other, far_other, tok_v, grad_v, sems):
+def weight_copies(half, core, wg_ref, wu_ref, wd_ref, out_ref, sems):
+    at = core * half
+    rows = pl.ds(pl.multiple_of(at, 256), half)
+    copies = [
+        pltpu.make_async_copy(wg_ref.at[0, rows, :], out_ref.at[pl.ds(0, half), :], sems.at[0]),
+        pltpu.make_async_copy(wu_ref.at[0, rows, :], out_ref.at[pl.ds(half, half), :], sems.at[1]),
+    ]
+    for n in range(half // 256):
+        cols = pl.ds(pl.multiple_of(at + 256 * n, 256), 256)
+        into = out_ref.at[pl.ds(2 * half + 256 * n, 256), :]
+        copies.append(pltpu.make_async_copy(wd_ref.at[0, :, cols], into, sems.at[2 + n]))
+    for copy in copies:
+        copy.start()
+    return copies
+
+
+def weights_kernel(half, after_ref, wg_ref, wu_ref, wd_ref, out_ref, sems):
+    core = lax.axis_index("expert") & 1
+    for copy in weight_copies(half, core, wg_ref, wu_ref, wd_ref, out_ref, sems):
+        copy.wait()
+
+
+def dispatch_kernel(
+    half,
+    ids_hbm,
+    gates_hbm,
+    tok_hbm,
+    grad_hbm,
+    wg_hbm,
+    wu_hbm,
+    wd_hbm,
+    near_own,
+    far_own,
+    near_other,
+    far_other,
+    w_send,
+    ids_ref,
+    gates_ref,
+    tok_v,
+    grad_v,
+    sems,
+    small,
+    w_sems,
+):
+    few = [
+        pltpu.make_async_copy(ids_hbm, ids_ref, small.at[0]),
+        pltpu.make_async_copy(gates_hbm, gates_ref, small.at[1]),
+    ]
+    for copy in few:
+        copy.start()
     at = lax.axis_index("expert")
     core = at & 1
     h = (at >> 2) & 1
@@ -94,6 +145,9 @@
         one.start()
         two.start()
         copies.append((one, two))
+    big = weight_copies(half, 1 - core, wg_hbm, wu_hbm, wd_hbm, w_send, w_sems)
+    for copy in few:
+        copy.wait()
     rows, tok = 32, ids_ref.shape[1]
     s = lax.broadcasted_iota(jnp.int32, (rows, tok), 0)
     sel_first, sel_second = selection(ids_ref[...], rows, slot_expert((s >> 1) & 3, s >> 4, z, h), s & 1)
@@ -114,6 +168,8 @@
         got = got.astype(BF)
         near[...] = got[0:16, :]
         far[...] = got[16:32, :]
+    for copy in big:
+        copy.wait()
 
 
 def merge_kernel(near_own, near_got, far_own, far_got, *outs):
@@ -128,34 +184,21 @@
         out[...] = both[16 * n : 16 * n + 16, :]
 
 
-def assemble_kernel(*refs):
-    msgs, out = refs[:4], refs[4]
-    wide = [m[...].astype(F32) for m in msgs]
-    out[...] = jnp.concatenate([m[0:8] for m in wide] + [m[8:16] for m in wide], axis=0).astype(BF)
-
-
-def weights_kernel(half, flip, wg_ref, wu_ref, wd_ref, out_ref, sems):
-    core = lax.axis_index("expert") & 1
-    at = (1 - core if flip else core) * half
-    rows = pl.ds(pl.multiple_of(at, 256), half)
-    copies = [
-        pltpu.make_async_copy(wg_ref.at[0, rows, :], out_ref.at[pl.ds(0, half), :], sems.at[0]),
-        pltpu.make_async_copy(wu_ref.at[0, rows, :], out_ref.at[pl.ds(half, half), :], sems.at[1]),
-    ]
-    for n in range(half // 256):
-        cols = pl.ds(pl.multiple_of(at + 256 * n, 256), 256)
-        into = out_ref.at[pl.ds(2 * half + 256 * n, 256), :]
-        copies.append(pltpu.make_async_copy(wd_ref.at[0, :, cols], into, sems.at[2 + n]))
-    for copy in copies:
-        copy.start()
-    for copy in copies:
-        copy.wait()
-
-
-def first_kernel(half, c0, c1, c2, c3, own, got, out, rows, grads):
-    for n, chunk in enumerate((c0, c1, c2, c3)):
-        rows[pl.ds(32 * n, 32), :] = chunk[0:32, :]
-        grads[pl.ds(32 * n, 32), :] = chunk[32:64, :]
+def assemble_kernel(m0, m1, m2, m3, *outs):
+    wide = [m[...].astype(F32) for m in (m0, m1, m2, m3)]
+    full = jnp.concatenate([m[0:8] for m in wide] + [m[8:16] for m in wide], axis=0).astype(BF)
+    part = full.shape[1] // len(outs)
+    for n, out in enumerate(outs):
+        out[...] = full[:, part * n : part * n + part]
+
+
+def first_kernel(half, *refs):
+    chunks, (own, got, out, rows, grads) = refs[:-5], refs[-5:]
+    part = chunks[0].shape[1]
+    for n, chunk in enumerate(chunks):
+        at, cols = pl.ds(32 * (n // HALVES), 32), pl.ds(part * (n % HALVES), part)
+        rows[at, cols] = chunk[0:32, :]
+        grads[at, cols] = chunk[32:64, :]
     for m, w in enumerate((own, got)):
         at = 256 * m
         out[:, at : at + 256] = dot(rows[...], w[0:half, :], ((1,), (0,)))
@@ -175,7 +218,7 @@
 
 def second_kernel(half, chunks, *refs):
     parts, (own, got) = refs[:4], refs[4:6]
-    outs, (hid_ref, ga_ref, gb_ref) = refs[6:10], refs[10:]
+    outs, (hid_ref, ga_ref, gb_ref) = refs[6:-3], refs[-3:]
     for n, (a_at, b_at) in enumerate(chunks):
         late = (a_at, b_at) in LATE
         mine, theirs = parts[1 if late else 0], parts[3 if late else 2]
@@ -210,16 +253,23 @@
             res = one if res is None else res + one
             gres = two if gres is None else gres + two
         res, gres = res.astype(BF), gres.astype(BF)
-        for k, out in enumerate(outs):
-            out[0:32, at : at + 256] = res[32 * k : 32 * k + 32, :]
-            out[32:64, at : at + 256] = gres[32 * k : 32 * k + 32, :]
+        part = half // HALVES
+        for k in range(len(chunks)):
+            out = outs[HALVES * k + at // part]
+            into = at % part
+            out[0:32, into : into + 256] = res[32 * k : 32 * k + 32, :]
+            out[32:64, into : into + 256] = gres[32 * k : 32 * k + 32, :]
 
 
 def finish_kernel(*refs):
-    terms, outs = refs[:4], refs[4:]
-    total = terms[0][...].astype(F32)
-    for ref in terms[1:]:
-        total += ref[...].astype(F32)
+    terms, outs = refs[:-4], refs[-4:]
+    totals = []
+    for n in range(HALVES):
+        total = terms[4 * n][...].astype(F32)
+        for ref in terms[4 * n + 1 : 4 * n + 4]:
+            total += ref[...].astype(F32)
+        totals.append(total)
+    total = jnp.concatenate(totals, axis=1)
     for k, out in enumerate(outs):
         out[...] = jnp.concatenate([total[8 * k : 8 * k + 8], total[32 + 8 * k : 40 + 8 * k]], axis=0).astype(BF)
 
@@ -237,9 +287,14 @@
         out[...] = both[16 * n : 16 * n + 16, :]
 
 
-def tail_kernel(half, ids_ref, gates_ref, tok_ref, grad_ref, near_own, near_got, far_own, far_got, mixed_ref, gt_ref, gg_ref):
+def tail_kernel(half, other, ids_ref, gates_ref, tok_ref, grad_ref, near, far, *refs):
+    if other:
+        inner_ref, _, _, mixed_hbm, gt_hbm, gg_ref, mixed_ref, gt_ref, sems = refs
+    else:
+        mixed_hbm, gt_hbm, inner_ref, mixed_ref, gt_ref, sems = refs
     at = lax.axis_index("expert")
     core = at & 1
+    which = 1 - core if other else core
     rows, tok = 16, ids_ref.shape[1]
     s = lax.broadcasted_iota(jnp.int32, (rows, tok), 0)
     expert = slot_expert((s >> 1) & 3, s >> 3, at >> 3, (at >> 2) & 1)
@@ -251,51 +306,91 @@
         axis=1,
         keepdims=True,
     )
-    inner = jnp.zeros((16, 1), F32)
-    for which, near, far in ((core, near_own, far_own), (1 - core, near_got, far_got)):
-        cols = pl.ds(pl.multiple_of(which * half, 128), half)
-        one, two = near[...].astype(F32), far[...].astype(F32)
-        out_rows = jnp.concatenate([one[0:8], two[0:8]], axis=0)
-        grad_rows = jnp.concatenate([one[8:16], two[8:16]], axis=0).astype(BF)
-        grad = grad_ref[:, cols]
-        inner += jnp.sum(dot(member, grad, ((1,), (0,))) * out_rows, axis=1, keepdims=True)
-        scaled = out_rows * gate
-        high = scaled.astype(BF)
-        low = (scaled - high.astype(F32)).astype(BF)
-        add = dot(member, high, ((0,), (0,))) + dot(member, low, ((0,), (0,)))
-        mixed_ref[:, cols] = (tok_ref[:, cols].astype(F32) + add).astype(BF)
-        gt_ref[:, cols] = (grad.astype(F32) + dot(member, grad_rows, ((0,), (0,)))).astype(BF)
-    gg_ref[0:1, :] = jnp.sum(sel_first * inner, axis=0, keepdims=True)
-    gg_ref[1:2, :] = jnp.sum(sel_second * inner, axis=0, keepdims=True)
-
-
-def params():
-    return pltpu.CompilerParams(vmem_limit_bytes=LIMIT)
+    cols = pl.ds(pl.multiple_of(which * half, 128), half)
+    one, two = near[...].astype(F32), far[...].astype(F32)
+    out_rows = jnp.concatenate([one[0:8], two[0:8]], axis=0)
+    grad_rows = jnp.concatenate([one[8:16], two[8:16]], axis=0).astype(BF)
+    grad = grad_ref[:, cols]
+    gt_ref[...] = (grad.astype(F32) + dot(member, grad_rows, ((0,), (0,)))).astype(BF)
+    first = pltpu.make_async_copy(gt_ref, gt_hbm.at[:, cols], sems.at[0])
+    first.start()
+    scaled = out_rows * gate
+    high = scaled.astype(BF)
+    low = (scaled - high.astype(F32)).astype(BF)
+    add = dot(member, high, ((0,), (0,))) + dot(member, low, ((0,), (0,)))
+    mixed_ref[...] = (tok_ref[:, cols].astype(F32) + add).astype(BF)
+    second = pltpu.make_async_copy(mixed_ref, mixed_hbm.at[:, cols], sems.at[1])
+    second.start()
+    inner = jnp.sum(dot(member, grad, ((1,), (0,))) * out_rows, axis=1, keepdims=True)
+    if other:
+        inner += inner_ref[:, 0:1]
+        gg_ref[0:1, :] = jnp.sum(sel_first * inner, axis=0, keepdims=True)
+        gg_ref[1:2, :] = jnp.sum(sel_second * inner, axis=0, keepdims=True)
+    else:
+        inner_ref[...] = jnp.broadcast_to(inner, inner_ref.shape)
+    first.wait()
+    second.wait()
 
 
 def shape(rows, cols, dtype=BF):
     return jax.ShapeDtypeStruct((rows, cols), dtype)
 
 
-def whole(kernel, outs, args, scratch=(), specs=None):
+def whole(kernel, outs, args, scratch=(), specs=None, limit=LIMIT):
     return pl.pallas_call(
         kernel,
         out_shape=outs,
         in_specs=specs or [VMEM] * len(args),
         out_specs=jax.tree.map(lambda _: VMEM, outs),
         scratch_shapes=list(scratch),
-        compiler_params=params(),
+        compiler_params=pltpu.CompilerParams(vmem_limit_bytes=limit),
     )(*args)
 
 
-def weights(half, flip, w_gate, w_up, w_down):
+def weights(half, after, w_gate, w_up, w_down):
     return whole(
-        functools.partial(weights_kernel, half, flip),
+        functools.partial(weights_kernel, half),
         shape(3 * half, w_gate.shape[2]),
-        (w_gate, w_up, w_down),
+        (after, w_gate, w_up, w_down),
         [pltpu.SemaphoreType.DMA((2 + half // 256,))],
-        [HBM] * 3,
+        [HBM] * 4,
     )
+
+
+def add(*terms):
+    total = terms[0].astype(F32)
+    for term in terms[1:]:
+        total = total + term.astype(F32)
+    return total.astype(BF)
+
+
+def first_hops(start):
+    return {
+        (0, 0): start,
+        (0, 1): other_l(start),
+        (3, 0): along_x(start, 1),
+        (1, 0): along_x(start, -1),
+    }
+
+
+def other_hops(t):
+    t[0, 1], t[3, 0], t[1, 0] = lax.optimization_barrier((t[0, 1], t[3, 0], t[1, 0]))
+    t[1, 1] = along_x(t[0, 1], -1)
+    t[3, 1] = other_l(t[3, 0])
+    t[2, 0] = along_x(t[3, 0], 1)
+    t[2, 1] = along_x(t[1, 1], -1)
+
+
+def reduced(q):
+    f21 = along_x(q[2, 1], 1)
+    f20 = along_x(q[2, 0], -1)
+    f31 = other_l(q[3, 1])
+    q10, f21 = lax.optimization_barrier((q[1, 0], f21))
+    f10 = along_x(q10, 1)
+    f11 = along_x(add(q[1, 1], f21), 1)
+    f30 = along_x(add(q[3, 0], f20, f31), -1)
+    f01 = other_l(add(q[0, 1], f11))
+    return [q[0, 0], f10, f30, f01]
 
 
 def shards(tokens, expert_ids, gates, grad_mixed, w_gate, w_up, w_down):
@@ -304,32 +399,38 @@
     ids_t = expert_ids.T
     gates_t = gates.T
 
-    near_own, far_own, near_other, far_other = whole(
+    near_own, far_own, near_other, far_other, w_send = whole(
         functools.partial(dispatch_kernel, half),
-        [shape(16, half)] * 4,
-        (ids_t, gates_t, tokens, grad_mixed),
-        [pltpu.VMEM((2, tok, half), BF), pltpu.VMEM((2, tok, half), BF), pltpu.SemaphoreType.DMA((2, 2))],
-        [VMEM, VMEM, HBM, HBM],
+        [shape(16, half)] * 4 + [shape(3 * half, w_gate.shape[2])],
+        (ids_t, gates_t, tokens, grad_mixed, w_gate, w_up, w_down),
+        [
+            pltpu.VMEM((2, tok), jnp.int32),
+            pltpu.VMEM((2, tok), F32),
+            pltpu.VMEM((2, tok, half), BF),
+            pltpu.VMEM((2, tok, half), BF),
+            pltpu.SemaphoreType.DMA((2, 2)),
+            pltpu.SemaphoreType.DMA((2,)),
+            pltpu.SemaphoreType.DMA((2 + half // 256,)),
+        ],
+        [HBM] * 7,
+        BIG,
     )
     near_got = other_core(near_other)
     far_got = [other_y(far_own), other_y_core(far_other)]
-    near_got, wg_src, wu_src, wd_src = lax.optimization_barrier((near_got, w_gate, w_up, w_down))
-    w_got = other_core(weights(half, True, wg_src, wu_src, wd_src))
+    w_got = other_core(w_send)
     msgs = whole(merge_kernel, [shape(16, half)] * 4, (near_own, near_got, *far_got))
     across = along_z(msgs[2], 2)
     msgs = [msgs[0], along_z(msgs[1], 1), across, along_z(msgs[3], 3)]
-    t = {(0, 0): whole(assemble_kernel, shape(64, half), msgs)}
-
-    t[0, 1] = other_l(t[0, 0])
-    t[3, 0] = along_x(t[0, 0], 1)
-    t[1, 0] = along_x(t[0, 0], -1)
-    w_got, wg_src, wu_src, wd_src = lax.optimization_barrier((w_got, wg_src, wu_src, wd_src))
-    w_own = weights(half, False, wg_src, wu_src, wd_src)
-    t[0, 1], t[3, 0], t[1, 0] = lax.optimization_barrier((t[0, 1], t[3, 0], t[1, 0]))
-    t[1, 1] = along_x(t[0, 1], -1)
-    t[3, 1] = other_l(t[3, 0])
-    t[2, 0] = along_x(t[3, 0], 1)
-    t[2, 1] = along_x(t[1, 1], -1)
+    part = half // HALVES
+    starts = whole(assemble_kernel, [shape(64, part)] * HALVES, msgs)
+    gathered = []
+    for start in starts:
+        if gathered:
+            gathered[0][0, 1], start = lax.optimization_barrier((gathered[0][0, 1], start))
+        gathered.append(first_hops(start))
+    w_own = weights(half, w_got, w_gate, w_up, w_down)
+    for t in gathered:
+        other_hops(t)
 
     fdev = w_gate.shape[2]
     parts = []
@@ -338,7 +439,7 @@
             whole(
                 functools.partial(first_kernel, half),
                 shape(128, 6 * fdev, F32),
-                [t[o] for o in group] + [w_own, w_got],
+                [t[o] for o in group for t in gathered] + [w_own, w_got],
                 [pltpu.VMEM((128, half), BF)] * 2,
             )
         )
@@ -347,35 +448,39 @@
     for group in (SENT, KEPT):
         res = whole(
             functools.partial(second_kernel, half, group),
-            [shape(64, half)] * 4,
+            [shape(64, part)] * (len(group) * HALVES),
             parts + [w_own, w_got],
-            [pltpu.VMEM((128, 2 * fdev), BF)] * 3,
+            [pltpu.VMEM((32 * len(group), 2 * fdev), BF)] * 3,
         )
-        q.update(zip(group, res))
-
-    def add(*terms):
-        total = terms[0].astype(F32)
-        for term in terms[1:]:
-            total = total + term.astype(F32)
-        return total.astype(BF)
-
-    f21 = along_x(q[2, 1], 1)
-    f20 = along_x(q[2, 0], -1)
-    f31 = other_l(q[3, 1])
-    q[1, 0], f21 = lax.optimization_barrier((q[1, 0], f21))
-    f10 = along_x(q[1, 0], 1)
-    f11 = along_x(add(q[1, 1], f21), 1)
-    f30 = along_x(add(q[3, 0], f20, f31), -1)
-    f01 = other_l(add(q[0, 1], f11))
-    back = whole(finish_kernel, [shape(16, half)] * 4, (q[0, 0], f10, f30, f01))
+        q.update(zip([(n, *o) for o in group for n in range(HALVES)], res))
+
+    terms = []
+    for n in range(HALVES):
+        terms += reduced({key[1:]: value for key, value in q.items() if key[0] == n})
+    back = whole(finish_kernel, [shape(16, half)] * 4, terms)
     across = along_z(back[2], -2)
     back = [back[0], along_z(back[1], -1), across, along_z(back[3], -3)]
     near_mine, near_theirs, far_mine, far_theirs = whole(cores_kernel, [shape(16, half)] * 4, back)
-    mixed, grad_tokens, grad_gates = whole(
-        functools.partial(tail_kernel, half),
-        [shape(tok, width), shape(tok, width), shape(2, tok, F32)],
-        (ids_t, gates_t, tokens, grad_mixed, near_mine, other_core(near_theirs), other_y(far_mine), other_y_core(far_theirs)),
-    )
+    outs = [shape(tok, width), shape(tok, width)]
+    scratch = [pltpu.VMEM((tok, half), BF), pltpu.VMEM((tok, half), BF), pltpu.SemaphoreType.DMA((2,))]
+    rest = (ids_t, gates_t, tokens, grad_mixed)
+    mixed, grad_tokens, inner = pl.pallas_call(
+        functools.partial(tail_kernel, half, False),
+        out_shape=outs + [shape(16, 128, F32)],
+        in_specs=[VMEM] * 6,
+        out_specs=[HBM, HBM, VMEM],
+        scratch_shapes=scratch,
+        compiler_params=pltpu.CompilerParams(vmem_limit_bytes=LIMIT),
+    )(*rest, near_mine, other_y(far_mine))
+    mixed, grad_tokens, grad_gates = pl.pallas_call(
+        functools.partial(tail_kernel, half, True),
+        out_shape=outs + [shape(2, tok, F32)],
+        in_specs=[VMEM] * 7 + [HBM, HBM],
+        out_specs=[HBM, HBM, VMEM],
+        input_output_aliases={7: 0, 8: 1},
+        scratch_shapes=scratch,
+        compiler_params=pltpu.CompilerParams(vmem_limit_bytes=LIMIT),
+    )(*rest, other_core(near_theirs), other_y_core(far_theirs), inner, mixed, grad_tokens)
     return mixed, grad_tokens, grad_gates.T
 
 

time: 138 us -> 132 us (0.957)
  waiting for transfers between devices: 63.2 us -> 48.5 us
  starting transfers between devices: 47.5 us -> 54.7 us
  Pallas kernels: 17.6 us -> 23.8 us
  local copies, waits for them, and re-layouts: 8.61 us -> 2.97 us
    ppermute x10 -> x20, waiting for transfers between devices: 36.3 us -> 19.6 us  [along_x(): return lax.ppermute(value, ('dp', 'expert'), pairs)]
    unnamed x24 -> x16, local copies, waits for them, and re-layouts: 8.61 us -> 2.97 us
    pallas_call x0 -> x2, Pallas kernels: none -> 4.62 us  [the longest x1 2.65 us: shards(): pl.pallas_call(functools.partial(tail_kernel, half, True), out_shape=outs...]
    ppermute x19 -> x23, starting transfers between devices: 32.6 us -> 36.9 us  [over_expert(): return lax.ppermute(value, 'expert', pairs)]
    ppermute x10 -> x20, starting transfers between devices: 14.9 us -> 17.9 us  [along_x(): return lax.ppermute(value, ('dp', 'expert'), pairs)]
    ppermute x19 -> x23, waiting for transfers between devices: 27 us -> 28.9 us  [over_expert(): return lax.ppermute(value, 'expert', pairs)]
    pallas_call x12 -> x10, Pallas kernels: 17.6 us -> 19.2 us  [whole(): pl.pallas_call(kernel, out_shape=outs, in_specs=specs or [VMEM] * len(arg...]
  transfers between devices with their start and end apart: 29 -> 43, of which waited for: 18 -> 21; matrix products, arithmetic and copies ran while one was open for 0% -> 0% of each run, Pallas kernels for 6% -> 8%
where the time goes in v3:
time: 132 us; the launch traced here: 131 us
  starting transfers between devices  54.7 us (41%)
  waiting for transfers between devices  48.5 us (37%)
  Pallas kernels  23.8 us (18%)
  local copies, waits for them, and re-layouts  2.97 us (2%)
    ppermute x23, starting transfers between devices, over_expert(): return lax.ppermute(value, 'expert', pairs)  36.9 us
    ppermute x23, waiting for transfers between devices, over_expert(): return lax.ppermute(value, 'expert', pairs)  28.9 us
    ppermute x20, waiting for transfers between devices, along_x(): return lax.ppermute(value, ('dp', 'expert'), pairs)  19.6 us
    pallas_call x10, Pallas kernels, whole(): pl.pallas_call(kernel, out_shape=outs, in_specs=specs or [VMEM] * len(arg...  19.2 us
    ppermute x20, starting transfers between devices, along_x(): return lax.ppermute(value, ('dp', 'expert'), pairs)  17.9 us
    unnamed x16, local copies, waits for them, and re-layouts  2.97 us
    pallas_call x1, Pallas kernels, shards(): pl.pallas_call(functools.partial(tail_kernel, half, True), out_shape=outs...  2.65 us
  transfers between devices with their start and end apart: 43, of which 21 were waited for; matrix products, arithmetic and copies ran while one was open for 0% of the time, Pallas kernels for 8%

profile of v3, /device:TPU:1, one launch (start us, length us, event | category | flops | bytes accessed | tf_op | source)
XLA Modules:
  0.0 131.4 jit_solution(13144450272834465318)
XLA Ops:
  0.7 7.1 %shard_map.94 = (bf16[16,3584]{1,0:T(8,128)(2,1)}, bf16[16,3584]{1,0:T(8,128)(2,1)}, bf16[16,3584]{1,0:T(8,128)(2,1)}, bf16[16,3584]{1,0:T(8,128)(2,1)}, bf16[10752,256]{1,0:T(8,128)(2,1)}) custom-call(s32[2,128]{1,0:T(2,128)} %bitcast.3, f32[2,128]{1,0:T(2,128)} %bitcast.6, bf16[128,7168]{1,0:T(8,128)(2,1)} %tok_ref.3, bf16[128,7168]{1,0:T(8,128)(2,1)} %grad_ref.3, ...), custom_call_target="tpu_custom_call" | custom-call | tf_op jit(solution)/shard_map/pallas_call | solution.py:340
  9.4 2.8 %collective-permute-start.1 = (bf16[16,3584]{1,0:T(8,128)(2,1)}, bf16[16,3584]{1,0:T(8,128)(2,1)S(1)}, u32[]{:S(2)}, u32[]{:S(2)}) collective-permute-start(bf16[16,3584]{1,0:T(8,128)(2,1)} %get-tuple-element.58), channel_id=1, source_target_pairs={{0,6},{1,7},{2,4},{3,5},{4,2},{5,3},{6,0},{7,1},{8,14},{9,15},{10,... | collective-permute-start | bytes 344072 | tf_op jit(solution)/shard_map/ppermute | solution.py:36
  12.7 5.7 %collective-permute-done.near_got = bf16[16,3584]{1,0:T(8,128)(2,1)S(1)} collective-permute-done((bf16[16,3584]{1,0:T(8,128)(2,1)}, bf16[16,3584]{1,0:T(8,128)(2,1)S(1)}, u32[]{:S(2)}, u32[]{:S(2)}) %collective-permute-start) | collective-permute-done | bytes 114720 | tf_op jit(solution)/shard_map/ppermute | solution.py:36
  22.2 3.3 %collective-permute-start.4 = (bf16[16,3584]{1,0:T(8,128)(2,1)S(1)}, bf16[16,3584]{1,0:T(8,128)(2,1)S(1)}, u32[]{:S(2)}, u32[]{:S(2)}) collective-permute-start(bf16[16,3584]{1,0:T(8,128)(2,1)S(1)} %get-tuple-element.62), channel_id=1, source_target_pairs={{0,16},{1,17},{2,18},{3,19},{4,20},{5,21},{6,22},{7,23},{8,24},{9,... | collective-permute-start | bytes 344072 | tf_op jit(solution)/shard_map/ppermute | solution.py:36
  27.5 3.3 %collective-permute-done.4.m2 = bf16[16,3584]{1,0:T(8,128)(2,1)S(1)} collective-permute-done((bf16[16,3584]{1,0:T(8,128)(2,1)S(1)}, bf16[16,3584]{1,0:T(8,128)(2,1)S(1)}, u32[]{:S(2)}, u32[]{:S(2)}) %collective-permute-start.4) | collective-permute-done | bytes 114720 | tf_op jit(solution)/shard_map/ppermute | solution.py:36
  34.1 2.8 %collective-permute-done.6.refs_6_ = bf16[64,1792]{1,0:T(8,128)(2,1)S(1)} collective-permute-done((bf16[64,1792]{1,0:T(8,128)(2,1)S(1)}, bf16[64,1792]{1,0:T(8,128)(2,1)S(1)}, u32[]{:S(2)}, u32[]{:S(2)}) %collective-permute-start.6) | collective-permute-done | bytes 229408 | tf_op jit(solution)/shard_map/ppermute | solution.py:36
  40.7 3.9 %collective-permute-done.11.refs_5_ = bf16[64,1792]{1,0:T(8,128)(2,1)S(1)} collective-permute-done((bf16[64,1792]{1,0:T(8,128)(2,1)S(1)}, bf16[64,1792]{1,0:T(8,128)(2,1)S(1)}, u32[]{:S(2)}, u32[]{:S(2)}) %collective-permute-start.11) | collective-permute-done | bytes 229408 | tf_op jit(solution)/shard_map/ppermute | solution.py:65
  48.7 3.2 %collective-permute-done.17.refs_4_ = bf16[64,1792]{1,0:T(8,128)(2,1)S(1)} collective-permute-done((bf16[64,1792]{1,0:T(8,128)(2,1)S(1)}, bf16[64,1792]{1,0:T(8,128)(2,1)S(1)}, u32[]{:S(2)}, u32[]{:S(2)}) %collective-permute-start.17) | collective-permute-done | bytes 229408 | tf_op jit(solution)/shard_map/ppermute | solution.py:65
  58.0 2.2 %shard_map.98.refs_0_ = f32[128,1536]{1,0:T(8,128)S(1)} custom-call(bf16[64,1792]{1,0:T(8,128)(2,1)S(1)} %get-tuple-element.64.refs_0_, bf16[64,1792]{1,0:T(8,128)(2,1)S(1)} %get-tuple-element.66.refs_1_, bf16[64,1792]{1,0:T(8,128)(2,1)S(1)} %collective-permute-done.7.refs_2_, bf16[64,1792]{1,0:T(8,128)(2,1)S(1)} %collective-permute-done.10.refs_3_, ...), custom_call_target="tpu_custom_call" | custom-call | tf_op jit(solution)/shard_map/pallas_call | solution.py:340
  60.3 5.6 %collective-permute-start.21 = (f32[128,1536]{1,0:T(8,128)S(1)}, f32[128,1536]{1,0:T(8,128)S(1)}, u32[]{:S(2)}, u32[]{:S(2)}) collective-permute-start(f32[128,1536]{1,0:T(8,128)S(1)} %shard_map.98.refs_0_), channel_id=1, source_target_pairs={{0,1},{1,0},{2,3},{3,2},{4,5},{5,4},{6,7},{7,6},{8,9},{9,8},{10,11... | collective-permute-start | bytes 2359304 | tf_op jit(solution)/shard_map/ppermute | solution.py:36
  65.9 2.2 %shard_map.99.refs_1_ = f32[128,1536]{1,0:T(8,128)S(1)} custom-call(bf16[64,1792]{1,0:T(8,128)(2,1)S(1)} %collective-permute-done.13.refs_0_, bf16[64,1792]{1,0:T(8,128)(2,1)S(1)} %collective-permute-done.14.refs_1_, bf16[64,1792]{1,0:T(8,128)(2,1)S(1)} %collective-permute-done.15.refs_2_, bf16[64,1792]{1,0:T(8,128)(2,1)S(1)} %collective-permute-done.16.refs_3_, ...), custom_call_target="tpu_custom_call" | custom-call | tf_op jit(solution)/shard_map/pallas_call | solution.py:340
  68.2 2.2 %collective-permute-done.22.refs_3_ = f32[128,1536]{1,0:T(8,128)S(1)} collective-permute-done((f32[128,1536]{1,0:T(8,128)S(1)}, f32[128,1536]{1,0:T(8,128)S(1)}, u32[]{:S(2)}, u32[]{:S(2)}) %collective-permute-start.22) | collective-permute-done | bytes 786464 | tf_op jit(solution)/shard_map/ppermute | solution.py:36
  70.5 3.1 %shard_map.101 = (bf16[64,1792]{1,0:T(8,128)(2,1)S(1)}, bf16[64,1792]{1,0:T(8,128)(2,1)S(1)}, bf16[64,1792]{1,0:T(8,128)(2,1)S(1)}, bf16[64,1792]{1,0:T(8,128)(2...) custom-call(f32[128,1536]{1,0:T(8,128)S(1)} %shard_map.98.refs_0_, ...), custom_call_target="tpu_custom_call" | custom-call | tf_op jit(solution)/shard_map/pallas_call | solution.py:340
  75.2 2.5 %collective-permute-start.30 = (bf16[64,1792]{1,0:T(8,128)(2,1)S(1)}, bf16[64,1792]{1,0:T(8,128)(2,1)S(1)}, u32[]{:S(2)}, u32[]{:S(2)}) collective-permute-start(bf16[64,1792]{1,0:T(8,128)(2,1)S(1)} %get-tuple-element.87), channel_id=1, source_target_pairs={{0,32},{1,97},{2,34},{3,99},{4,36},{5,101},{6,38},{7,103},{8,40},{... | collective-permute-start | bytes 688136 | tf_op jit(solution)/shard_map/ppermute | solution.py:65
  77.8 3.1 %shard_map.100 = (bf16[64,1792]{1,0:T(8,128)(2,1)S(1)}, bf16[64,1792]{1,0:T(8,128)(2,1)S(1)}, bf16[64,1792]{1,0:T(8,128)(2,1)S(1)}, bf16[64,1792]{1,0:T(8,128)(2...) custom-call(f32[128,1536]{1,0:T(8,128)S(1)} %shard_map.98.refs_0_, ...), custom_call_target="tpu_custom_call" | custom-call | tf_op jit(solution)/shard_map/pallas_call | solution.py:340
  88.1 2.7 %collective-permute-start.31 = (bf16[64,1792]{1,0:T(8,128)(2,1)S(1)}, bf16[64,1792]{1,0:T(8,128)(2,1)S(1)}, u32[]{:S(2)}, u32[]{:S(2)}) collective-permute-start(bf16[64,1792]{1,0:T(8,128)(2,1)S(1)} %get-tuple-element.88), channel_id=1, source_target_pairs={{0,32},{1,97},{2,34},{3,99},{4,36},{5,101},{6,38},{7,103},{8,40},{... | collective-permute-start | bytes 688136 | tf_op jit(solution)/shard_map/ppermute | solution.py:65
  91.1 5.2 %collective-permute-done.35 = bf16[64,1792]{1,0:T(8,128)(2,1)S(1)} collective-permute-done((bf16[64,1792]{1,0:T(8,128)(2,1)S(1)}, bf16[64,1792]{1,0:T(8,128)(2,1)S(1)}, u32[]{:S(2)}, u32[]{:S(2)}) %collective-permute-start.35) | collective-permute-done | bytes 229408 | tf_op jit(solution)/shard_map/ppermute | solution.py:65
  97.9 2.1 %collective-permute-done.31.refs_5_ = bf16[64,1792]{1,0:T(8,128)(2,1)S(1)} collective-permute-done((bf16[64,1792]{1,0:T(8,128)(2,1)S(1)}, bf16[64,1792]{1,0:T(8,128)(2,1)S(1)}, u32[]{:S(2)}, u32[]{:S(2)}) %collective-permute-start.31) | collective-permute-done | bytes 229408 | tf_op jit(solution)/shard_map/ppermute | solution.py:65
  101.4 2.5 %collective-permute-done.36.refs_7_ = bf16[64,1792]{1,0:T(8,128)(2,1)S(1)} collective-permute-done((bf16[64,1792]{1,0:T(8,128)(2,1)S(1)}, bf16[64,1792]{1,0:T(8,128)(2,1)S(1)}, u32[]{:S(2)}, u32[]{:S(2)}) %collective-permute-start.36) | collective-permute-done | bytes 229408 | tf_op jit(solution)/shard_map/ppermute | solution.py:36
  106.7 2.1 %collective-permute-done.37.refs_1_ = bf16[16,3584]{1,0:T(8,128)(2,1)S(1)} collective-permute-done((bf16[16,3584]{1,0:T(8,128)(2,1)S(1)}, bf16[16,3584]{1,0:T(8,128)(2,1)S(1)}, u32[]{:S(2)}, u32[]{:S(2)}) %collective-permute-start.37) | collective-permute-done | bytes 114720 | tf_op jit(solution)/shard_map/ppermute | solution.py:36
  108.8 2.3 %collective-permute-done.38.refs_2_ = bf16[16,3584]{1,0:T(8,128)(2,1)S(1)} collective-permute-done((bf16[16,3584]{1,0:T(8,128)(2,1)S(1)}, bf16[16,3584]{1,0:T(8,128)(2,1)S(1)}, u32[]{:S(2)}, u32[]{:S(2)}) %collective-permute-start.38) | collective-permute-done | bytes 114720 | tf_op jit(solution)/shard_map/ppermute | solution.py:36
  114.2 8.4 %collective-permute-start.40 = (bf16[16,3584]{1,0:T(8,128)(2,1)S(1)}, bf16[16,3584]{1,0:T(8,128)(2,1)S(1)}, u32[]{:S(2)}, u32[]{:S(2)}) collective-permute-start(bf16[16,3584]{1,0:T(8,128)(2,1)S(1)} %get-tuple-element.99), channel_id=1, source_target_pairs={{0,1},{1,0},{2,3},{3,2},{4,5},{5,4},{6,7},{7,6},{8,9},{9,8},{10,11... | collective-permute-start | bytes 344072 | tf_op jit(solution)/shard_map/ppermute | solution.py:36
  125.4 3.2 %collective-permute-done.41.far = bf16[16,3584]{1,0:T(8,128)(2,1)S(1)} collective-permute-done((bf16[16,3584]{1,0:T(8,128)(2,1)S(1)}, bf16[16,3584]{1,0:T(8,128)(2,1)S(1)}, u32[]{:S(2)}, u32[]{:S(2)}) %collective-permute-start.41) | collective-permute-done | bytes 114720 | tf_op jit(solution)/shard_map/ppermute | solution.py:36
  128.6 2.6 %shard_map.105 = (bf16[128,7168]{1,0:T(8,128)(2,1)}, bf16[128,7168]{1,0:T(8,128)(2,1)}, f32[2,128]{1,0:T(2,128)}) custom-call(s32[2,128]{1,0:T(2,128)S(1)} %bitcast.5, f32[2,128]{1,0:T(2,128)S(1)} %bitcast.8, bf16[128,7168]{1,0:T(8,128)(2,1)S(1)} %copy-done, bf16[128,7168]{1,0:T(8,128)(2,1)S(1)} %copy-done.1, ...), custom_call_target="tpu_custom_call", output_to_operand_aliasing={{0}: (7, {}), {1}: (8, {})} | custom-call | tf_op jit(solution)/shard_map/pallas_call | solution.py:475
  (96 shorter events, 46.3 us)
Async XLA Ops:
  7.8 47.5 %collective-permute-start.12 = (bf16[10752,256]{1,0:T(8,128)(2,1)}, bf16[10752,256]{1,0:T(8,128)(2,1)S(1)}, u32[]{:S(2)}, u32[]{:S(2)}) collective-permute-start(bf16[10752,256]{1,0:T(8,128)(2,1)} %get-tuple-element.74), channel_id=1, source_target_pairs={{0,1},{1,0},{2,3},{3,2},{4,5},{5,4},{6,7},{7,6},{8,9},{9,8},{10,11... | collective-permute-start | bytes 16515080 | tf_op jit(solution)/shard_map/ppermute | solution.py:36
  9.3 9.0 %collective-permute-start = (bf16[16,3584]{1,0:T(8,128)(2,1)}, bf16[16,3584]{1,0:T(8,128)(2,1)S(1)}, u32[]{:S(2)}, u32[]{:S(2)}) collective-permute-start(bf16[16,3584]{1,0:T(8,128)(2,1)} %get-tuple-element.57), channel_id=1, source_target_pairs={{0,1},{1,0},{2,3},{3,2},{4,5},{5,4},{6,7},{7,6},{8,9},{9,8},{10,11... | collective-permute-start | bytes 344072 | tf_op jit(solution)/shard_map/ppermute | solution.py:36
  9.4 8.9 %collective-permute-start.1 = (bf16[16,3584]{1,0:T(8,128)(2,1)}, bf16[16,3584]{1,0:T(8,128)(2,1)S(1)}, u32[]{:S(2)}, u32[]{:S(2)}) collective-permute-start(bf16[16,3584]{1,0:T(8,128)(2,1)} %get-tuple-element.58), channel_id=1, source_target_pairs={{0,6},{1,7},{2,4},{3,5},{4,2},{5,3},{6,0},{7,1},{8,14},{9,15},{10,... | collective-permute-start | bytes 344072 | tf_op jit(solution)/shard_map/ppermute | solution.py:36
  22.2 8.6 %collective-permute-start.4 = (bf16[16,3584]{1,0:T(8,128)(2,1)S(1)}, bf16[16,3584]{1,0:T(8,128)(2,1)S(1)}, u32[]{:S(2)}, u32[]{:S(2)}) collective-permute-start(bf16[16,3584]{1,0:T(8,128)(2,1)S(1)} %get-tuple-element.62), channel_id=1, source_target_pairs={{0,16},{1,17},{2,18},{3,19},{4,20},{5,21},{6,22},{7,23},{8,24},{9,... | collective-permute-start | bytes 344072 | tf_op jit(solution)/shard_map/ppermute | solution.py:36
  31.4 8.1 %collective-permute-start.8 = (bf16[64,1792]{1,0:T(8,128)(2,1)S(1)}, bf16[64,1792]{1,0:T(8,128)(2,1)S(1)}, u32[]{:S(2)}, u32[]{:S(2)}) collective-permute-start(bf16[64,1792]{1,0:T(8,128)(2,1)S(1)} %get-tuple-element.64.refs_0_), channel_id=1, source_target_pairs={{0,96},{1,33},{2,98},{3,35},{4,100},{5,37},{6,102},{7,39},{8,104},... | collective-permute-start | bytes 688136 | tf_op jit(solution)/shard_map/ppermute | solution.py:65
  40.0 8.6 %collective-permute-start.13 = (bf16[64,1792]{1,0:T(8,128)(2,1)S(1)}, bf16[64,1792]{1,0:T(8,128)(2,1)S(1)}, u32[]{:S(2)}, u32[]{:S(2)}) collective-permute-start(bf16[64,1792]{1,0:T(8,128)(2,1)S(1)} %collective-permute-done.6.refs_6_), channel_id=1, source_target_pairs={{0,96},{1,33},{2,98},{3,35},{4,100},{5,37},{6,102},{7,39},{8,104},... | collective-permute-start | bytes 688136 | tf_op jit(solution)/shard_map/ppermute | solution.py:65
  44.7 8.9 %collective-permute-start.14 = (bf16[64,1792]{1,0:T(8,128)(2,1)S(1)}, bf16[64,1792]{1,0:T(8,128)(2,1)S(1)}, u32[]{:S(2)}, u32[]{:S(2)}) collective-permute-start(bf16[64,1792]{1,0:T(8,128)(2,1)S(1)} %collective-permute-done.9.refs_7_), channel_id=1, source_target_pairs={{0,96},{1,33},{2,98},{3,35},{4,100},{5,37},{6,102},{7,39},{8,104},... | collective-permute-start | bytes 688136 | tf_op jit(solution)/shard_map/ppermute | solution.py:65
  46.1 14.2 %collective-permute-start.15 = (bf16[64,1792]{1,0:T(8,128)(2,1)S(1)}, bf16[64,1792]{1,0:T(8,128)(2,1)S(1)}, u32[]{:S(2)}, u32[]{:S(2)}) collective-permute-start(bf16[64,1792]{1,0:T(8,128)(2,1)S(1)} %collective-permute-done.7.refs_2_), channel_id=1, source_target_pairs={{0,2},{1,3},{2,0},{3,1},{4,6},{5,7},{6,4},{7,5},{8,10},{9,11},{10,... | collective-permute-start | bytes 688136 | tf_op jit(solution)/shard_map/ppermute | solution.py:36
  48.5 17.3 %collective-permute-start.18 = (bf16[64,1792]{1,0:T(8,128)(2,1)S(1)}, bf16[64,1792]{1,0:T(8,128)(2,1)S(1)}, u32[]{:S(2)}, u32[]{:S(2)}) collective-permute-start(bf16[64,1792]{1,0:T(8,128)(2,1)S(1)} %collective-permute-done.10.refs_3_), channel_id=1, source_target_pairs={{0,32},{1,97},{2,34},{3,99},{4,36},{5,101},{6,38},{7,103},{8,40},{... | collective-permute-start | bytes 688136 | tf_op jit(solution)/shard_map/ppermute | solution.py:65
  51.9 13.9 %collective-permute-start.19 = (bf16[64,1792]{1,0:T(8,128)(2,1)S(1)}, bf16[64,1792]{1,0:T(8,128)(2,1)S(1)}, u32[]{:S(2)}, u32[]{:S(2)}) collective-permute-start(bf16[64,1792]{1,0:T(8,128)(2,1)S(1)} %collective-permute-done.13.refs_0_), channel_id=1, source_target_pairs={{0,96},{1,33},{2,98},{3,35},{4,100},{5,37},{6,102},{7,39},{8,104},... | collective-permute-start | bytes 688136 | tf_op jit(solution)/shard_map/ppermute | solution.py:65
  53.6 12.3 %collective-permute-start.16 = (bf16[64,1792]{1,0:T(8,128)(2,1)S(1)}, bf16[64,1792]{1,0:T(8,128)(2,1)S(1)}, u32[]{:S(2)}, u32[]{:S(2)}) collective-permute-start(bf16[64,1792]{1,0:T(8,128)(2,1)S(1)} %collective-permute-done.10.refs_3_), channel_id=1, source_target_pairs={{0,2},{1,3},{2,0},{3,1},{4,6},{5,7},{6,4},{7,5},{8,10},{9,11},{10,... | collective-permute-start | bytes 688136 | tf_op jit(solution)/shard_map/ppermute | solution.py:36
  55.3 10.6 %collective-permute-start.20 = (bf16[64,1792]{1,0:T(8,128)(2,1)S(1)}, bf16[64,1792]{1,0:T(8,128)(2,1)S(1)}, u32[]{:S(2)}, u32[]{:S(2)}) collective-permute-start(bf16[64,1792]{1,0:T(8,128)(2,1)S(1)} %collective-permute-done.14.refs_1_), channel_id=1, source_target_pairs={{0,96},{1,33},{2,98},{3,35},{4,100},{5,37},{6,102},{7,39},{8,104},... | collective-permute-start | bytes 688136 | tf_op jit(solution)/shard_map/ppermute | solution.py:65
  60.3 8.0 %collective-permute-start.21 = (f32[128,1536]{1,0:T(8,128)S(1)}, f32[128,1536]{1,0:T(8,128)S(1)}, u32[]{:S(2)}, u32[]{:S(2)}) collective-permute-start(f32[128,1536]{1,0:T(8,128)S(1)} %shard_map.98.refs_0_), channel_id=1, source_target_pairs={{0,1},{1,0},{2,3},{3,2},{4,5},{5,4},{6,7},{7,6},{8,9},{9,8},{10,11... | collective-permute-start | bytes 2359304 | tf_op jit(solution)/shard_map/ppermute | solution.py:36
  74.9 8.8 %collective-permute-start.25 = (bf16[64,1792]{1,0:T(8,128)(2,1)S(1)}, bf16[64,1792]{1,0:T(8,128)(2,1)S(1)}, u32[]{:S(2)}, u32[]{:S(2)}) collective-permute-start(bf16[64,1792]{1,0:T(8,128)(2,1)S(1)} %get-tuple-element.80), channel_id=1, source_target_pairs={{0,96},{1,33},{2,98},{3,35},{4,100},{5,37},{6,102},{7,39},{8,104},... | collective-permute-start | bytes 688136 | tf_op jit(solution)/shard_map/ppermute | solution.py:65
  75.1 10.0 %collective-permute-start.26 = (bf16[64,1792]{1,0:T(8,128)(2,1)S(1)}, bf16[64,1792]{1,0:T(8,128)(2,1)S(1)}, u32[]{:S(2)}, u32[]{:S(2)}) collective-permute-start(bf16[64,1792]{1,0:T(8,128)(2,1)S(1)} %get-tuple-element.81), channel_id=1, source_target_pairs={{0,2},{1,3},{2,0},{3,1},{4,6},{5,7},{6,4},{7,5},{8,10},{9,11},{10,... | collective-permute-start | bytes 688136 | tf_op jit(solution)/shard_map/ppermute | solution.py:36
  75.2 10.0 %collective-permute-start.30 = (bf16[64,1792]{1,0:T(8,128)(2,1)S(1)}, bf16[64,1792]{1,0:T(8,128)(2,1)S(1)}, u32[]{:S(2)}, u32[]{:S(2)}) collective-permute-start(bf16[64,1792]{1,0:T(8,128)(2,1)S(1)} %get-tuple-element.87), channel_id=1, source_target_pairs={{0,32},{1,97},{2,34},{3,99},{4,36},{5,101},{6,38},{7,103},{8,40},{... | collective-permute-start | bytes 688136 | tf_op jit(solution)/shard_map/ppermute | solution.py:65
  77.8 9.9 %collective-permute-start.32 = (bf16[64,1792]{1,0:T(8,128)(2,1)S(1)}, bf16[64,1792]{1,0:T(8,128)(2,1)S(1)}, u32[]{:S(2)}, u32[]{:S(2)}) collective-permute-start(bf16[64,1792]{1,0:T(8,128)(2,1)S(1)} %get-tuple-element.90), channel_id=1, source_target_pairs={{0,96},{1,33},{2,98},{3,35},{4,100},{5,37},{6,102},{7,39},{8,104},... | collective-permute-start | bytes 688136 | tf_op jit(solution)/shard_map/ppermute | solution.py:65
  85.1 11.2 %collective-permute-start.24 = (bf16[64,1792]{1,0:T(8,128)(2,1)S(1)}, bf16[64,1792]{1,0:T(8,128)(2,1)S(1)}, u32[]{:S(2)}, u32[]{:S(2)}) collective-permute-start(bf16[64,1792]{1,0:T(8,128)(2,1)S(1)} %get-tuple-element.78), channel_id=1, source_target_pairs={{0,32},{1,97},{2,34},{3,99},{4,36},{5,101},{6,38},{7,103},{8,40},{... | collective-permute-start | bytes 688136 | tf_op jit(solution)/shard_map/ppermute | solution.py:65
  85.3 12.6 %collective-permute-start.27 = (bf16[64,1792]{1,0:T(8,128)(2,1)S(1)}, bf16[64,1792]{1,0:T(8,128)(2,1)S(1)}, u32[]{:S(2)}, u32[]{:S(2)}) collective-permute-start(bf16[64,1792]{1,0:T(8,128)(2,1)S(1)} %add_convert_fusion.5), channel_id=1, source_target_pairs={{0,96},{1,33},{2,98},{3,35},{4,100},{5,37},{6,102},{7,39},{8,104},... | collective-permute-start | bytes 688136 | tf_op jit(solution)/shard_map/ppermute | solution.py:65
  87.6 8.6 %collective-permute-start.35 = (bf16[64,1792]{1,0:T(8,128)(2,1)S(1)}, bf16[64,1792]{1,0:T(8,128)(2,1)S(1)}, u32[]{:S(2)}, u32[]{:S(2)}) collective-permute-start(bf16[64,1792]{1,0:T(8,128)(2,1)S(1)} %add_convert_fusion.1), channel_id=1, source_target_pairs={{0,32},{1,97},{2,34},{3,99},{4,36},{5,101},{6,38},{7,103},{8,40},{... | collective-permute-start | bytes 688136 | tf_op jit(solution)/shard_map/ppermute | solution.py:65
  88.1 11.8 %collective-permute-start.31 = (bf16[64,1792]{1,0:T(8,128)(2,1)S(1)}, bf16[64,1792]{1,0:T(8,128)(2,1)S(1)}, u32[]{:S(2)}, u32[]{:S(2)}) collective-permute-start(bf16[64,1792]{1,0:T(8,128)(2,1)S(1)} %get-tuple-element.88), channel_id=1, source_target_pairs={{0,32},{1,97},{2,34},{3,99},{4,36},{5,101},{6,38},{7,103},{8,40},{... | collective-permute-start | bytes 688136 | tf_op jit(solution)/shard_map/ppermute | solution.py:65
  90.9 9.1 %collective-permute-start.34 = (bf16[64,1792]{1,0:T(8,128)(2,1)S(1)}, bf16[64,1792]{1,0:T(8,128)(2,1)S(1)}, u32[]{:S(2)}, u32[]{:S(2)}) collective-permute-start(bf16[64,1792]{1,0:T(8,128)(2,1)S(1)} %add_convert_fusion.2), channel_id=1, source_target_pairs={{0,96},{1,33},{2,98},{3,35},{4,100},{5,37},{6,102},{7,39},{8,104},... | collective-permute-start | bytes 688136 | tf_op jit(solution)/shard_map/ppermute | solution.py:65
  112.4 11.0 %collective-permute-start.42 = (bf16[16,3584]{1,0:T(8,128)(2,1)S(1)}, bf16[16,3584]{1,0:T(8,128)(2,1)S(1)}, u32[]{:S(2)}, u32[]{:S(2)}) collective-permute-start(bf16[16,3584]{1,0:T(8,128)(2,1)S(1)} %get-tuple-element.102), channel_id=1, source_target_pairs={{0,6},{1,7},{2,4},{3,5},{4,2},{5,3},{6,0},{7,1},{8,14},{9,15},{10,... | collective-permute-start | bytes 344072 | tf_op jit(solution)/shard_map/ppermute | solution.py:36
  114.2 11.2 %collective-permute-start.40 = (bf16[16,3584]{1,0:T(8,128)(2,1)S(1)}, bf16[16,3584]{1,0:T(8,128)(2,1)S(1)}, u32[]{:S(2)}, u32[]{:S(2)}) collective-permute-start(bf16[16,3584]{1,0:T(8,128)(2,1)S(1)} %get-tuple-element.99), channel_id=1, source_target_pairs={{0,1},{1,0},{2,3},{3,2},{4,5},{5,4},{6,7},{7,6},{8,9},{9,8},{10,11... | collective-permute-start | bytes 344072 | tf_op jit(solution)/shard_map/ppermute | solution.py:36
  (27 other events, 400.8 us)

commit v4 on v3

--- a/solution.py
+++ b/solution.py
@@ -12,7 +12,7 @@
 VMEM = pl.BlockSpec(memory_space=pltpu.VMEM)
 HBM = pl.BlockSpec(memory_space=pltpu.HBM)
 LIMIT = 16 * 1024 * 1024
-BIG = 54 * 1024 * 1024
+BIG = 52 * 1024 * 1024
 NZ = 4
 HALVES = 2
 
@@ -385,11 +385,11 @@
     f21 = along_x(q[2, 1], 1)
     f20 = along_x(q[2, 0], -1)
     f31 = other_l(q[3, 1])
-    q10, f21 = lax.optimization_barrier((q[1, 0], f21))
-    f10 = along_x(q10, 1)
     f11 = along_x(add(q[1, 1], f21), 1)
     f30 = along_x(add(q[3, 0], f20, f31), -1)
+    q10, f11 = lax.optimization_barrier((q[1, 0], f11))
     f01 = other_l(add(q[0, 1], f11))
+    f10 = along_x(q10, 1)
     return [q[0, 0], f10, f30, f01]
 
 
@@ -401,7 +401,7 @@
 
     near_own, far_own, near_other, far_other, w_send = whole(
         functools.partial(dispatch_kernel, half),
-        [shape(16, half)] * 4 + [shape(3 * half, w_gate.shape[2])],
+        [pltpu.VMEM((16, half), BF)] * 4 + [pltpu.VMEM((3 * half, w_gate.shape[2]), BF)],
         (ids_t, gates_t, tokens, grad_mixed, w_gate, w_up, w_down),
         [
             pltpu.VMEM((2, tok), jnp.int32),

time: 132 us -> 126 us (0.955)
  starting transfers between devices: 54.7 us -> 51.4 us
  Pallas kernels: 23.8 us -> 21.1 us
    ppermute x23, waiting for transfers between devices: 28.9 us -> 25.4 us  [over_expert(): return lax.ppermute(value, 'expert', pairs)]
    ppermute x20, waiting for transfers between devices: 19.6 us -> 22.4 us  [along_x(): return lax.ppermute(value, ('dp', 'expert'), pairs)]
    pallas_call x10, Pallas kernels: 19.2 us -> 16.5 us  [whole(): pl.pallas_call(kernel, out_shape=outs, in_specs=specs or [VMEM] * len(arg...]
    ppermute x23, starting transfers between devices: 36.9 us -> 34.6 us  [over_expert(): return lax.ppermute(value, 'expert', pairs)]
    unnamed x16 -> x14, local copies, waits for them, and re-layouts: 2.97 us -> 4.1 us
  transfers between devices with their start and end apart: 43 -> 43, of which waited for: 21 -> 25; matrix products, arithmetic and copies ran while one was open for 0% -> 0% of each run, Pallas kernels for 8% -> 8%
where the time goes in v4:
time: 126 us
  starting transfers between devices  51.4 us (41%)
  waiting for transfers between devices  47.8 us (38%)
  Pallas kernels  21.1 us (17%)
  local copies, waits for them, and re-layouts  4.1 us (3%)
    ppermute x23, starting transfers between devices, over_expert(): return lax.ppermute(value, 'expert', pairs)  34.6 us
    ppermute x23, waiting for transfers between devices, over_expert(): return lax.ppermute(value, 'expert', pairs)  25.4 us
    ppermute x20, waiting for transfers between devices, along_x(): return lax.ppermute(value, ('dp', 'expert'), pairs)  22.4 us
    ppermute x20, starting transfers between devices, along_x(): return lax.ppermute(value, ('dp', 'expert'), pairs)  16.8 us
    pallas_call x10, Pallas kernels, whole(): pl.pallas_call(kernel, out_shape=outs, in_specs=specs or [VMEM] * len(arg...  16.5 us
    unnamed x14, local copies, waits for them, and re-layouts  4.1 us
    pallas_call x1, Pallas kernels, shards(): pl.pallas_call(functools.partial(tail_kernel, half, True), out_shape=outs...  2.64 us
  transfers between devices with their start and end apart: 43, of which 25 were waited for; matrix products, arithmetic and copies ran while one was open for 0% of the time, Pallas kernels for 8%

profile of v4, /device:TPU:1, one launch (start us, length us, event | category | flops | bytes accessed | tf_op | source)
XLA Modules:
  0.0 125.9 jit_solution(13614908082994011814)
XLA Ops:
  0.6 4.5 %shard_map.94 = (bf16[16,3584]{1,0:T(8,128)(2,1)S(1)}, bf16[16,3584]{1,0:T(8,128)(2,1)S(1)}, bf16[16,3584]{1,0:T(8,128)(2,1)S(1)}, bf16[16,3584]{1,0:T(8,128)(2,1)S(1)}, bf16[10752,256]{1,0:T(8,128)(2,1)S(1)}) custom-call(s32[2,128]{1,0:T(2,128)} %bitcast.3, f32[2,128]{1,0:T(2,128)} %bitcast.6, bf16[128,7168]{1,0:T(8,128)(2,1)} %tok_ref.3, ...), custom_call_target="tpu_custom_call" | custom-call | tf_op jit(solution)/shard_map/pallas_call | solution.py:340
  6.7 2.8 %collective-permute-start.1 = (bf16[16,3584]{1,0:T(8,128)(2,1)S(1)}, bf16[16,3584]{1,0:T(8,128)(2,1)S(1)}, u32[]{:S(2)}, u32[]{:S(2)}) collective-permute-start(bf16[16,3584]{1,0:T(8,128)(2,1)S(1)} %get-tuple-element.58), channel_id=1, source_target_pairs={{0,6},{1,7},{2,4},{3,5},{4,2},{5,3},{6,0},{7,1},{8,14},{9,15},{10,... | collective-permute-start | bytes 344072 | tf_op jit(solution)/shard_map/ppermute | solution.py:36
  10.0 5.5 %collective-permute-done.near_got = bf16[16,3584]{1,0:T(8,128)(2,1)S(1)} collective-permute-done((bf16[16,3584]{1,0:T(8,128)(2,1)S(1)}, bf16[16,3584]{1,0:T(8,128)(2,1)S(1)}, u32[]{:S(2)}, u32[]{:S(2)}) %collective-permute-start) | collective-permute-done | bytes 114720 | tf_op jit(solution)/shard_map/ppermute | solution.py:36
  18.4 3.3 %collective-permute-start.4 = (bf16[16,3584]{1,0:T(8,128)(2,1)S(1)}, bf16[16,3584]{1,0:T(8,128)(2,1)S(1)}, u32[]{:S(2)}, u32[]{:S(2)}) collective-permute-start(bf16[16,3584]{1,0:T(8,128)(2,1)S(1)} %get-tuple-element.62), channel_id=1, source_target_pairs={{0,16},{1,17},{2,18},{3,19},{4,20},{5,21},{6,22},{7,23},{8,24},{9,... | collective-permute-start | bytes 344072 | tf_op jit(solution)/shard_map/ppermute | solution.py:36
  23.8 3.3 %collective-permute-done.4.m2 = bf16[16,3584]{1,0:T(8,128)(2,1)S(1)} collective-permute-done((bf16[16,3584]{1,0:T(8,128)(2,1)S(1)}, bf16[16,3584]{1,0:T(8,128)(2,1)S(1)}, u32[]{:S(2)}, u32[]{:S(2)}) %collective-permute-start.4) | collective-permute-done | bytes 114720 | tf_op jit(solution)/shard_map/ppermute | solution.py:36
  30.3 2.8 %collective-permute-done.6.refs_6_ = bf16[64,1792]{1,0:T(8,128)(2,1)S(1)} collective-permute-done((bf16[64,1792]{1,0:T(8,128)(2,1)S(1)}, bf16[64,1792]{1,0:T(8,128)(2,1)S(1)}, u32[]{:S(2)}, u32[]{:S(2)}) %collective-permute-start.6) | collective-permute-done | bytes 229408 | tf_op jit(solution)/shard_map/ppermute | solution.py:36
  36.9 3.9 %collective-permute-done.11.refs_5_ = bf16[64,1792]{1,0:T(8,128)(2,1)S(1)} collective-permute-done((bf16[64,1792]{1,0:T(8,128)(2,1)S(1)}, bf16[64,1792]{1,0:T(8,128)(2,1)S(1)}, u32[]{:S(2)}, u32[]{:S(2)}) %collective-permute-start.11) | collective-permute-done | bytes 229408 | tf_op jit(solution)/shard_map/ppermute | solution.py:65
  44.9 3.2 %collective-permute-done.17.refs_4_ = bf16[64,1792]{1,0:T(8,128)(2,1)S(1)} collective-permute-done((bf16[64,1792]{1,0:T(8,128)(2,1)S(1)}, bf16[64,1792]{1,0:T(8,128)(2,1)S(1)}, u32[]{:S(2)}, u32[]{:S(2)}) %collective-permute-start.17) | collective-permute-done | bytes 229408 | tf_op jit(solution)/shard_map/ppermute | solution.py:65
  51.5 2.0 %copy-done.3 = bf16[1,7168,256]{2,1,0:T(8,128)(2,1)S(1)} copy-done((bf16[1,7168,256]{2,1,0:T(8,128)(2,1)S(1)}, bf16[1,7168,256]{2,1,0:T(8,128)(2,1)}, u32[]{:S(2)}) %copy-start.3) | copy-done | bytes 3670040
  53.5 2.0 %copy-done.4 = bf16[1,256,7168]{2,1,0:T(8,128)(2,1)S(1)} copy-done((bf16[1,256,7168]{2,1,0:T(8,128)(2,1)S(1)}, bf16[1,256,7168]{2,1,0:T(8,128)(2,1)}, u32[]{:S(2)}) %copy-start.4) | copy-done | bytes 3670040
  56.3 2.2 %shard_map.98.refs_0_ = f32[128,1536]{1,0:T(8,128)S(1)} custom-call(bf16[64,1792]{1,0:T(8,128)(2,1)S(1)} %get-tuple-element.64.refs_0_, bf16[64,1792]{1,0:T(8,128)(2,1)S(1)} %get-tuple-element.66.refs_1_, bf16[64,1792]{1,0:T(8,128)(2,1)S(1)} %collective-permute-done.7.refs_2_, bf16[64,1792]{1,0:T(8,128)(2,1)S(1)} %collective-permute-done.10.refs_3_, ...), custom_call_target="tpu_custom_call" | custom-call | tf_op jit(solution)/shard_map/pallas_call | solution.py:340
  58.5 5.6 %collective-permute-start.21 = (f32[128,1536]{1,0:T(8,128)S(1)}, f32[128,1536]{1,0:T(8,128)S(1)}, u32[]{:S(2)}, u32[]{:S(2)}) collective-permute-start(f32[128,1536]{1,0:T(8,128)S(1)} %shard_map.98.refs_0_), channel_id=1, source_target_pairs={{0,1},{1,0},{2,3},{3,2},{4,5},{5,4},{6,7},{7,6},{8,9},{9,8},{10,11... | collective-permute-start | bytes 2359304 | tf_op jit(solution)/shard_map/ppermute | solution.py:36
  64.1 2.2 %shard_map.99.refs_1_ = f32[128,1536]{1,0:T(8,128)S(1)} custom-call(bf16[64,1792]{1,0:T(8,128)(2,1)S(1)} %collective-permute-done.13.refs_0_, bf16[64,1792]{1,0:T(8,128)(2,1)S(1)} %collective-permute-done.14.refs_1_, bf16[64,1792]{1,0:T(8,128)(2,1)S(1)} %collective-permute-done.15.refs_2_, bf16[64,1792]{1,0:T(8,128)(2,1)S(1)} %collective-permute-done.16.refs_3_, ...), custom_call_target="tpu_custom_call" | custom-call | tf_op jit(solution)/shard_map/pallas_call | solution.py:340
  66.5 2.2 %collective-permute-done.22.refs_3_ = f32[128,1536]{1,0:T(8,128)S(1)} collective-permute-done((f32[128,1536]{1,0:T(8,128)S(1)}, f32[128,1536]{1,0:T(8,128)S(1)}, u32[]{:S(2)}, u32[]{:S(2)}) %collective-permute-start.22) | collective-permute-done | bytes 786464 | tf_op jit(solution)/shard_map/ppermute | solution.py:36
  68.7 3.1 %shard_map.101 = (bf16[64,1792]{1,0:T(8,128)(2,1)S(1)}, bf16[64,1792]{1,0:T(8,128)(2,1)S(1)}, bf16[64,1792]{1,0:T(8,128)(2,1)S(1)}, bf16[64,1792]{1,0:T(8,128)(2...) custom-call(f32[128,1536]{1,0:T(8,128)S(1)} %shard_map.98.refs_0_, ...), custom_call_target="tpu_custom_call" | custom-call | tf_op jit(solution)/shard_map/pallas_call | solution.py:340
  74.9 3.1 %shard_map.100 = (bf16[64,1792]{1,0:T(8,128)(2,1)S(1)}, bf16[64,1792]{1,0:T(8,128)(2,1)S(1)}, bf16[64,1792]{1,0:T(8,128)(2,1)S(1)}, bf16[64,1792]{1,0:T(8,128)(2...) custom-call(f32[128,1536]{1,0:T(8,128)S(1)} %shard_map.98.refs_0_, ...), custom_call_target="tpu_custom_call" | custom-call | tf_op jit(solution)/shard_map/pallas_call | solution.py:340
  89.2 2.2 %collective-permute-done.31 = bf16[64,1792]{1,0:T(8,128)(2,1)S(1)} collective-permute-done((bf16[64,1792]{1,0:T(8,128)(2,1)S(1)}, bf16[64,1792]{1,0:T(8,128)(2,1)S(1)}, u32[]{:S(2)}, u32[]{:S(2)}) %collective-permute-start.31) | collective-permute-done | bytes 229408 | tf_op jit(solution)/shard_map/ppermute | solution.py:65
  92.1 2.1 %collective-permute-done.35.refs_6_ = bf16[64,1792]{1,0:T(8,128)(2,1)S(1)} collective-permute-done((bf16[64,1792]{1,0:T(8,128)(2,1)S(1)}, bf16[64,1792]{1,0:T(8,128)(2,1)S(1)}, u32[]{:S(2)}, u32[]{:S(2)}) %collective-permute-start.35) | collective-permute-done | bytes 229408 | tf_op jit(solution)/shard_map/ppermute | solution.py:65
  96.7 2.4 %collective-permute-done.32.refs_5_ = bf16[64,1792]{1,0:T(8,128)(2,1)S(1)} collective-permute-done((bf16[64,1792]{1,0:T(8,128)(2,1)S(1)}, bf16[64,1792]{1,0:T(8,128)(2,1)S(1)}, u32[]{:S(2)}, u32[]{:S(2)}) %collective-permute-start.32) | collective-permute-done | bytes 229408 | tf_op jit(solution)/shard_map/ppermute | solution.py:65
  102.0 2.1 %collective-permute-done.37.refs_1_ = bf16[16,3584]{1,0:T(8,128)(2,1)S(1)} collective-permute-done((bf16[16,3584]{1,0:T(8,128)(2,1)S(1)}, bf16[16,3584]{1,0:T(8,128)(2,1)S(1)}, u32[]{:S(2)}, u32[]{:S(2)}) %collective-permute-start.37) | collective-permute-done | bytes 114720 | tf_op jit(solution)/shard_map/ppermute | solution.py:36
  104.1 2.3 %collective-permute-done.38.refs_2_ = bf16[16,3584]{1,0:T(8,128)(2,1)S(1)} collective-permute-done((bf16[16,3584]{1,0:T(8,128)(2,1)S(1)}, bf16[16,3584]{1,0:T(8,128)(2,1)S(1)}, u32[]{:S(2)}, u32[]{:S(2)}) %collective-permute-start.38) | collective-permute-done | bytes 114720 | tf_op jit(solution)/shard_map/ppermute | solution.py:36
  109.6 7.5 %collective-permute-start.40 = (bf16[16,3584]{1,0:T(8,128)(2,1)S(1)}, bf16[16,3584]{1,0:T(8,128)(2,1)S(1)}, u32[]{:S(2)}, u32[]{:S(2)}) collective-permute-start(bf16[16,3584]{1,0:T(8,128)(2,1)S(1)} %get-tuple-element.99), channel_id=1, source_target_pairs={{0,1},{1,0},{2,3},{3,2},{4,5},{5,4},{6,7},{7,6},{8,9},{9,8},{10,11... | collective-permute-start | bytes 344072 | tf_op jit(solution)/shard_map/ppermute | solution.py:36
  119.8 3.2 %collective-permute-done.41.far = bf16[16,3584]{1,0:T(8,128)(2,1)S(1)} collective-permute-done((bf16[16,3584]{1,0:T(8,128)(2,1)S(1)}, bf16[16,3584]{1,0:T(8,128)(2,1)S(1)}, u32[]{:S(2)}, u32[]{:S(2)}) %collective-permute-start.41) | collective-permute-done | bytes 114720 | tf_op jit(solution)/shard_map/ppermute | solution.py:36
  123.1 2.6 %shard_map.105 = (bf16[128,7168]{1,0:T(8,128)(2,1)}, bf16[128,7168]{1,0:T(8,128)(2,1)}, f32[2,128]{1,0:T(2,128)}) custom-call(s32[2,128]{1,0:T(2,128)S(1)} %bitcast.5, f32[2,128]{1,0:T(2,128)S(1)} %bitcast.8, bf16[128,7168]{1,0:T(8,128)(2,1)S(1)} %copy-done, bf16[128,7168]{1,0:T(8,128)(2,1)S(1)} %copy-done.1, ...), custom_call_target="tpu_custom_call", output_to_operand_aliasing={{0}: (7, {}), {1}: (8, {})} | custom-call | tf_op jit(solution)/shard_map/pallas_call | solution.py:475
  (94 shorter events, 48.7 us)
Async XLA Ops:
  5.1 46.4 %collective-permute-start.12 = (bf16[10752,256]{1,0:T(8,128)(2,1)S(1)}, bf16[10752,256]{1,0:T(8,128)(2,1)S(1)}, u32[]{:S(2)}, u32[]{:S(2)}) collective-permute-start(bf16[10752,256]{1,0:T(8,128)(2,1)S(1)} %get-tuple-element.74), channel_id=1, source_target_pairs={{0,1},{1,0},{2,3},{3,2},{4,5},{5,4},{6,7},{7,6},{8,9},{9,8},{10,11... | collective-permute-start | bytes 16515080 | tf_op jit(solution)/shard_map/ppermute | solution.py:36
  6.6 8.8 %collective-permute-start = (bf16[16,3584]{1,0:T(8,128)(2,1)S(1)}, bf16[16,3584]{1,0:T(8,128)(2,1)S(1)}, u32[]{:S(2)}, u32[]{:S(2)}) collective-permute-start(bf16[16,3584]{1,0:T(8,128)(2,1)S(1)} %get-tuple-element.57), channel_id=1, source_target_pairs={{0,1},{1,0},{2,3},{3,2},{4,5},{5,4},{6,7},{7,6},{8,9},{9,8},{10,11... | collective-permute-start | bytes 344072 | tf_op jit(solution)/shard_map/ppermute | solution.py:36
  6.7 8.7 %collective-permute-start.1 = (bf16[16,3584]{1,0:T(8,128)(2,1)S(1)}, bf16[16,3584]{1,0:T(8,128)(2,1)S(1)}, u32[]{:S(2)}, u32[]{:S(2)}) collective-permute-start(bf16[16,3584]{1,0:T(8,128)(2,1)S(1)} %get-tuple-element.58), channel_id=1, source_target_pairs={{0,6},{1,7},{2,4},{3,5},{4,2},{5,3},{6,0},{7,1},{8,14},{9,15},{10,... | collective-permute-start | bytes 344072 | tf_op jit(solution)/shard_map/ppermute | solution.py:36
  18.4 8.6 %collective-permute-start.4 = (bf16[16,3584]{1,0:T(8,128)(2,1)S(1)}, bf16[16,3584]{1,0:T(8,128)(2,1)S(1)}, u32[]{:S(2)}, u32[]{:S(2)}) collective-permute-start(bf16[16,3584]{1,0:T(8,128)(2,1)S(1)} %get-tuple-element.62), channel_id=1, source_target_pairs={{0,16},{1,17},{2,18},{3,19},{4,20},{5,21},{6,22},{7,23},{8,24},{9,... | collective-permute-start | bytes 344072 | tf_op jit(solution)/shard_map/ppermute | solution.py:36
  27.6 8.2 %collective-permute-start.8 = (bf16[64,1792]{1,0:T(8,128)(2,1)S(1)}, bf16[64,1792]{1,0:T(8,128)(2,1)S(1)}, u32[]{:S(2)}, u32[]{:S(2)}) collective-permute-start(bf16[64,1792]{1,0:T(8,128)(2,1)S(1)} %get-tuple-element.64.refs_0_), channel_id=1, source_target_pairs={{0,96},{1,33},{2,98},{3,35},{4,100},{5,37},{6,102},{7,39},{8,104},... | collective-permute-start | bytes 688136 | tf_op jit(solution)/shard_map/ppermute | solution.py:65
  33.1 7.8 %collective-permute-start.11 = (bf16[64,1792]{1,0:T(8,128)(2,1)S(1)}, bf16[64,1792]{1,0:T(8,128)(2,1)S(1)}, u32[]{:S(2)}, u32[]{:S(2)}) collective-permute-start(bf16[64,1792]{1,0:T(8,128)(2,1)S(1)} %get-tuple-element.66.refs_1_), channel_id=1, source_target_pairs={{0,96},{1,33},{2,98},{3,35},{4,100},{5,37},{6,102},{7,39},{8,104},... | collective-permute-start | bytes 688136 | tf_op jit(solution)/shard_map/ppermute | solution.py:65
  36.2 8.6 %collective-permute-start.13 = (bf16[64,1792]{1,0:T(8,128)(2,1)S(1)}, bf16[64,1792]{1,0:T(8,128)(2,1)S(1)}, u32[]{:S(2)}, u32[]{:S(2)}) collective-permute-start(bf16[64,1792]{1,0:T(8,128)(2,1)S(1)} %collective-permute-done.6.refs_6_), channel_id=1, source_target_pairs={{0,96},{1,33},{2,98},{3,35},{4,100},{5,37},{6,102},{7,39},{8,104},... | collective-permute-start | bytes 688136 | tf_op jit(solution)/shard_map/ppermute | solution.py:65
  40.9 8.9 %collective-permute-start.14 = (bf16[64,1792]{1,0:T(8,128)(2,1)S(1)}, bf16[64,1792]{1,0:T(8,128)(2,1)S(1)}, u32[]{:S(2)}, u32[]{:S(2)}) collective-permute-start(bf16[64,1792]{1,0:T(8,128)(2,1)S(1)} %collective-permute-done.9.refs_7_), channel_id=1, source_target_pairs={{0,96},{1,33},{2,98},{3,35},{4,100},{5,37},{6,102},{7,39},{8,104},... | collective-permute-start | bytes 688136 | tf_op jit(solution)/shard_map/ppermute | solution.py:65
  42.3 16.2 %collective-permute-start.15 = (bf16[64,1792]{1,0:T(8,128)(2,1)S(1)}, bf16[64,1792]{1,0:T(8,128)(2,1)S(1)}, u32[]{:S(2)}, u32[]{:S(2)}) collective-permute-start(bf16[64,1792]{1,0:T(8,128)(2,1)S(1)} %collective-permute-done.7.refs_2_), channel_id=1, source_target_pairs={{0,2},{1,3},{2,0},{3,1},{4,6},{5,7},{6,4},{7,5},{8,10},{9,11},{10,... | collective-permute-start | bytes 688136 | tf_op jit(solution)/shard_map/ppermute | solution.py:36
  44.7 19.4 %collective-permute-start.18 = (bf16[64,1792]{1,0:T(8,128)(2,1)S(1)}, bf16[64,1792]{1,0:T(8,128)(2,1)S(1)}, u32[]{:S(2)}, u32[]{:S(2)}) collective-permute-start(bf16[64,1792]{1,0:T(8,128)(2,1)S(1)} %collective-permute-done.10.refs_3_), channel_id=1, source_target_pairs={{0,32},{1,97},{2,34},{3,99},{4,36},{5,101},{6,38},{7,103},{8,40},{... | collective-permute-start | bytes 688136 | tf_op jit(solution)/shard_map/ppermute | solution.py:65
  48.1 16.0 %collective-permute-start.19 = (bf16[64,1792]{1,0:T(8,128)(2,1)S(1)}, bf16[64,1792]{1,0:T(8,128)(2,1)S(1)}, u32[]{:S(2)}, u32[]{:S(2)}) collective-permute-start(bf16[64,1792]{1,0:T(8,128)(2,1)S(1)} %collective-permute-done.13.refs_0_), channel_id=1, source_target_pairs={{0,96},{1,33},{2,98},{3,35},{4,100},{5,37},{6,102},{7,39},{8,104},... | collective-permute-start | bytes 688136 | tf_op jit(solution)/shard_map/ppermute | solution.py:65
  49.8 14.3 %collective-permute-start.16 = (bf16[64,1792]{1,0:T(8,128)(2,1)S(1)}, bf16[64,1792]{1,0:T(8,128)(2,1)S(1)}, u32[]{:S(2)}, u32[]{:S(2)}) collective-permute-start(bf16[64,1792]{1,0:T(8,128)(2,1)S(1)} %collective-permute-done.10.refs_3_), channel_id=1, source_target_pairs={{0,2},{1,3},{2,0},{3,1},{4,6},{5,7},{6,4},{7,5},{8,10},{9,11},{10,... | collective-permute-start | bytes 688136 | tf_op jit(solution)/shard_map/ppermute | solution.py:36
  51.5 12.6 %collective-permute-start.20 = (bf16[64,1792]{1,0:T(8,128)(2,1)S(1)}, bf16[64,1792]{1,0:T(8,128)(2,1)S(1)}, u32[]{:S(2)}, u32[]{:S(2)}) collective-permute-start(bf16[64,1792]{1,0:T(8,128)(2,1)S(1)} %collective-permute-done.14.refs_1_), channel_id=1, source_target_pairs={{0,96},{1,33},{2,98},{3,35},{4,100},{5,37},{6,102},{7,39},{8,104},... | collective-permute-start | bytes 688136 | tf_op jit(solution)/shard_map/ppermute | solution.py:65
  58.5 8.0 %collective-permute-start.21 = (f32[128,1536]{1,0:T(8,128)S(1)}, f32[128,1536]{1,0:T(8,128)S(1)}, u32[]{:S(2)}, u32[]{:S(2)}) collective-permute-start(f32[128,1536]{1,0:T(8,128)S(1)} %shard_map.98.refs_0_), channel_id=1, source_target_pairs={{0,1},{1,0},{2,3},{3,2},{4,5},{5,4},{6,7},{7,6},{8,9},{9,8},{10,11... | collective-permute-start | bytes 2359304 | tf_op jit(solution)/shard_map/ppermute | solution.py:36
  71.9 8.5 %collective-permute-start.26 = (bf16[64,1792]{1,0:T(8,128)(2,1)S(1)}, bf16[64,1792]{1,0:T(8,128)(2,1)S(1)}, u32[]{:S(2)}, u32[]{:S(2)}) collective-permute-start(bf16[64,1792]{1,0:T(8,128)(2,1)S(1)} %get-tuple-element.81), channel_id=1, source_target_pairs={{0,96},{1,33},{2,98},{3,35},{4,100},{5,37},{6,102},{7,39},{8,104},... | collective-permute-start | bytes 688136 | tf_op jit(solution)/shard_map/ppermute | solution.py:65
  73.3 8.8 %collective-permute-start.27 = (bf16[64,1792]{1,0:T(8,128)(2,1)S(1)}, bf16[64,1792]{1,0:T(8,128)(2,1)S(1)}, u32[]{:S(2)}, u32[]{:S(2)}) collective-permute-start(bf16[64,1792]{1,0:T(8,128)(2,1)S(1)} %get-tuple-element.82), channel_id=1, source_target_pairs={{0,2},{1,3},{2,0},{3,1},{4,6},{5,7},{6,4},{7,5},{8,10},{9,11},{10,... | collective-permute-start | bytes 688136 | tf_op jit(solution)/shard_map/ppermute | solution.py:36
  73.5 9.8 %collective-permute-start.30 = (bf16[64,1792]{1,0:T(8,128)(2,1)S(1)}, bf16[64,1792]{1,0:T(8,128)(2,1)S(1)}, u32[]{:S(2)}, u32[]{:S(2)}) collective-permute-start(bf16[64,1792]{1,0:T(8,128)(2,1)S(1)} %get-tuple-element.88), channel_id=1, source_target_pairs={{0,32},{1,97},{2,34},{3,99},{4,36},{5,101},{6,38},{7,103},{8,40},{... | collective-permute-start | bytes 688136 | tf_op jit(solution)/shard_map/ppermute | solution.py:65
  74.8 10.5 %collective-permute-start.33 = (bf16[64,1792]{1,0:T(8,128)(2,1)S(1)}, bf16[64,1792]{1,0:T(8,128)(2,1)S(1)}, u32[]{:S(2)}, u32[]{:S(2)}) collective-permute-start(bf16[64,1792]{1,0:T(8,128)(2,1)S(1)} %get-tuple-element.91), channel_id=1, source_target_pairs={{0,96},{1,33},{2,98},{3,35},{4,100},{5,37},{6,102},{7,39},{8,104},... | collective-permute-start | bytes 688136 | tf_op jit(solution)/shard_map/ppermute | solution.py:65
  82.2 9.5 %collective-permute-start.28 = (bf16[64,1792]{1,0:T(8,128)(2,1)S(1)}, bf16[64,1792]{1,0:T(8,128)(2,1)S(1)}, u32[]{:S(2)}, u32[]{:S(2)}) collective-permute-start(bf16[64,1792]{1,0:T(8,128)(2,1)S(1)} %add_convert_fusion.4), channel_id=1, source_target_pairs={{0,96},{1,33},{2,98},{3,35},{4,100},{5,37},{6,102},{7,39},{8,104},... | collective-permute-start | bytes 688136 | tf_op jit(solution)/shard_map/ppermute | solution.py:65
  83.3 8.1 %collective-permute-start.31 = (bf16[64,1792]{1,0:T(8,128)(2,1)S(1)}, bf16[64,1792]{1,0:T(8,128)(2,1)S(1)}, u32[]{:S(2)}, u32[]{:S(2)}) collective-permute-start(bf16[64,1792]{1,0:T(8,128)(2,1)S(1)} %add_convert_fusion.2), channel_id=1, source_target_pairs={{0,32},{1,97},{2,34},{3,99},{4,36},{5,101},{6,38},{7,103},{8,40},{... | collective-permute-start | bytes 688136 | tf_op jit(solution)/shard_map/ppermute | solution.py:65
  85.3 8.9 %collective-permute-start.35 = (bf16[64,1792]{1,0:T(8,128)(2,1)S(1)}, bf16[64,1792]{1,0:T(8,128)(2,1)S(1)}, u32[]{:S(2)}, u32[]{:S(2)}) collective-permute-start(bf16[64,1792]{1,0:T(8,128)(2,1)S(1)} %add_convert_fusion.1), channel_id=1, source_target_pairs={{0,96},{1,33},{2,98},{3,35},{4,100},{5,37},{6,102},{7,39},{8,104},... | collective-permute-start | bytes 688136 | tf_op jit(solution)/shard_map/ppermute | solution.py:65
  87.1 9.1 %collective-permute-start.25 = (bf16[64,1792]{1,0:T(8,128)(2,1)S(1)}, bf16[64,1792]{1,0:T(8,128)(2,1)S(1)}, u32[]{:S(2)}, u32[]{:S(2)}) collective-permute-start(bf16[64,1792]{1,0:T(8,128)(2,1)S(1)} %get-tuple-element.79), channel_id=1, source_target_pairs={{0,32},{1,97},{2,34},{3,99},{4,36},{5,101},{6,38},{7,103},{8,40},{... | collective-permute-start | bytes 688136 | tf_op jit(solution)/shard_map/ppermute | solution.py:65
  107.8 10.0 %collective-permute-start.42 = (bf16[16,3584]{1,0:T(8,128)(2,1)S(1)}, bf16[16,3584]{1,0:T(8,128)(2,1)S(1)}, u32[]{:S(2)}, u32[]{:S(2)}) collective-permute-start(bf16[16,3584]{1,0:T(8,128)(2,1)S(1)} %get-tuple-element.102), channel_id=1, source_target_pairs={{0,6},{1,7},{2,4},{3,5},{4,2},{5,3},{6,0},{7,1},{8,14},{9,15},{10,... | collective-permute-start | bytes 344072 | tf_op jit(solution)/shard_map/ppermute | solution.py:36
  109.6 10.2 %collective-permute-start.40 = (bf16[16,3584]{1,0:T(8,128)(2,1)S(1)}, bf16[16,3584]{1,0:T(8,128)(2,1)S(1)}, u32[]{:S(2)}, u32[]{:S(2)}) collective-permute-start(bf16[16,3584]{1,0:T(8,128)(2,1)S(1)} %get-tuple-element.99), channel_id=1, source_target_pairs={{0,1},{1,0},{2,3},{3,2},{4,5},{5,4},{6,7},{7,6},{8,9},{9,8},{10,11... | collective-permute-start | bytes 344072 | tf_op jit(solution)/shard_map/ppermute | solution.py:36
  (26 other events, 329.6 us)

commit v5 on v4

--- a/solution.py
+++ b/solution.py
@@ -212,8 +212,8 @@
 
 EARLY = [(0, 0), (3, 0), (1, 0), (0, 1)]
 LATE = [(1, 1), (3, 1), (2, 0), (2, 1)]
-SENT = [(2, 1), (2, 0), (3, 1), (1, 0)]
-KEPT = [(1, 1), (3, 0), (0, 1), (0, 0)]
+SENT = [(2, 1), (2, 0), (3, 1)]
+KEPT = [(1, 1), (3, 0), (0, 1), (1, 0), (0, 0)]
 
 
 def second_kernel(half, chunks, *refs):
@@ -387,7 +387,7 @@
     f31 = other_l(q[3, 1])
     f11 = along_x(add(q[1, 1], f21), 1)
     f30 = along_x(add(q[3, 0], f20, f31), -1)
-    q10, f11 = lax.optimization_barrier((q[1, 0], f11))
+    q10, f11, f30 = lax.optimization_barrier((q[1, 0], f11, f30))
     f01 = other_l(add(q[0, 1], f11))
     f10 = along_x(q10, 1)
     return [q[0, 0], f10, f30, f01]

time: 126 us -> 125 us (level)
  starting transfers between devices: 51.4 us -> 46.5 us
  waiting for transfers between devices: 47.8 us -> 52.5 us
    ppermute x20, waiting for transfers between devices: 22.4 us -> 26 us  [along_x(): return lax.ppermute(value, ('dp', 'expert'), pairs)]
    ppermute x20, starting transfers between devices: 16.8 us -> 13.7 us  [along_x(): return lax.ppermute(value, ('dp', 'expert'), pairs)]
    ppermute x23, starting transfers between devices: 34.6 us -> 32.7 us  [over_expert(): return lax.ppermute(value, 'expert', pairs)]
  transfers between devices with their start and end apart: 43 -> 43, of which waited for: 25 -> 26; matrix products, arithmetic and copies ran while one was open for 0% -> 0% of each run, Pallas kernels for 8% -> 8%
where the time goes in v5:
time: 125 us
  waiting for transfers between devices  52.5 us (42%)
  starting transfers between devices  46.5 us (37%)
  Pallas kernels  20.6 us (16%)
  local copies, waits for them, and re-layouts  4.1 us (3%)
    ppermute x23, starting transfers between devices, over_expert(): return lax.ppermute(value, 'expert', pairs)  32.7 us
    ppermute x23, waiting for transfers between devices, over_expert(): return lax.ppermute(value, 'expert', pairs)  26.4 us
    ppermute x20, waiting for transfers between devices, along_x(): return lax.ppermute(value, ('dp', 'expert'), pairs)  26 us
    pallas_call x10, Pallas kernels, whole(): pl.pallas_call(kernel, out_shape=outs, in_specs=specs or [VMEM] * len(arg...  16 us
    ppermute x20, starting transfers between devices, along_x(): return lax.ppermute(value, ('dp', 'expert'), pairs)  13.7 us
    unnamed x14, local copies, waits for them, and re-layouts  4.1 us
    pallas_call x1, Pallas kernels, shards(): pl.pallas_call(functools.partial(tail_kernel, half, True), out_shape=outs...  2.65 us
  transfers between devices with their start and end apart: 43, of which 26 were waited for; matrix products, arithmetic and copies ran while one was open for 0% of the time, Pallas kernels for 8%

profile of v5, /device:TPU:1, one launch (start us, length us, event | category | flops | bytes accessed | tf_op | source)
XLA Modules:
  0.0 125.1 jit_solution(9729727948592351915)
XLA Ops:
  0.6 4.5 %shard_map.94 = (bf16[16,3584]{1,0:T(8,128)(2,1)S(1)}, bf16[16,3584]{1,0:T(8,128)(2,1)S(1)}, bf16[16,3584]{1,0:T(8,128)(2,1)S(1)}, bf16[16,3584]{1,0:T(8,128)(2,1)S(1)}, bf16[10752,256]{1,0:T(8,128)(2,1)S(1)}) custom-call(s32[2,128]{1,0:T(2,128)} %bitcast.3, f32[2,128]{1,0:T(2,128)} %bitcast.6, bf16[128,7168]{1,0:T(8,128)(2,1)} %tok_ref.3, ...), custom_call_target="tpu_custom_call" | custom-call | tf_op jit(solution)/shard_map/pallas_call | solution.py:340
  6.7 2.8 %collective-permute-start.1 = (bf16[16,3584]{1,0:T(8,128)(2,1)S(1)}, bf16[16,3584]{1,0:T(8,128)(2,1)S(1)}, u32[]{:S(2)}, u32[]{:S(2)}) collective-permute-start(bf16[16,3584]{1,0:T(8,128)(2,1)S(1)} %get-tuple-element.60), channel_id=1, source_target_pairs={{0,6},{1,7},{2,4},{3,5},{4,2},{5,3},{6,0},{7,1},{8,14},{9,15},{10,... | collective-permute-start | bytes 344072 | tf_op jit(solution)/shard_map/ppermute | solution.py:36
  10.0 5.5 %collective-permute-done.near_got = bf16[16,3584]{1,0:T(8,128)(2,1)S(1)} collective-permute-done((bf16[16,3584]{1,0:T(8,128)(2,1)S(1)}, bf16[16,3584]{1,0:T(8,128)(2,1)S(1)}, u32[]{:S(2)}, u32[]{:S(2)}) %collective-permute-start) | collective-permute-done | bytes 114720 | tf_op jit(solution)/shard_map/ppermute | solution.py:36
  18.4 3.3 %collective-permute-start.4 = (bf16[16,3584]{1,0:T(8,128)(2,1)S(1)}, bf16[16,3584]{1,0:T(8,128)(2,1)S(1)}, u32[]{:S(2)}, u32[]{:S(2)}) collective-permute-start(bf16[16,3584]{1,0:T(8,128)(2,1)S(1)} %get-tuple-element.64), channel_id=1, source_target_pairs={{0,16},{1,17},{2,18},{3,19},{4,20},{5,21},{6,22},{7,23},{8,24},{9,... | collective-permute-start | bytes 344072 | tf_op jit(solution)/shard_map/ppermute | solution.py:36
  23.8 3.3 %collective-permute-done.4.m2 = bf16[16,3584]{1,0:T(8,128)(2,1)S(1)} collective-permute-done((bf16[16,3584]{1,0:T(8,128)(2,1)S(1)}, bf16[16,3584]{1,0:T(8,128)(2,1)S(1)}, u32[]{:S(2)}, u32[]{:S(2)}) %collective-permute-start.4) | collective-permute-done | bytes 114720 | tf_op jit(solution)/shard_map/ppermute | solution.py:36
  30.3 2.8 %collective-permute-done.6.refs_6_ = bf16[64,1792]{1,0:T(8,128)(2,1)S(1)} collective-permute-done((bf16[64,1792]{1,0:T(8,128)(2,1)S(1)}, bf16[64,1792]{1,0:T(8,128)(2,1)S(1)}, u32[]{:S(2)}, u32[]{:S(2)}) %collective-permute-start.6) | collective-permute-done | bytes 229408 | tf_op jit(solution)/shard_map/ppermute | solution.py:36
  36.9 3.9 %collective-permute-done.11.refs_5_ = bf16[64,1792]{1,0:T(8,128)(2,1)S(1)} collective-permute-done((bf16[64,1792]{1,0:T(8,128)(2,1)S(1)}, bf16[64,1792]{1,0:T(8,128)(2,1)S(1)}, u32[]{:S(2)}, u32[]{:S(2)}) %collective-permute-start.11) | collective-permute-done | bytes 229408 | tf_op jit(solution)/shard_map/ppermute | solution.py:65
  44.9 3.2 %collective-permute-done.17.refs_4_ = bf16[64,1792]{1,0:T(8,128)(2,1)S(1)} collective-permute-done((bf16[64,1792]{1,0:T(8,128)(2,1)S(1)}, bf16[64,1792]{1,0:T(8,128)(2,1)S(1)}, u32[]{:S(2)}, u32[]{:S(2)}) %collective-permute-start.17) | collective-permute-done | bytes 229408 | tf_op jit(solution)/shard_map/ppermute | solution.py:65
  51.5 2.0 %copy-done.3 = bf16[1,7168,256]{2,1,0:T(8,128)(2,1)S(1)} copy-done((bf16[1,7168,256]{2,1,0:T(8,128)(2,1)S(1)}, bf16[1,7168,256]{2,1,0:T(8,128)(2,1)}, u32[]{:S(2)}) %copy-start.3) | copy-done | bytes 3670040
  53.5 2.0 %copy-done.4 = bf16[1,256,7168]{2,1,0:T(8,128)(2,1)S(1)} copy-done((bf16[1,256,7168]{2,1,0:T(8,128)(2,1)S(1)}, bf16[1,256,7168]{2,1,0:T(8,128)(2,1)}, u32[]{:S(2)}) %copy-start.4) | copy-done | bytes 3670040
  56.3 2.2 %shard_map.98.refs_0_ = f32[128,1536]{1,0:T(8,128)S(1)} custom-call(bf16[64,1792]{1,0:T(8,128)(2,1)S(1)} %get-tuple-element.66.refs_0_, bf16[64,1792]{1,0:T(8,128)(2,1)S(1)} %get-tuple-element.68.refs_1_, bf16[64,1792]{1,0:T(8,128)(2,1)S(1)} %collective-permute-done.7.refs_2_, bf16[64,1792]{1,0:T(8,128)(2,1)S(1)} %collective-permute-done.10.refs_3_, ...), custom_call_target="tpu_custom_call" | custom-call | tf_op jit(solution)/shard_map/pallas_call | solution.py:340
  58.5 5.6 %collective-permute-start.21 = (f32[128,1536]{1,0:T(8,128)S(1)}, f32[128,1536]{1,0:T(8,128)S(1)}, u32[]{:S(2)}, u32[]{:S(2)}) collective-permute-start(f32[128,1536]{1,0:T(8,128)S(1)} %shard_map.98.refs_0_), channel_id=1, source_target_pairs={{0,1},{1,0},{2,3},{3,2},{4,5},{5,4},{6,7},{7,6},{8,9},{9,8},{10,11... | collective-permute-start | bytes 2359304 | tf_op jit(solution)/shard_map/ppermute | solution.py:36
  64.1 2.2 %shard_map.99.refs_1_ = f32[128,1536]{1,0:T(8,128)S(1)} custom-call(bf16[64,1792]{1,0:T(8,128)(2,1)S(1)} %collective-permute-done.13.refs_0_, bf16[64,1792]{1,0:T(8,128)(2,1)S(1)} %collective-permute-done.14.refs_1_, bf16[64,1792]{1,0:T(8,128)(2,1)S(1)} %collective-permute-done.15.refs_2_, bf16[64,1792]{1,0:T(8,128)(2,1)S(1)} %collective-permute-done.16.refs_3_, ...), custom_call_target="tpu_custom_call" | custom-call | tf_op jit(solution)/shard_map/pallas_call | solution.py:340
  66.5 2.2 %collective-permute-done.22.refs_3_ = f32[128,1536]{1,0:T(8,128)S(1)} collective-permute-done((f32[128,1536]{1,0:T(8,128)S(1)}, f32[128,1536]{1,0:T(8,128)S(1)}, u32[]{:S(2)}, u32[]{:S(2)}) %collective-permute-start.22) | collective-permute-done | bytes 786464 | tf_op jit(solution)/shard_map/ppermute | solution.py:36
  68.7 2.8 %shard_map.101 = (bf16[64,1792]{1,0:T(8,128)(2,1)S(1)}, bf16[64,1792]{1,0:T(8,128)(2,1)S(1)}, bf16[64,1792]{1,0:T(8,128)(2,1)S(1)}, bf16[64,1792]{1,0:T(8,128)(2...) custom-call(f32[128,1536]{1,0:T(8,128)S(1)} %shard_map.98.refs_0_, ...), custom_call_target="tpu_custom_call" | custom-call | tf_op jit(solution)/shard_map/pallas_call | solution.py:340
  74.7 2.8 %shard_map.100 = (bf16[64,1792]{1,0:T(8,128)(2,1)S(1)}, bf16[64,1792]{1,0:T(8,128)(2,1)S(1)}, bf16[64,1792]{1,0:T(8,128)(2,1)S(1)}, bf16[64,1792]{1,0:T(8,128)(2...) custom-call(f32[128,1536]{1,0:T(8,128)S(1)} %shard_map.98.refs_0_, ...), custom_call_target="tpu_custom_call" | custom-call | tf_op jit(solution)/shard_map/pallas_call | solution.py:340
  88.9 2.5 %collective-permute-done.31 = bf16[64,1792]{1,0:T(8,128)(2,1)S(1)} collective-permute-done((bf16[64,1792]{1,0:T(8,128)(2,1)S(1)}, bf16[64,1792]{1,0:T(8,128)(2,1)S(1)}, u32[]{:S(2)}, u32[]{:S(2)}) %collective-permute-start.31) | collective-permute-done | bytes 229408 | tf_op jit(solution)/shard_map/ppermute | solution.py:65
  91.4 2.6 %collective-permute-done.34.refs_6_ = bf16[64,1792]{1,0:T(8,128)(2,1)S(1)} collective-permute-done((bf16[64,1792]{1,0:T(8,128)(2,1)S(1)}, bf16[64,1792]{1,0:T(8,128)(2,1)S(1)}, u32[]{:S(2)}, u32[]{:S(2)}) %collective-permute-start.34) | collective-permute-done | bytes 229408 | tf_op jit(solution)/shard_map/ppermute | solution.py:65
  96.3 2.9 %collective-permute-done.35.refs_5_ = bf16[64,1792]{1,0:T(8,128)(2,1)S(1)} collective-permute-done((bf16[64,1792]{1,0:T(8,128)(2,1)S(1)}, bf16[64,1792]{1,0:T(8,128)(2,1)S(1)}, u32[]{:S(2)}, u32[]{:S(2)}) %collective-permute-start.35) | collective-permute-done | bytes 229408 | tf_op jit(solution)/shard_map/ppermute | solution.py:65
  103.5 2.1 %collective-permute-done.37.refs_1_ = bf16[16,3584]{1,0:T(8,128)(2,1)S(1)} collective-permute-done((bf16[16,3584]{1,0:T(8,128)(2,1)S(1)}, bf16[16,3584]{1,0:T(8,128)(2,1)S(1)}, u32[]{:S(2)}, u32[]{:S(2)}) %collective-permute-start.37) | collective-permute-done | bytes 114720 | tf_op jit(solution)/shard_map/ppermute | solution.py:36
  105.6 2.3 %collective-permute-done.38.refs_2_ = bf16[16,3584]{1,0:T(8,128)(2,1)S(1)} collective-permute-done((bf16[16,3584]{1,0:T(8,128)(2,1)S(1)}, bf16[16,3584]{1,0:T(8,128)(2,1)S(1)}, u32[]{:S(2)}, u32[]{:S(2)}) %collective-permute-start.38) | collective-permute-done | bytes 114720 | tf_op jit(solution)/shard_map/ppermute | solution.py:36
  111.2 5.1 %collective-permute-start.40 = (bf16[16,3584]{1,0:T(8,128)(2,1)S(1)}, bf16[16,3584]{1,0:T(8,128)(2,1)S(1)}, u32[]{:S(2)}, u32[]{:S(2)}) collective-permute-start(bf16[16,3584]{1,0:T(8,128)(2,1)S(1)} %get-tuple-element.103), channel_id=1, source_target_pairs={{0,1},{1,0},{2,3},{3,2},{4,5},{5,4},{6,7},{7,6},{8,9},{9,8},{10,11... | collective-permute-start | bytes 344072 | tf_op jit(solution)/shard_map/ppermute | solution.py:36
  119.1 3.2 %collective-permute-done.41.far = bf16[16,3584]{1,0:T(8,128)(2,1)S(1)} collective-permute-done((bf16[16,3584]{1,0:T(8,128)(2,1)S(1)}, bf16[16,3584]{1,0:T(8,128)(2,1)S(1)}, u32[]{:S(2)}, u32[]{:S(2)}) %collective-permute-start.41) | collective-permute-done | bytes 114720 | tf_op jit(solution)/shard_map/ppermute | solution.py:36
  122.3 2.6 %shard_map.105 = (bf16[128,7168]{1,0:T(8,128)(2,1)}, bf16[128,7168]{1,0:T(8,128)(2,1)}, f32[2,128]{1,0:T(2,128)}) custom-call(s32[2,128]{1,0:T(2,128)S(1)} %bitcast.5, f32[2,128]{1,0:T(2,128)S(1)} %bitcast.8, bf16[128,7168]{1,0:T(8,128)(2,1)S(1)} %copy-done, bf16[128,7168]{1,0:T(8,128)(2,1)S(1)} %copy-done.1, ...), custom_call_target="tpu_custom_call", output_to_operand_aliasing={{0}: (7, {}), {1}: (8, {})} | custom-call | tf_op jit(solution)/shard_map/pallas_call | solution.py:475
  (94 shorter events, 49.5 us)
Async XLA Ops:
  5.1 46.4 %collective-permute-start.12 = (bf16[10752,256]{1,0:T(8,128)(2,1)S(1)}, bf16[10752,256]{1,0:T(8,128)(2,1)S(1)}, u32[]{:S(2)}, u32[]{:S(2)}) collective-permute-start(bf16[10752,256]{1,0:T(8,128)(2,1)S(1)} %get-tuple-element.76), channel_id=1, source_target_pairs={{0,1},{1,0},{2,3},{3,2},{4,5},{5,4},{6,7},{7,6},{8,9},{9,8},{10,11... | collective-permute-start | bytes 16515080 | tf_op jit(solution)/shard_map/ppermute | solution.py:36
  6.6 8.8 %collective-permute-start = (bf16[16,3584]{1,0:T(8,128)(2,1)S(1)}, bf16[16,3584]{1,0:T(8,128)(2,1)S(1)}, u32[]{:S(2)}, u32[]{:S(2)}) collective-permute-start(bf16[16,3584]{1,0:T(8,128)(2,1)S(1)} %get-tuple-element.59), channel_id=1, source_target_pairs={{0,1},{1,0},{2,3},{3,2},{4,5},{5,4},{6,7},{7,6},{8,9},{9,8},{10,11... | collective-permute-start | bytes 344072 | tf_op jit(solution)/shard_map/ppermute | solution.py:36
  6.7 8.7 %collective-permute-start.1 = (bf16[16,3584]{1,0:T(8,128)(2,1)S(1)}, bf16[16,3584]{1,0:T(8,128)(2,1)S(1)}, u32[]{:S(2)}, u32[]{:S(2)}) collective-permute-start(bf16[16,3584]{1,0:T(8,128)(2,1)S(1)} %get-tuple-element.60), channel_id=1, source_target_pairs={{0,6},{1,7},{2,4},{3,5},{4,2},{5,3},{6,0},{7,1},{8,14},{9,15},{10,... | collective-permute-start | bytes 344072 | tf_op jit(solution)/shard_map/ppermute | solution.py:36
  18.4 8.6 %collective-permute-start.4 = (bf16[16,3584]{1,0:T(8,128)(2,1)S(1)}, bf16[16,3584]{1,0:T(8,128)(2,1)S(1)}, u32[]{:S(2)}, u32[]{:S(2)}) collective-permute-start(bf16[16,3584]{1,0:T(8,128)(2,1)S(1)} %get-tuple-element.64), channel_id=1, source_target_pairs={{0,16},{1,17},{2,18},{3,19},{4,20},{5,21},{6,22},{7,23},{8,24},{9,... | collective-permute-start | bytes 344072 | tf_op jit(solution)/shard_map/ppermute | solution.py:36
  27.6 8.2 %collective-permute-start.8 = (bf16[64,1792]{1,0:T(8,128)(2,1)S(1)}, bf16[64,1792]{1,0:T(8,128)(2,1)S(1)}, u32[]{:S(2)}, u32[]{:S(2)}) collective-permute-start(bf16[64,1792]{1,0:T(8,128)(2,1)S(1)} %get-tuple-element.66.refs_0_), channel_id=1, source_target_pairs={{0,96},{1,33},{2,98},{3,35},{4,100},{5,37},{6,102},{7,39},{8,104},... | collective-permute-start | bytes 688136 | tf_op jit(solution)/shard_map/ppermute | solution.py:65
  33.1 7.8 %collective-permute-start.11 = (bf16[64,1792]{1,0:T(8,128)(2,1)S(1)}, bf16[64,1792]{1,0:T(8,128)(2,1)S(1)}, u32[]{:S(2)}, u32[]{:S(2)}) collective-permute-start(bf16[64,1792]{1,0:T(8,128)(2,1)S(1)} %get-tuple-element.68.refs_1_), channel_id=1, source_target_pairs={{0,96},{1,33},{2,98},{3,35},{4,100},{5,37},{6,102},{7,39},{8,104},... | collective-permute-start | bytes 688136 | tf_op jit(solution)/shard_map/ppermute | solution.py:65
  36.2 8.6 %collective-permute-start.13 = (bf16[64,1792]{1,0:T(8,128)(2,1)S(1)}, bf16[64,1792]{1,0:T(8,128)(2,1)S(1)}, u32[]{:S(2)}, u32[]{:S(2)}) collective-permute-start(bf16[64,1792]{1,0:T(8,128)(2,1)S(1)} %collective-permute-done.6.refs_6_), channel_id=1, source_target_pairs={{0,96},{1,33},{2,98},{3,35},{4,100},{5,37},{6,102},{7,39},{8,104},... | collective-permute-start | bytes 688136 | tf_op jit(solution)/shard_map/ppermute | solution.py:65
  40.9 8.9 %collective-permute-start.14 = (bf16[64,1792]{1,0:T(8,128)(2,1)S(1)}, bf16[64,1792]{1,0:T(8,128)(2,1)S(1)}, u32[]{:S(2)}, u32[]{:S(2)}) collective-permute-start(bf16[64,1792]{1,0:T(8,128)(2,1)S(1)} %collective-permute-done.9.refs_7_), channel_id=1, source_target_pairs={{0,96},{1,33},{2,98},{3,35},{4,100},{5,37},{6,102},{7,39},{8,104},... | collective-permute-start | bytes 688136 | tf_op jit(solution)/shard_map/ppermute | solution.py:65
  42.3 16.2 %collective-permute-start.15 = (bf16[64,1792]{1,0:T(8,128)(2,1)S(1)}, bf16[64,1792]{1,0:T(8,128)(2,1)S(1)}, u32[]{:S(2)}, u32[]{:S(2)}) collective-permute-start(bf16[64,1792]{1,0:T(8,128)(2,1)S(1)} %collective-permute-done.7.refs_2_), channel_id=1, source_target_pairs={{0,2},{1,3},{2,0},{3,1},{4,6},{5,7},{6,4},{7,5},{8,10},{9,11},{10,... | collective-permute-start | bytes 688136 | tf_op jit(solution)/shard_map/ppermute | solution.py:36
  44.7 19.4 %collective-permute-start.18 = (bf16[64,1792]{1,0:T(8,128)(2,1)S(1)}, bf16[64,1792]{1,0:T(8,128)(2,1)S(1)}, u32[]{:S(2)}, u32[]{:S(2)}) collective-permute-start(bf16[64,1792]{1,0:T(8,128)(2,1)S(1)} %collective-permute-done.10.refs_3_), channel_id=1, source_target_pairs={{0,32},{1,97},{2,34},{3,99},{4,36},{5,101},{6,38},{7,103},{8,40},{... | collective-permute-start | bytes 688136 | tf_op jit(solution)/shard_map/ppermute | solution.py:65
  48.1 16.0 %collective-permute-start.19 = (bf16[64,1792]{1,0:T(8,128)(2,1)S(1)}, bf16[64,1792]{1,0:T(8,128)(2,1)S(1)}, u32[]{:S(2)}, u32[]{:S(2)}) collective-permute-start(bf16[64,1792]{1,0:T(8,128)(2,1)S(1)} %collective-permute-done.13.refs_0_), channel_id=1, source_target_pairs={{0,96},{1,33},{2,98},{3,35},{4,100},{5,37},{6,102},{7,39},{8,104},... | collective-permute-start | bytes 688136 | tf_op jit(solution)/shard_map/ppermute | solution.py:65
  49.8 14.3 %collective-permute-start.16 = (bf16[64,1792]{1,0:T(8,128)(2,1)S(1)}, bf16[64,1792]{1,0:T(8,128)(2,1)S(1)}, u32[]{:S(2)}, u32[]{:S(2)}) collective-permute-start(bf16[64,1792]{1,0:T(8,128)(2,1)S(1)} %collective-permute-done.10.refs_3_), channel_id=1, source_target_pairs={{0,2},{1,3},{2,0},{3,1},{4,6},{5,7},{6,4},{7,5},{8,10},{9,11},{10,... | collective-permute-start | bytes 688136 | tf_op jit(solution)/shard_map/ppermute | solution.py:36
  51.5 12.6 %collective-permute-start.20 = (bf16[64,1792]{1,0:T(8,128)(2,1)S(1)}, bf16[64,1792]{1,0:T(8,128)(2,1)S(1)}, u32[]{:S(2)}, u32[]{:S(2)}) collective-permute-start(bf16[64,1792]{1,0:T(8,128)(2,1)S(1)} %collective-permute-done.14.refs_1_), channel_id=1, source_target_pairs={{0,96},{1,33},{2,98},{3,35},{4,100},{5,37},{6,102},{7,39},{8,104},... | collective-permute-start | bytes 688136 | tf_op jit(solution)/shard_map/ppermute | solution.py:65
  58.5 8.0 %collective-permute-start.21 = (f32[128,1536]{1,0:T(8,128)S(1)}, f32[128,1536]{1,0:T(8,128)S(1)}, u32[]{:S(2)}, u32[]{:S(2)}) collective-permute-start(f32[128,1536]{1,0:T(8,128)S(1)} %shard_map.98.refs_0_), channel_id=1, source_target_pairs={{0,1},{1,0},{2,3},{3,2},{4,5},{5,4},{6,7},{7,6},{8,9},{9,8},{10,11... | collective-permute-start | bytes 2359304 | tf_op jit(solution)/shard_map/ppermute | solution.py:36
  71.6 8.5 %collective-permute-start.25 = (bf16[64,1792]{1,0:T(8,128)(2,1)S(1)}, bf16[64,1792]{1,0:T(8,128)(2,1)S(1)}, u32[]{:S(2)}, u32[]{:S(2)}) collective-permute-start(bf16[64,1792]{1,0:T(8,128)(2,1)S(1)} %get-tuple-element.82), channel_id=1, source_target_pairs={{0,96},{1,33},{2,98},{3,35},{4,100},{5,37},{6,102},{7,39},{8,104},... | collective-permute-start | bytes 688136 | tf_op jit(solution)/shard_map/ppermute | solution.py:65
  73.1 8.5 %collective-permute-start.26 = (bf16[64,1792]{1,0:T(8,128)(2,1)S(1)}, bf16[64,1792]{1,0:T(8,128)(2,1)S(1)}, u32[]{:S(2)}, u32[]{:S(2)}) collective-permute-start(bf16[64,1792]{1,0:T(8,128)(2,1)S(1)} %get-tuple-element.83), channel_id=1, source_target_pairs={{0,2},{1,3},{2,0},{3,1},{4,6},{5,7},{6,4},{7,5},{8,10},{9,11},{10,... | collective-permute-start | bytes 688136 | tf_op jit(solution)/shard_map/ppermute | solution.py:36
  73.2 9.8 %collective-permute-start.30 = (bf16[64,1792]{1,0:T(8,128)(2,1)S(1)}, bf16[64,1792]{1,0:T(8,128)(2,1)S(1)}, u32[]{:S(2)}, u32[]{:S(2)}) collective-permute-start(bf16[64,1792]{1,0:T(8,128)(2,1)S(1)} %get-tuple-element.91), channel_id=1, source_target_pairs={{0,32},{1,97},{2,34},{3,99},{4,36},{5,101},{6,38},{7,103},{8,40},{... | collective-permute-start | bytes 688136 | tf_op jit(solution)/shard_map/ppermute | solution.py:65
  74.5 10.5 %collective-permute-start.32 = (bf16[64,1792]{1,0:T(8,128)(2,1)S(1)}, bf16[64,1792]{1,0:T(8,128)(2,1)S(1)}, u32[]{:S(2)}, u32[]{:S(2)}) collective-permute-start(bf16[64,1792]{1,0:T(8,128)(2,1)S(1)} %get-tuple-element.93), channel_id=1, source_target_pairs={{0,96},{1,33},{2,98},{3,35},{4,100},{5,37},{6,102},{7,39},{8,104},... | collective-permute-start | bytes 688136 | tf_op jit(solution)/shard_map/ppermute | solution.py:65
  83.1 8.4 %collective-permute-start.31 = (bf16[64,1792]{1,0:T(8,128)(2,1)S(1)}, bf16[64,1792]{1,0:T(8,128)(2,1)S(1)}, u32[]{:S(2)}, u32[]{:S(2)}) collective-permute-start(bf16[64,1792]{1,0:T(8,128)(2,1)S(1)} %add_convert_fusion.2), channel_id=1, source_target_pairs={{0,32},{1,97},{2,34},{3,99},{4,36},{5,101},{6,38},{7,103},{8,40},{... | collective-permute-start | bytes 688136 | tf_op jit(solution)/shard_map/ppermute | solution.py:65
  85.1 9.0 %collective-permute-start.34 = (bf16[64,1792]{1,0:T(8,128)(2,1)S(1)}, bf16[64,1792]{1,0:T(8,128)(2,1)S(1)}, u32[]{:S(2)}, u32[]{:S(2)}) collective-permute-start(bf16[64,1792]{1,0:T(8,128)(2,1)S(1)} %add_convert_fusion.1), channel_id=1, source_target_pairs={{0,96},{1,33},{2,98},{3,35},{4,100},{5,37},{6,102},{7,39},{8,104},... | collective-permute-start | bytes 688136 | tf_op jit(solution)/shard_map/ppermute | solution.py:65
  88.5 7.9 %collective-permute-start.28 = (bf16[64,1792]{1,0:T(8,128)(2,1)S(1)}, bf16[64,1792]{1,0:T(8,128)(2,1)S(1)}, u32[]{:S(2)}, u32[]{:S(2)}) collective-permute-start(bf16[64,1792]{1,0:T(8,128)(2,1)S(1)} %get-tuple-element.84), channel_id=1, source_target_pairs={{0,32},{1,97},{2,34},{3,99},{4,36},{5,101},{6,38},{7,103},{8,40},{... | collective-permute-start | bytes 688136 | tf_op jit(solution)/shard_map/ppermute | solution.py:65
  88.5 7.8 %collective-permute-start.29 = (bf16[64,1792]{1,0:T(8,128)(2,1)S(1)}, bf16[64,1792]{1,0:T(8,128)(2,1)S(1)}, u32[]{:S(2)}, u32[]{:S(2)}) collective-permute-start(bf16[64,1792]{1,0:T(8,128)(2,1)S(1)} %add_convert_fusion.3), channel_id=1, source_target_pairs={{0,2},{1,3},{2,0},{3,1},{4,6},{5,7},{6,4},{7,5},{8,10},{9,11},{10,... | collective-permute-start | bytes 688136 | tf_op jit(solution)/shard_map/ppermute | solution.py:36
  109.3 7.8 %collective-permute-start.42 = (bf16[16,3584]{1,0:T(8,128)(2,1)S(1)}, bf16[16,3584]{1,0:T(8,128)(2,1)S(1)}, u32[]{:S(2)}, u32[]{:S(2)}) collective-permute-start(bf16[16,3584]{1,0:T(8,128)(2,1)S(1)} %get-tuple-element.106), channel_id=1, source_target_pairs={{0,6},{1,7},{2,4},{3,5},{4,2},{5,3},{6,0},{7,1},{8,14},{9,15},{10,... | collective-permute-start | bytes 344072 | tf_op jit(solution)/shard_map/ppermute | solution.py:36
  111.2 7.9 %collective-permute-start.40 = (bf16[16,3584]{1,0:T(8,128)(2,1)S(1)}, bf16[16,3584]{1,0:T(8,128)(2,1)S(1)}, u32[]{:S(2)}, u32[]{:S(2)}) collective-permute-start(bf16[16,3584]{1,0:T(8,128)(2,1)S(1)} %get-tuple-element.103), channel_id=1, source_target_pairs={{0,1},{1,0},{2,3},{3,2},{4,5},{5,4},{6,7},{7,6},{8,9},{9,8},{10,11... | collective-permute-start | bytes 344072 | tf_op jit(solution)/shard_map/ppermute | solution.py:36
  (26 other events, 327.3 us)
